TPU v7x, 32 devices: a whole 2x2x4 slice. The times are simulated.
32 devices in a mesh: seq: 8 (over z, x), head: 4 (over y, core).
Axes of the slice: x: 2, y: 2, z: 4, core: 2. Of those that a mesh axis runs over, the one named last changes fastest.
Arguments:
- query: bfloat16 [2048, 256], P('seq', 'head'), may hold values from -5 to 5
- key: bfloat16 [2048, 256], P('seq', 'head'), may hold values from -5 to 5
- value: bfloat16 [2048, 2048], P('seq', 'head'), may hold values from -76 to 76
- window_query: bfloat16 [2048, 2048], P('seq', 'head'), may hold values from -4.5 to 4.5
- window_key: bfloat16 [2048, 2048], P('seq', 'head'), may hold values from -4.5 to 4.5
- gain: float32 [2048], P('head'), may hold values from 0.5 to 1.5
- cotangent: bfloat16 [2048, 2048], P('seq', 'head'), may hold values from -11 to 11
Outputs:
- normed: bfloat16 [2048, 2048], P('seq', 'head')
- grad_query: bfloat16 [2048, 256], P('seq', 'head')
- grad_key: bfloat16 [2048, 256], P('seq', 'head')
- grad_value: bfloat16 [2048, 2048], P('seq', 'head')
- grad_window_query: bfloat16 [2048, 2048], P('seq', 'head')
- grad_window_key: bfloat16 [2048, 2048], P('seq', 'head')
All inputs are finite; a program needn't handle non-finite values.
Results may differ from a plain program's by a relative error of at most 0.0065.
Values may be sent and summed in bfloat16 or wider, within the bound.
No kernel may reach another device: no remote copies, remote signals or barrier semaphores. Data moves between devices by JAX's collectives and lax.ppermute only.
A program may use at most 128 MiB of HBM per device.

v0:
```python
import math

import jax
import jax.numpy as jnp
from jax import lax
from jax.sharding import PartitionSpec as P

HEADS = 16
HEAD_DIM = 128
FEAT = 16
WINDOW = 64


HIGHEST = lax.Precision.HIGHEST


def passed_along(block, axis, distance):
    devices = range(lax.axis_size(axis))
    route = [(i - distance, i) for i in devices if i - distance in devices]
    return lax.ppermute(block, axis, route)


def prefix(part, axis, combine, identity, reverse):
    count = lax.axis_size(axis)
    place = lax.axis_index(axis)
    ahead = count - 1 - place if reverse else place
    gathered = jax.tree.map(lambda a: lax.all_gather(a, axis), part)
    state = jax.tree.map(lambda a, e: jnp.zeros_like(a) + jnp.asarray(e, a.dtype), part, identity)

    def one(step, state):
        source = count - 1 - step if reverse else step
        return combine(
            state, jax.tree.map(lambda a: lax.dynamic_index_in_dim(a, source, 0, False), gathered)
        )

    return lax.fori_loop(0, ahead, one, state)


def narrow(tensor):
    return lax.optimization_barrier(tensor.astype(jnp.bfloat16))


def add_pair(earlier, later):
    return (earlier[0] + later[0], earlier[1] + later[1])


def taylor(inputs, head_count, features):
    length = inputs.shape[0]
    scaled = inputs.astype(jnp.float32).reshape(length, head_count, features) * features ** (-0.25)
    square = (scaled[:, :, :, None] * scaled[:, :, None, :]).reshape(
        length, head_count, features * features
    ) * math.sqrt(0.5)
    return jnp.concatenate([jnp.ones((length, head_count, 1), jnp.float32), scaled, square], axis=2)


def taylor_back(inputs, head_count, features, upstream):
    length = inputs.shape[0]
    scaled = inputs.astype(jnp.float32).reshape(length, head_count, features) * features ** (-0.25)
    linear_part = upstream[:, :, 1 : 1 + features]
    square = upstream[:, :, 1 + features :].reshape(
        length, head_count, features, features
    ) * math.sqrt(0.5)
    summed = (
        linear_part
        + jnp.sum(square * scaled[:, :, None, :], axis=3)
        + jnp.sum(square * scaled[:, :, :, None], axis=2)
    )
    return (summed * features ** (-0.25)).reshape(length, head_count * features)


def window_blocks(rows_in, window):
    groups = rows_in.shape[0] // window
    grouped = rows_in.reshape(groups, window, rows_in.shape[1], rows_in.shape[2])
    return jnp.concatenate([grouped[:-1], grouped[1:]], axis=1)


def unblock(blocked, window):
    zero_block = jnp.zeros_like(blocked[:1, :window])
    lower = jnp.concatenate([blocked[:, :window], zero_block], axis=0)
    upper = jnp.concatenate([zero_block, blocked[:, window:]], axis=0)
    joined = lower + upper
    return joined.reshape(joined.shape[0] * window, joined.shape[2] * joined.shape[3])


def window_mask(groups, window, rim_live):
    shape = (groups, 1, window, 2 * window)
    block_index = lax.broadcasted_iota(jnp.int32, shape, 0)
    row_index = lax.broadcasted_iota(jnp.int32, shape, 2)
    col_index = lax.broadcasted_iota(jnp.int32, shape, 3)
    inside = (col_index > row_index) & (col_index <= row_index + window)
    return inside & ((block_index > 0) | (col_index >= window) | rim_live)


def shards(query, key, value, window_query, window_key, gain, cotangent):
    head_count = HEADS // lax.axis_size("head")
    features = FEAT
    head_width = HEAD_DIM
    window = WINDOW
    length = query.shape[0]
    rim_rows = window - 1
    cut = length - rim_rows
    full_width = HEADS * HEAD_DIM
    local_width = head_count * head_width
    groups = length // window
    rim_key, rim_value = passed_along((window_key[cut:], value[cut:]), "seq", 1)
    rim_live = lax.axis_index("seq") > 0
    feat_query = narrow(taylor(query, head_count, features))
    feat_key = narrow(taylor(key, head_count, features))
    feat_query_f = feat_query.astype(jnp.float32)
    feat_key_f = feat_key.astype(jnp.float32)
    value_heads = value.reshape(length, head_count, head_width)
    block_state = jnp.einsum(
        "the,thd->hed", feat_key, value_heads, preferred_element_type=jnp.float32
    )
    block_norm = jnp.sum(feat_key_f, axis=0)
    prefix_state, prefix_norm = prefix(
        (block_state, block_norm),
        "seq",
        add_pair,
        (jnp.zeros_like(block_state), jnp.zeros_like(block_norm)),
        False,
    )
    query_heads = query.reshape(length, head_count, features)
    key_heads = key.reshape(length, head_count, features)
    scores = jnp.einsum(
        "thf,shf->hts", query_heads, key_heads, preferred_element_type=jnp.float32
    ) / math.sqrt(features)
    causal = lax.broadcasted_iota(jnp.int32, (1, length, length), 1) >= lax.broadcasted_iota(
        jnp.int32, (1, length, length), 2
    )
    kernel = jnp.where(causal, 1.0 + scores + 0.5 * scores * scores, 0.0)
    kernel_narrow = narrow(kernel)
    pad_row = jnp.zeros((1, local_width), jnp.bfloat16)
    key_rows = jnp.concatenate([pad_row, rim_key, window_key], axis=0).reshape(
        length + window, head_count, head_width
    )
    value_rows = jnp.concatenate([pad_row, rim_value, value], axis=0).reshape(
        length + window, head_count, head_width
    )
    key_blocks = window_blocks(key_rows, window)
    value_blocks = window_blocks(value_rows, window)
    query_blocks = window_query.reshape(groups, window, head_count, head_width)
    logits = jnp.einsum(
        "bihd,bjhd->bhij", query_blocks, key_blocks, preferred_element_type=jnp.float32
    ) / math.sqrt(head_width)
    allowed = window_mask(groups, window, rim_live)
    masked = jnp.where(allowed, logits, -1e30)
    row_max = jnp.max(masked, axis=3, keepdims=True)
    exponent = jnp.where(allowed, jnp.exp(masked - row_max), 0.0)
    weights = exponent / jnp.sum(exponent, axis=3, keepdims=True)
    weights_narrow = narrow(weights)
    window_out = jnp.einsum(
        "bhij,bjhd->bihd", weights_narrow, value_blocks, preferred_element_type=jnp.float32
    ).reshape(length, head_count, head_width)
    numer = jnp.einsum(
        "hts,shd->thd", kernel_narrow, value_heads, preferred_element_type=jnp.float32
    ) + jnp.einsum("the,hed->thd", feat_query_f, prefix_state, precision=HIGHEST)
    denom = jnp.sum(kernel, axis=2).T + jnp.einsum(
        "the,he->th", feat_query_f, prefix_norm, precision=HIGHEST
    )
    linear = numer / denom[:, :, None]
    merged = linear + window_out
    gain_heads = gain.reshape(head_count, head_width)
    scaled_cot = cotangent.astype(jnp.float32).reshape(length, head_count, head_width) * gain_heads
    square_sum, cross_sum = lax.psum(
        (jnp.sum(merged * merged, axis=(1, 2)), jnp.sum(scaled_cot * merged, axis=(1, 2))), "head"
    )
    rms = jnp.sqrt(square_sum / full_width + 1e-06)
    normed = (
        (merged / rms[:, None, None] * gain_heads).astype(jnp.bfloat16).reshape(length, local_width)
    )
    grad_out = (scaled_cot - merged * (cross_sum / (full_width * rms * rms))[:, None, None]) / rms[
        :, None, None
    ]
    scaled_grad = grad_out / denom[:, :, None]
    scaled_narrow = narrow(scaled_grad)
    ratio_grad = jnp.sum(grad_out * linear, axis=2) / denom
    suffix_term = jnp.einsum(
        "the,thd->hed", feat_query, scaled_narrow, preferred_element_type=jnp.float32
    )
    suffix_norm_term = jnp.einsum("the,th->he", feat_query_f, ratio_grad, precision=HIGHEST)
    suffix_state, suffix_norm = prefix(
        (suffix_term, suffix_norm_term),
        "seq",
        add_pair,
        (jnp.zeros_like(suffix_term), jnp.zeros_like(suffix_norm_term)),
        True,
    )
    grad_narrow = narrow(grad_out)
    grad_blocks = grad_narrow.reshape(groups, window, head_count, head_width)
    dprob = jnp.einsum(
        "bihd,bjhd->bhij", grad_blocks, value_blocks, preferred_element_type=jnp.float32
    )
    delta = jnp.sum(weights * dprob, axis=3, keepdims=True)
    dlogits = narrow(weights * (dprob - delta))
    grad_window_query = (
        (
            jnp.einsum("bhij,bjhd->bihd", dlogits, key_blocks, preferred_element_type=jnp.float32)
            / math.sqrt(head_width)
        )
        .reshape(length, local_width)
        .astype(jnp.bfloat16)
    )
    key_grads = unblock(
        jnp.einsum("bhij,bihd->bjhd", dlogits, query_blocks, preferred_element_type=jnp.float32)
        / math.sqrt(head_width),
        window,
    )
    value_grads = unblock(
        jnp.einsum(
            "bhij,bihd->bjhd", weights_narrow, grad_blocks, preferred_element_type=jnp.float32
        ),
        window,
    )
    back_key, back_value = (
        passed_along(key_grads[1:window].astype(jnp.bfloat16), "seq", -1).astype(jnp.float32),
        passed_along(value_grads[1:window].astype(jnp.bfloat16), "seq", -1).astype(jnp.float32),
    )
    dscores = (
        jnp.einsum("thd,shd->hts", scaled_narrow, value_heads, preferred_element_type=jnp.float32)
        - ratio_grad.T[:, :, None]
    ) * (1.0 + scores)
    dscores_narrow = narrow(jnp.where(causal, dscores, 0.0))
    local_query = jnp.einsum(
        "hts,shf->thf", dscores_narrow, key_heads, preferred_element_type=jnp.float32
    ) / math.sqrt(features)
    local_key = jnp.einsum(
        "hts,thf->shf", dscores_narrow, query_heads, preferred_element_type=jnp.float32
    ) / math.sqrt(features)
    dfeat_query = (
        jnp.einsum("hed,thd->the", prefix_state, scaled_grad, precision=HIGHEST)
        - ratio_grad[:, :, None] * prefix_norm[None]
    )
    dfeat_key = (
        jnp.einsum("hed,thd->the", suffix_state, value_heads.astype(jnp.float32), precision=HIGHEST)
        - suffix_norm[None]
    )
    grad_query = (
        local_query.reshape(length, head_count * features)
        + taylor_back(query, head_count, features, dfeat_query)
    ).astype(jnp.bfloat16)
    grad_key = (
        local_key.reshape(length, head_count * features)
        + taylor_back(key, head_count, features, dfeat_key)
    ).astype(jnp.bfloat16)
    value_linear = (
        jnp.einsum("hts,thd->shd", kernel_narrow, scaled_narrow, preferred_element_type=jnp.float32)
        + jnp.einsum("the,hed->thd", feat_key_f, suffix_state, precision=HIGHEST)
    ).reshape(length, local_width)
    value_sum = value_linear + value_grads[window:]
    key_sum = key_grads[window:]
    grad_value = jnp.concatenate(
        [value_sum[:cut].astype(jnp.bfloat16), (value_sum[cut:] + back_value).astype(jnp.bfloat16)],
        axis=0,
    )
    grad_window_key = jnp.concatenate(
        [key_sum[:cut].astype(jnp.bfloat16), (key_sum[cut:] + back_key).astype(jnp.bfloat16)],
        axis=0,
    )
    return (normed, grad_query, grad_key, grad_value, grad_window_query, grad_window_key)


def solution(mesh):
    placed = (
        P("seq", "head"),
        P("seq", "head"),
        P("seq", "head"),
        P("seq", "head"),
        P("seq", "head"),
        P("head"),
        P("seq", "head"),
    )
    return jax.shard_map(
        shards,
        mesh=mesh,
        in_specs=placed,
        out_specs=(
            P("seq", "head"),
            P("seq", "head"),
            P("seq", "head"),
            P("seq", "head"),
            P("seq", "head"),
            P("seq", "head"),
        ),
        check_vma=False,
    )
```

profile of v0, /device:TPU:0, one launch (start us, length us, event | category | flops | bytes accessed | tf_op | source)
XLA Modules:
  0.0 221.1 jit_solution(14788666499794375079)
XLA Ops:
  7.2 1.4 convert_multiply_fusion.2
  8.7 1.4 convert_multiply_fusion
  10.3 0.4 pad_maximum_fusion.1
  10.7 0.5 copy-done
  11.2 1.2 fusion.36
  12.5 0.6 slice.84
  13.1 5.5 %collective-permute-start = (bf16[63,512]{1,0:T(8,128)(2,1)}, bf16[63,512]{1,0:T(8,128)(2,1)}, u32[]{:S(2)}, u32[]{:S(2)}) collective-permute-start(bf16[63,512]{1,0:T(8,128)(2,1)} %slice.84), channel_id=1, source_target_pairs={{0,4},{4,8},{8,12},{12,16},{16,20},{20,24},{24,28},{1,5},{5,9},{9,... | collective-permute-start | bytes 193544 | tf_op jit(solution)/shard_map/ppermute | solution.py:20
  18.6 0.6 slice.88
  19.2 3.5 %collective-permute-start.1 = (bf16[63,512]{1,0:T(8,128)(2,1)}, bf16[63,512]{1,0:T(8,128)(2,1)}, u32[]{:S(2)}, u32[]{:S(2)}) collective-permute-start(bf16[63,512]{1,0:T(8,128)(2,1)} %slice.88), channel_id=1, source_target_pairs={{0,4},{4,8},{8,12},{12,16},{16,20},{20,24},{24,28},{1,5},{5,9},{9,... | collective-permute-start | bytes 193544 | tf_op jit(solution)/shard_map/ppermute | solution.py:20
  22.7 2.0 fusion.26
  24.8 0.8 fusion.52
  25.5 1.1 convolution_bitcast_fusion.3
  26.7 0.9 convert_reduce_fusion
  27.7 0.5 slice.110
  28.3 1.2 copy.74
  29.5 32.6 %all-gather.4 = f32[8,4,273]{2,1,0:T(4,128)} all-gather(f32[1,4,273]{2,1,0:T(4,128)} %bitcast.211), channel_id=3, replica_groups=mesh['seq'=8,'head'=4] {'seq'}, dimensions={0}, use_global_device_ids=true | all-gather | bytes 39312 | tf_op jit(solution)/shard_map/all_gather | solution.py:27
  62.2 1.0 pad_maximum_fusion.2
  63.2 0.8 slice.86
  64.2 1.4 fusion.66
  65.6 0.6 copy-done.38
  66.2 1.3 fusion.63
  67.4 1.0 copy_dynamic-update-slice_fusion.3
  68.8 1.1 copy.73
  69.9 24.2 %all-gather.9.cloned.1.call-done = f32[32,273,128]{2,1,0:T(8,128)} async-done(((f32[4,273,128]{2,1,0:T(8,128)}), f32[32,273,128]{2,1,0:T(8,128)}) %all-gather.9.cloned.1.call-update) | async-done | bytes 4472848 | tf_op jit(solution)/shard_map/all_gather | solution.py:27
  94.1 0.4 fusion.57
  94.5 0.6 copy-done.29
  95.1 3.1 %multiply_reduce_fusion.5 = (f32[256]{0:T(256)S(1)}, f32[256]{0:T(256)S(1)}, f32[256,4,128]{0,2,1:T(8,128)}, f32[256,4,128]{0,2,1:T(8,128)}) fusion(f32[256,512]{0,1:T(8,128)S(1)} %copy.74, f32[4,128]{1,0:T(4,128)S(1)} %bitcast.215, f32[256,4,128]{0,2,1:T(8,128)} %copy.73, f32[256,4]{0,1:T(4,128)S(1)} %fusion.61, ...), kind=kOutput, calls=%fused_computation.70 | convolution fusion | flops 430439936 | bytes 3747840 | tf_op jit(solution)/shard_map/the,hed->thd/dot_general | solution.py:157
  98.2 5.6 %all-reduce.4 = (f32[256]{0:T(256)S(1)}, f32[256]{0:T(256)S(1)}) all-reduce(f32[256]{0:T(256)S(1)} %get-tuple-element.144, f32[256]{0:T(256)S(1)} %get-tuple-element.143), channel_id=1, replica_groups=mesh['seq'=8,'head'=4] {'head'}, use_global_device_ids=true, to_apply=%region_7.8 | all-reduce | flops 512 | bytes 4096 | tf_op jit(solution)/shard_map/psum | solution.py:165
  103.9 2.0 fusion.43
  106.0 0.7 copy-done.5
  106.7 1.1 fusion.69
  107.9 0.6 div.102
  108.5 2.4 %fusion.7 = bf16[4,256,256]{1,2,0:T(8,128)(2,1)} fusion(bf16[256,4,128]{0,2,1:T(8,128)(2,1)S(1)} %get-tuple-element.186, f32[4,256,256]{1,2,0:T(8,128)} %get-tuple-element.197, f32[4,256]{1,0:T(4,128)S(1)} %bitcast_divide_fusion, pred[256,256]{0,1:T(8,128)(4,1)S(1)} %copy-done.28, bf16[256,512]{1,0:T(8,128)(2,1)S(1)} %copy-done), kind=kOutput, calls=%fused_computation.16 | convolution fusion | flops 68681728 | bytes 2166784 | tf_op jit(solution)/shard_map/thd,shd->hts/dot_general | solution.py:220
  111.1 0.4 fusion.38
  111.6 0.6 copy-done.15
  112.2 5.5 %fusion.18 = bf16[4,4,64,128]{3,2,1,0:T(8,128)(2,1)S(1)} fusion(f32[4,4,64,128]{3,2,1,0:T(8,128)S(1)} %fusion.38, f32[4,4,64,128]{3,2,1,0:T(8,128)S(1)} %copy-done.15, f32[4,4,64]{2,1,0:T(4,128)S(1)} %copy-done.39), kind=kOutput, calls=%fused_computation.33 | output fusion | flops 787583 | bytes 1314816 | tf_op jit(solution)/shard_map/sub | solution.py:195
  117.7 0.9 copy.94
  119.5 1.3 collective-permute-start.3
  120.8 0.4 convolution_bitcast_fusion.1
  121.7 0.6 slice.122
  122.3 1.5 collective-permute-start.2
  123.8 1.2 fusion.3
  125.2 0.8 copy-done.14
  125.9 0.5 multiply_reduce_fusion.3
  126.4 0.5 fusion.59
  127.0 0.8 fusion.24
  128.7 0.7 copy.161
  130.2 43.3 %all-gather.5 = f32[8,4,273]{2,1,0:T(4,128)S(1)} all-gather(f32[1,4,273]{2,1,0:T(4,128)S(1)} %bitcast.212), channel_id=5, replica_groups=mesh['seq'=8,'head'=4] {'seq'}, dimensions={0}, use_global_device_ids=true | all-gather | bytes 39312 | tf_op jit(solution)/shard_map/all_gather | solution.py:27
  173.5 0.7 pad_maximum_fusion.7
  174.3 26.2 %all-gather.11.cloned.1.call-done = f32[32,273,128]{2,1,0:T(8,128)} async-done(((f32[4,273,128]{2,1,0:T(8,128)}), f32[32,273,128]{2,1,0:T(8,128)}) %all-gather.11.cloned.1.call-update) | async-done | bytes 4472848 | tf_op jit(solution)/shard_map/all_gather | solution.py:27
  200.5 8.5 %while.27 = (s32[]{:T(128)}, f32[4,273,128]{2,1,0:T(8,128)S(1)}, f32[4,273]{1,0:T(4,128)S(1)}, s32[]{:T(128)}, f32[8,4,273,128]{3,2,1,0:T(8,128)}, /*index=5*/f3...) while((s32[]{:T(128)}, f32[4,273,128]{2,1,0:T(8,128)S(1)}, f32[4,273]{1,0:T(4,128)S(1)}, ...), condition=%wide.region_14.15_spmd, body=%wide.region_13.14_spmd.sunk | while | flops 140874 | bytes 1690579 | solution.py:36
  200.5 1.2 bitcast_add_fusion.12
  201.8 1.2 bitcast_add_fusion.12
  203.0 1.2 bitcast_add_fusion.12
  204.2 1.2 bitcast_add_fusion.12
  205.4 1.2 bitcast_add_fusion.12
  206.6 1.2 bitcast_add_fusion.12
  207.8 1.2 bitcast_add_fusion.12
  209.0 0.9 convolution_add_fusion
  210.1 0.6 fusion.2
  211.0 0.9 fusion.50
  211.9 0.7 pad_maximum_fusion.6
  212.6 0.5 multiply_reduce_fusion.1
  213.4 0.9 fusion.25
  (144 shorter events, 5.7 us)
Async XLA Ops:
  7.2 86.9 %all-gather.9.cloned.1.call-start = ((), (), s32[]{:S(2)}) async-start(), calls=%async_computation | async-start | bytes 5160960 | tf_op jit(solution)/shard_map/all_gather | solution.py:27
  10.3 1.0 copy-start
  10.7 7.8 %copy-start.7 = (bf16[256,512]{1,0:T(8,128)(2,1)S(1)}, bf16[256,512]{1,0:T(8,128)(2,1)}, u32[]{:S(2)}) copy-start(bf16[256,512]{1,0:T(8,128)(2,1)} %param.15) | copy-start | bytes 786436
  11.2 11.5 %copy-start.19 = (bf16[256,64]{0,1:T(8,128)(2,1)S(1)}, bf16[256,64]{0,1:T(8,128)(2,1)}, u32[]{:S(2)}) copy-start(bf16[256,64]{0,1:T(8,128)(2,1)} %param.12) | copy-start | bytes 98308
  11.2 11.5 %copy-start.21 = (bf16[256,64]{0,1:T(8,128)(2,1)S(1)}, bf16[256,64]{0,1:T(8,128)(2,1)}, u32[]{:S(2)}) copy-start(bf16[256,64]{0,1:T(8,128)(2,1)} %param.11) | copy-start | bytes 98308
  12.4 188.0 %all-gather.11.cloned.1.call-start = ((), (), s32[]{:S(2)}) async-start(), calls=%async_computation.1 | async-start | bytes 5160960 | tf_op jit(solution)/shard_map/all_gather | solution.py:27
  13.1 49.1 %collective-permute-start = (bf16[63,512]{1,0:T(8,128)(2,1)}, bf16[63,512]{1,0:T(8,128)(2,1)}, u32[]{:S(2)}, u32[]{:S(2)}) collective-permute-start(bf16[63,512]{1,0:T(8,128)(2,1)} %slice.84), channel_id=1, source_target_pairs={{0,4},{4,8},{8,12},{12,16},{16,20},{20,24},{24,28},{1,5},{5,9},{9,... | collective-permute-start | bytes 193544 | tf_op jit(solution)/shard_map/ppermute | solution.py:20
  19.2 43.0 %collective-permute-start.1 = (bf16[63,512]{1,0:T(8,128)(2,1)}, bf16[63,512]{1,0:T(8,128)(2,1)}, u32[]{:S(2)}, u32[]{:S(2)}) collective-permute-start(bf16[63,512]{1,0:T(8,128)(2,1)} %slice.88), channel_id=1, source_target_pairs={{0,4},{4,8},{8,12},{12,16},{16,20},{20,24},{24,28},{1,5},{5,9},{9,... | collective-permute-start | bytes 193544 | tf_op jit(solution)/shard_map/ppermute | solution.py:20
  22.7 2.1 copy-start.27
  24.7 2.9 %copy-start.3 = (bf16[4,256,256]{1,2,0:T(8,128)(2,1)}, bf16[4,256,256]{1,2,0:T(8,128)(2,1)S(1)}, u32[]{:S(2)}) copy-start(bf16[4,256,256]{1,2,0:T(8,128)(2,1)S(1)} %get-tuple-element.179) | copy-start | bytes 1572868
  25.5 2.7 %copy-start.18 = (bf16[256,512]{1,0:T(8,128)(2,1)S(1)}, bf16[256,512]{1,0:T(8,128)(2,1)}, u32[]{:S(2)}) copy-start(bf16[256,512]{1,0:T(8,128)(2,1)} %param.14) | copy-start | bytes 786436
  28.3 35.9 %copy-start.10 = (bf16[4,64,4,128]{3,2,1,0:T(4,128)(2,1)}, bf16[4,64,4,128]{3,2,1,0:T(4,128)(2,1)S(1)}, u32[]{:S(2)}) copy-start(bf16[4,64,4,128]{3,2,1,0:T(4,128)(2,1)S(1)} %reshape.162) | copy-start | bytes 786436
  63.2 1.0 copy-start.31
  64.2 3.2 %copy-start.8 = (bf16[4,128,4,128]{3,1,2,0:T(8,128)(2,1)}, bf16[4,128,4,128]{3,1,2,0:T(8,128)(2,1)S(1)}, u32[]{:S(2)}) copy-start(bf16[4,128,4,128]{3,1,2,0:T(8,128)(2,1)S(1)} %copy_dynamic-update-slice_fusion) | copy-start | bytes 1572868
  65.6 0.6 copy-start.38
  94.1 1.0 copy-start.33
  94.1 1.0 copy-start.37
  94.1 4.1 %copy-start.16 = (f32[4,273]{1,0:T(4,128)}, f32[4,273]{1,0:T(4,128)S(1)}, u32[]{:S(2)}) copy-start(f32[4,273]{1,0:T(4,128)S(1)} %get-tuple-element.122) | copy-start | bytes 13108
  94.5 0.6 copy-start.29
  95.1 3.1 %copy-start.23 = (f32[256,4]{0,1:T(4,128)}, f32[256,4]{0,1:T(4,128)S(1)}, u32[]{:S(2)}) copy-start(f32[256,4]{0,1:T(4,128)S(1)} %fusion.61) | copy-start | bytes 12292
  103.9 2.0 copy-start.1
  103.9 2.0 copy-start.24
  103.9 2.1 copy-start.35
  105.9 0.9 copy-start.5
  106.7 1.2 copy-start.25
  106.7 1.8 copy-start.30
  106.7 1.8 copy-start.34
  106.7 1.8 copy-start.28
  111.1 1.0 copy-start.15
  111.1 1.0 copy-start.39
  112.2 5.5 %copy-start.12 = (bf16[256,4,128]{0,2,1:T(8,128)(2,1)S(1)}, bf16[256,4,128]{0,2,1:T(8,128)(2,1)}, u32[]{:S(2)}) copy-start(bf16[256,4,128]{0,2,1:T(8,128)(2,1)} %get-tuple-element.184) | copy-start | bytes 786436
  112.2 6.4 %copy-start.11 = (bf16[4,64,4,128]{3,2,1,0:T(4,128)(2,1)S(1)}, bf16[4,64,4,128]{3,2,1,0:T(4,128)(2,1)}, u32[]{:S(2)}) copy-start(bf16[4,64,4,128]{3,2,1,0:T(4,128)(2,1)} %copy-done.10) | copy-start | bytes 786436
  119.5 54.0 %collective-permute-start.3 = (bf16[63,512]{1,0:T(8,128)(2,1)S(1)}, bf16[63,512]{1,0:T(8,128)(2,1)S(1)}, u32[]{:S(2)}, u32[]{:S(2)}) collective-permute-start(bf16[63,512]{1,0:T(8,128)(2,1)S(1)} %slice.129), channel_id=1, source_target_pairs={{4,0},{8,4},{12,8},{16,12},{20,16},{24,20},{28,24},{5,1},{9,5},{13... | collective-permute-start | bytes 193544 | tf_op jit(solution)/shard_map/ppermute | solution.py:20
  121.2 2.6 %copy-start.6 = (f32[256,4,128]{0,2,1:T(8,128)S(1)}, f32[256,4,128]{0,2,1:T(8,128)}, u32[]{:S(2)}) copy-start(f32[256,4,128]{0,2,1:T(8,128)} %copy-done.5) | copy-start | bytes 1572868
  121.2 2.6 %copy-start.17 = (f32[4,273]{1,0:T(4,128)S(1)}, f32[4,273]{1,0:T(4,128)}, u32[]{:S(2)}) copy-start(f32[4,273]{1,0:T(4,128)} %copy-done.16) | copy-start | bytes 13108
  121.2 2.6 %copy-start.26 = (f32[256,4]{0,1:T(4,128)S(1)}, f32[256,4]{0,1:T(4,128)}, u32[]{:S(2)}) copy-start(f32[256,4]{0,1:T(4,128)} %copy-done.23) | copy-start | bytes 12292
  121.2 2.6 %copy-start.32 = (f32[256,4]{0,1:T(4,128)S(1)}, f32[256,4]{0,1:T(4,128)}, u32[]{:S(2)}) copy-start(f32[256,4]{0,1:T(4,128)} %div.102) | copy-start | bytes 12292
  121.2 2.6 %copy-start.36 = (f32[256]{0:T(256)S(1)}, f32[256]{0:T(256)}, u32[]{:S(2)}) copy-start(f32[256]{0:T(256)} %copy-done.35) | copy-start | bytes 3076
  122.3 88.7 %collective-permute-start.2 = (bf16[63,512]{1,0:T(8,128)(2,1)}, bf16[63,512]{1,0:T(8,128)(2,1)}, u32[]{:S(2)}, u32[]{:S(2)}) collective-permute-start(bf16[63,512]{1,0:T(8,128)(2,1)} %slice.122), channel_id=1, source_target_pairs={{4,0},{8,4},{12,8},{16,12},{20,16},{24,20},{28,24},{5,1},{9,5},{13... | collective-permute-start | bytes 193544 | tf_op jit(solution)/shard_map/ppermute | solution.py:20
  125.1 0.8 copy-start.14
  125.9 1.1 copy-start.2
  125.9 1.1 copy-start.20
  126.4 1.4 copy-start.9
  126.4 1.7 copy-start.4
  210.9 1.7 copy-start.13
  212.6 0.8 copy-start.22
Sparse Core Ops, SparseCore 0:
  12.5 81.4 all-gather.8
  108.0 92.3 all-gather.10
where the time goes:
time: 222 us; the launch traced here: 221 us
  blocking collectives  81.6 us (37%)
  waiting for transfers between devices  50.4 us (23%)
  other arithmetic  27.6 us (12%)
  matrix products  19.6 us (9%)
  local copies, waits for them, and re-layouts  15.2 us (7%)
  between operations  14.7 us (7%)
  starting transfers between devices  11.7 us (5%)
    all_gather x2, blocking collectives, prefix(): gathered = jax.tree.map(lambda a: lax.all_gather(a, axis), part)  75.9 us
    all_gather x2, waiting for transfers between devices, prefix(): gathered = jax.tree.map(lambda a: lax.all_gather(a, axis), part)  50.3 us
    ppermute x4, starting transfers between devices, passed_along(): return lax.ppermute(block, axis, route)  11.7 us
    add x14, other arithmetic, add_pair(): return (earlier[0] + later[0], earlier[1] + later[1])  8.32 us
    unnamed x87, local copies, waits for them, and re-layouts  7 us
    psum x1, blocking collectives, shards(): lax.psum((jnp.sum(merged * merged, axis=(1, 2)), jnp.sum(scaled_cot * mer...  5.65 us
    sub x1, other arithmetic, shards(): dlogits = narrow(weights * (dprob - delta))  5.52 us
  transfers between devices with their start and end apart: 6, of which 2 were waited for; matrix products, arithmetic and copies ran while one was open for 20% of the time, Pallas kernels for 0%

commit v1 on v0

v1 whole, which is shorter than its diff:
```python
import math

import jax
import jax.numpy as jnp
import numpy as np
from jax import lax
from jax.experimental import pallas as pl
from jax.experimental.pallas import tpu as pltpu
from jax.sharding import PartitionSpec as P

HEADS = 16
HEAD_DIM = 128
FEAT = 16
WINDOW = 64
CHUNKS = 2

QUAD = FEAT * (FEAT + 1) // 2
LINEAR = QUAD
CONST = QUAD + FEAT
ROWS = 160
ROOT_HALF = float(np.float32(math.sqrt(0.5)))
SCORE = 1.0 / math.sqrt(FEAT)

F32 = jnp.float32
BF16 = jnp.bfloat16
VMEM_LIMIT = 24 * 1024 * 1024


def feature_tables():
    first = np.zeros((ROWS, FEAT), np.float32)
    second = np.zeros((ROWS, FEAT), np.float32)
    rows = np.zeros((8, ROWS), np.float32)
    scale = FEAT ** (-0.25)
    place = 0
    for distance in range(FEAT // 2 + 1):
        for i in range(FEAT if distance < FEAT // 2 else FEAT // 2):
            first[place, i] = scale
            second[place, (i + distance) % FEAT] = scale
            rows[2, place] = ROOT_HALF * (1.0 if distance == 0 else 2.0)
            place += 1
    for i in range(FEAT):
        first[LINEAR + i, i] = scale
    rows[1, LINEAR:CONST] = 1.0
    rows[0:2, CONST] = 1.0
    rows[2, LINEAR : CONST + 1] = 1.0
    sel = np.concatenate([first, second], axis=0)
    sel_t = np.concatenate([first.T, second.T], axis=0)
    return jnp.asarray(sel, BF16), jnp.asarray(sel_t, BF16), jnp.asarray(rows)


def mm(a, b):
    return lax.dot_general(a, b, (((1,), (0,)), ((), ())), preferred_element_type=F32)


def mm_nt(a, b):
    return lax.dot_general(a, b, (((1,), (1,)), ((), ())), preferred_element_type=F32)


def mm_tn(a, b):
    return lax.dot_general(a, b, (((0,), (0,)), ((), ())), preferred_element_type=F32)


def halves(x):
    high = x.astype(BF16)
    return high, (x - high.astype(F32)).astype(BF16)


def lane_sum(x):
    return jnp.sum(x, axis=1, keepdims=True)


def span(h, size):
    return slice(h * size, (h + 1) * size)


def iota(shape, axis):
    return lax.broadcasted_iota(jnp.int32, shape, axis)


def stack8(lines):
    count = -(-len(lines) // 8) * 8
    place = iota((count, lines[0].shape[1]), 0)
    out = jnp.zeros(place.shape, F32)
    for i, line in enumerate(lines):
        out = jnp.where(place == i, line, out)
    return out.astype(BF16)


def split(x):
    high = x.astype(BF16).astype(F32)
    return high, (x - high).astype(BF16).astype(F32)


def feature_rows(inputs_t, sel):
    a = mm(sel[:ROWS], inputs_t)
    b = mm(sel[ROWS : ROWS + QUAD], inputs_t)
    tail = (iota((ROWS - CONST, inputs_t.shape[1]), 0) == 0).astype(F32)
    return jnp.concatenate([a[:QUAD] * b * ROOT_HALF, a[LINEAR:CONST], tail], axis=0).astype(BF16)


def weighted_features(inputs_t, sel_t, rows):
    a = mm_tn(inputs_t, sel_t[:FEAT]) + rows[0:1]
    b = mm_tn(inputs_t, sel_t[FEAT:]) + rows[1:2]
    return (a * b * rows[2:3]).astype(BF16)


def pull_back(upstream, inputs_t, sel, sel_t):
    a = mm(sel[:QUAD], inputs_t)
    b = mm(sel[ROWS : ROWS + QUAD], inputs_t)
    squares = upstream[:FEAT] * ROOT_HALF
    others = upstream[FEAT:QUAD] * (2.0 * ROOT_HALF)
    on_first = jnp.concatenate([squares * b[:FEAT], others * b[FEAT:], upstream[LINEAR:CONST]], axis=0)
    on_second = jnp.concatenate([squares * a[:FEAT], others * a[FEAT:]], axis=0)
    first_high, first_low = halves(on_first)
    second_high, second_low = halves(on_second)
    first_t = sel_t[:FEAT, :CONST]
    second_t = sel_t[FEAT:, :QUAD]
    return (mm(first_t, first_high) + mm(second_t, second_high)) + (mm(first_t, first_low) + mm(second_t, second_low))


def norm_tile(norm):
    high, low = split(norm)
    pad = jnp.zeros((1, 256 - ROWS), F32)
    row = iota((8, 128), 0)
    out = jnp.where(row == 1, high[:, :128], 0.0)
    out = jnp.where(row == 2, jnp.concatenate([high[:, 128:], pad], axis=1), out)
    out = jnp.where(row == 3, low[:, :128], out)
    return jnp.where(row == 4, jnp.concatenate([low[:, 128:], pad], axis=1), out)


def tile_norm(tile):
    return jnp.concatenate([tile[1:2] + tile[3:4], (tile[2:3] + tile[4:5])[:, : ROWS - 128]], axis=1)


def outer(pairs):
    left, right = [], []
    for a, b in pairs:
        a_high, a_low = split(a)
        b_high, b_low = split(b)
        left += [a_high, a_low, a_high]
        right += [b_high, b_high, b_low]
    return mm_tn(stack8(left), stack8(right))


def store_state(out_ref, head, state, tile):
    row = iota((8, 128), 0)
    last = jnp.where(row == 0, state[CONST:], tile)
    out_ref[span(head, ROWS), :] = jnp.concatenate([state[:CONST], last], axis=0).astype(BF16)


def causal_mask(length):
    return iota((length, length), 0) >= iota((length, length), 1)


def state_body(key_hbm, value_hbm, wkey_hbm, sel_hbm, sel_t_hbm, rows_hbm, *refs):
    states = refs[:CHUNKS]
    rim_ref, key_ref, value_ref, sel_ref, sel_t_ref, rows_ref, sems = refs[CHUNKS:]
    length, width = value_ref.shape
    heads = width // HEAD_DIM
    cut = length - WINDOW
    pairs = [
        (key_hbm, key_ref),
        (sel_hbm, sel_ref),
        (value_hbm, value_ref),
        (wkey_hbm.at[cut:length, :], rim_ref.at[0:WINDOW, :]),
        (value_hbm.at[cut:length, :], rim_ref.at[WINDOW : 2 * WINDOW, :]),
        (sel_t_hbm, sel_t_ref),
        (rows_hbm, rows_ref),
    ]
    copies = [pltpu.make_async_copy(a, b, sems.at[i]) for i, (a, b) in enumerate(pairs)]
    for copy in copies:
        copy.start()
    for copy in copies[:3]:
        copy.wait()
    sel = sel_ref[...]
    ones = jnp.ones((8, length), BF16)
    place = iota((8, 128), 0)
    for h in range(heads):
        feat = feature_rows(key_ref[span(h, FEAT), :], sel)
        state = mm(feat, value_ref[:, span(h, HEAD_DIM)])
        norm = mm_nt(ones, feat)[0:1]
        middle = (state[CONST : CONST + 1] * (1.0 / length)).astype(BF16).astype(F32)
        high, low = split(norm)
        state = state - mm_tn(stack8([high, low]), stack8([middle, middle]))
        tile = jnp.where(place == 5, middle, norm_tile(norm))
        per = heads // CHUNKS
        store_state(states[h // per], h % per, state, tile)
    for copy in copies[3:]:
        copy.wait()


def add_about_body(mine_ref, theirs_ref, out_ref):
    place = iota((8, 128), 0)
    for h in range(mine_ref.shape[0] // ROWS):
        mine = mine_ref[span(h, ROWS), :].astype(F32)
        theirs = theirs_ref[span(h, ROWS), :].astype(F32)
        mine_tile, their_tile = mine[CONST:], theirs[CONST:]
        mine_norm, their_norm = tile_norm(mine_tile), tile_norm(their_tile)
        mine_middle, their_middle = mine_tile[5:6], their_tile[5:6]
        middle = (0.5 * (mine_middle + their_middle)).astype(BF16).astype(F32)
        moved = outer([(mine_norm, mine_middle - middle), (their_norm, their_middle - middle)])
        tile = jnp.where(place == 5, middle, norm_tile(mine_norm + their_norm))
        store_state(out_ref, h, mine + theirs + moved, tile)


def add_body(mine_ref, theirs_ref, out_ref):
    for h in range(mine_ref.shape[0] // ROWS):
        total = mine_ref[span(h, ROWS), :].astype(F32) + theirs_ref[span(h, ROWS), :].astype(F32)
        store_state(out_ref, h, total, norm_tile(tile_norm(total[CONST:])))


def local_body(query_hbm, wquery_hbm, wkey_hbm, cot_hbm, gain_hbm, key_ref, value_ref, sel_ref, sel_t_ref, rows_ref,
               numer_ref, denom_ref, featq_ref, featq_t_ref, featk_ref, query_ref, wquery_ref, wkey_ref, cot_ref, gain_ref, sems):
    pairs = [(query_hbm, query_ref), (wquery_hbm, wquery_ref), (wkey_hbm, wkey_ref), (cot_hbm, cot_ref), (gain_hbm, gain_ref)]
    copies = [pltpu.make_async_copy(a, b, sems.at[i]) for i, (a, b) in enumerate(pairs)]
    for copy in copies:
        copy.start()
    length = value_ref.shape[0]
    heads = value_ref.shape[1] // HEAD_DIM
    sel = sel_ref[...]
    sel_t = sel_t_ref[...]
    rows = rows_ref[...]
    for h in range(heads):
        featk_ref[h] = weighted_features(key_ref[span(h, FEAT), :], sel_t, rows)
    copies[0].wait()
    causal = causal_mask(length)
    lane = iota((length, 128), 1)
    denoms = jnp.zeros((length, 128), F32)
    for h in range(heads):
        query = query_ref[span(h, FEAT), :]
        featq_t_ref[span(h, ROWS), :] = feature_rows(query, sel)
        featq_ref[h] = weighted_features(query, sel_t, rows)
        scores = mm_tn(query, key_ref[span(h, FEAT), :]) * SCORE
        kernel = jnp.where(causal, 1.0 + scores + 0.5 * scores * scores, 0.0)
        denoms = jnp.where(lane == h, lane_sum(kernel), denoms)
        numer_ref[:, span(h, HEAD_DIM)] = mm(kernel.astype(BF16), value_ref[:, span(h, HEAD_DIM)])
    denom_ref[...] = denoms
    for copy in copies[1:]:
        copy.wait()


def window_body(place_ref, wquery_ref, wkey_ref, value_ref, rim_ref, out_ref, weights_ref):
    length = wquery_ref.shape[0]
    heads = value_ref.shape[1] // HEAD_DIM
    live = place_ref[0] > 0
    row = iota((WINDOW, 2 * WINDOW), 0)
    col = iota((WINDOW, 2 * WINDOW), 1)
    inside = (col > row) & (col <= row + WINDOW)
    edge = inside & ((col >= WINDOW) | live)
    starts = range(0, length, WINDOW)
    allowed = jnp.concatenate([edge] + [inside] * (len(starts) - 1), axis=0)
    for h in range(heads):
        columns = span(h, HEAD_DIM)
        keys = jnp.concatenate([rim_ref[:WINDOW, columns], wkey_ref[:, columns]], axis=0)
        values = jnp.concatenate([rim_ref[WINDOW:, columns], value_ref[:, columns]], axis=0)
        query = wquery_ref[:, columns]
        logits = jnp.concatenate([mm_nt(query[s : s + WINDOW], keys[s : s + 2 * WINDOW]) for s in starts], axis=0)
        masked = jnp.where(allowed, logits * (1.0 / math.sqrt(HEAD_DIM)), -1e30)
        exponent = jnp.where(allowed, jnp.exp(masked - jnp.max(masked, axis=1, keepdims=True)), 0.0)
        weights = exponent * (1.0 / lane_sum(exponent))
        weights_ref[h] = weights
        narrow = weights.astype(BF16)
        out_ref[:, columns] = jnp.concatenate([mm(narrow[s : s + WINDOW], values[s : s + 2 * WINDOW]) for s in starts], axis=0)


def taken(place_ref, step, later):
    bit = (place_ref[0] >> step) & 1
    return (1 - bit if later else bit).astype(F32)


def merge_body(steps, chunk, place_ref, *refs):
    parts = refs[:steps]
    feat_ref, numer_ref, denom_ref, window_ref, gain_ref, cot_ref = refs[steps : steps + 6]
    before = refs[steps + 6 : steps + 6 + (2 if chunk else 0)]
    outs = refs[steps + 6 + len(before) :]
    merged_ref, linear_ref, inverse_ref, prefix_ref, norm_ref = outs[:5]
    length = numer_ref.shape[0]
    per = merged_ref.shape[1] // HEAD_DIM
    lane = iota((length, 128), 1)
    inverses = jnp.zeros((length, 128), F32)
    squares = before[0][...] if chunk else jnp.zeros((length, HEAD_DIM), F32)
    crosses = before[1][...] if chunk else jnp.zeros((length, HEAD_DIM), F32)
    for h in range(per):
        whole = chunk * per + h
        state = norm = None
        left, right = [], []
        for step, part in enumerate(parts):
            take = taken(place_ref, step, False)
            block = part[span(h, ROWS), :].astype(F32) * take
            block_norm = tile_norm(block[CONST:])
            middle = part[span(h, ROWS), :].astype(F32)[CONST + 5 : CONST + 6]
            left += list(split(block_norm))
            right += [middle, middle]
            state = block if state is None else state + block
            norm = block_norm if norm is None else norm + block_norm
        state = state + mm_tn(stack8(left), stack8(right))
        prefix_ref[span(h, ROWS), :] = state
        norm_ref[span(h, 8), :] = jnp.broadcast_to(norm, (8, ROWS))
        high, low = halves(state)
        feat = feat_ref[whole]
        numer = numer_ref[:, span(whole, HEAD_DIM)] + mm(feat, high) + mm(feat, low)
        extra = mm_nt(feat, stack8(list(split(norm))))
        inverse = 1.0 / (denom_ref[:, whole : whole + 1] + (extra[:, 0:1] + extra[:, 1:2]))
        inverses = jnp.where(lane == h, inverse, inverses)
        linear = numer * inverse
        linear_ref[:, span(h, HEAD_DIM)] = linear
        merged = linear + window_ref[:, span(whole, HEAD_DIM)]
        merged_ref[:, span(h, HEAD_DIM)] = merged
        squares = squares + merged * merged
        scaled_cot = cot_ref[:, span(whole, HEAD_DIM)].astype(F32) * gain_ref[0:1, span(whole, HEAD_DIM)]
        crosses = crosses + scaled_cot * merged
    inverse_ref[...] = inverses
    if chunk + 1 < CHUNKS:
        outs[5][...] = squares
        outs[6][...] = crosses
    else:
        stats = jnp.where(lane == 0, lane_sum(squares), jnp.where(lane == 1, lane_sum(crosses), 0.0))
        outs[5][...] = jnp.transpose(stats)[:8]


def grad_body(width, stats_ref, *refs):
    merged_refs, linear_refs, inverse_refs = refs[:CHUNKS], refs[CHUNKS : 2 * CHUNKS], refs[2 * CHUNKS : 3 * CHUNKS]
    gain_ref, cot_ref, feat_t_ref = refs[3 * CHUNKS : 3 * CHUNKS + 3]
    terms = refs[3 * CHUNKS + 3 : 4 * CHUNKS + 3]
    grad_ref, cols_ref, ratios_ref = refs[4 * CHUNKS + 3 :]
    length = grad_ref.shape[0]
    heads = grad_ref.shape[1] // HEAD_DIM
    per = heads // CHUNKS
    sums = jnp.transpose(jnp.concatenate([stats_ref[...], jnp.zeros((120, length), F32)], axis=0))
    mean = sums[:, 0:1] / width + 1e-6
    inv_rms = 1.0 / jnp.sqrt(mean)
    pull = sums[:, 1:2] / (width * mean)
    lane = iota((length, 128), 1)
    cols = jnp.where(lane == heads, inv_rms, 0.0)
    narrows = []
    for h in range(heads):
        chunk, local = h // per, span(h % per, HEAD_DIM)
        inverse = inverse_refs[chunk][:, h % per : h % per + 1]
        scaled_cot = cot_ref[:, span(h, HEAD_DIM)].astype(F32) * gain_ref[0:1, span(h, HEAD_DIM)]
        grad = (scaled_cot - merged_refs[chunk][:, local] * pull) * inv_rms
        grad_ref[:, span(h, HEAD_DIM)] = grad
        narrows.append((grad * inverse).astype(BF16))
        cols = jnp.where(lane == h, lane_sum(grad * linear_refs[chunk][:, local]) * inverse, cols)
    cols_ref[...] = cols
    ratios = jnp.transpose(cols)[:8]
    ratios_ref[...] = ratios
    for h in range(heads):
        feat = feat_t_ref[span(h, ROWS), :]
        norm = mm_nt(stack8(list(split(ratios[h : h + 1]))), feat)
        store_state(terms[h // per], h % per, mm(feat, narrows[h]), norm_tile(norm[0:1] + norm[1:2]))


def window_back_body(wquery_ref, wkey_ref, value_ref, rim_ref, weights_ref, grad_ref, gwq_ref, gwk_ref, gv_ref, back_ref):
    length = wquery_ref.shape[0]
    heads = value_ref.shape[1] // HEAD_DIM
    root = 1.0 / math.sqrt(HEAD_DIM)
    starts = range(0, length, WINDOW)
    pad = jnp.zeros((WINDOW, HEAD_DIM), F32)
    for h in range(heads):
        columns = span(h, HEAD_DIM)
        keys = jnp.concatenate([rim_ref[:WINDOW, columns], wkey_ref[:, columns]], axis=0)
        values = jnp.concatenate([rim_ref[WINDOW:, columns], value_ref[:, columns]], axis=0)
        grad = grad_ref[:, columns].astype(BF16)
        query = wquery_ref[:, columns]
        weights = weights_ref[h]
        narrow = weights.astype(BF16)
        dprob = jnp.concatenate([mm_nt(grad[s : s + WINDOW], values[s : s + 2 * WINDOW]) for s in starts], axis=0)
        dlogits = (weights * (dprob - lane_sum(weights * dprob))).astype(BF16)
        grads = [mm(dlogits[s : s + WINDOW], keys[s : s + 2 * WINDOW]) for s in starts]
        gwq_ref[:, columns] = (jnp.concatenate(grads, axis=0) * root).astype(BF16)
        key_parts = [mm_tn(dlogits[s : s + WINDOW], query[s : s + WINDOW]) for s in starts]
        value_parts = [mm_tn(narrow[s : s + WINDOW], grad[s : s + WINDOW]) for s in starts]
        back_ref[:WINDOW, columns] = (key_parts[0][:WINDOW] * root).astype(BF16)
        back_ref[WINDOW:, columns] = value_parts[0][:WINDOW].astype(BF16)
        key_sum = [a[WINDOW:] + b[:WINDOW] for a, b in zip(key_parts, key_parts[1:] + [pad])]
        value_sum = [a[WINDOW:] + b[:WINDOW] for a, b in zip(value_parts, value_parts[1:] + [pad])]
        gwk_ref[:, columns] = jnp.concatenate(key_sum, axis=0) * root
        gv_ref[:, columns] = jnp.concatenate(value_sum, axis=0)


def local_back_body(query_ref, key_ref, value_ref, sel_ref, sel_t_ref, grad_ref, cols_ref, ratios_ref, gv_in_ref, gain_ref, *refs):
    merged_refs, inverse_refs = refs[:CHUNKS], refs[CHUNKS : 2 * CHUNKS]
    prefix_refs, norm_refs = refs[2 * CHUNKS : 3 * CHUNKS], refs[3 * CHUNKS : 4 * CHUNKS]
    gq_ref, gk_ref, gv_ref, normed_ref = refs[4 * CHUNKS :]
    length = value_ref.shape[0]
    heads = value_ref.shape[1] // HEAD_DIM
    per = heads // CHUNKS
    sel = sel_ref[...]
    sel_t = sel_t_ref[...]
    causal = causal_mask(length)
    inv_rms = cols_ref[:, heads : heads + 1]
    for h in range(heads):
        chunk, columns = h // per, span(h, HEAD_DIM)
        merged = merged_refs[chunk][:, span(h % per, HEAD_DIM)]
        normed_ref[:, columns] = (merged * inv_rms * gain_ref[0:1, columns]).astype(BF16)
        scaled = grad_ref[:, columns] * inverse_refs[chunk][:, h % per : h % per + 1]
        narrow, rest = halves(scaled)
        query = query_ref[span(h, FEAT), :]
        key = key_ref[span(h, FEAT), :]
        scores = mm_tn(query, key) * SCORE
        kernel = jnp.where(causal, 1.0 + scores + 0.5 * scores * scores, 0.0).astype(BF16)
        dscores = (mm_nt(narrow, value_ref[:, columns]) - cols_ref[:, h : h + 1]) * (1.0 + scores)
        dscores = jnp.where(causal, dscores, 0.0).astype(BF16)
        gk_ref[span(h, FEAT), :] = mm(query, dscores) * SCORE
        gv_ref[:, columns] = gv_in_ref[:, columns] + mm_tn(kernel, narrow)
        high, low = halves(prefix_refs[chunk][span(h % per, ROWS), :])
        upstream = mm_nt(high, narrow) + (mm_nt(low, narrow) + mm_nt(high, rest))
        upstream = upstream - outer([(norm_refs[chunk][h % per * 8 : h % per * 8 + 1, :], ratios_ref[h : h + 1, :])])
        through = pull_back(upstream, query, sel, sel_t)
        gq_ref[span(h, FEAT), :] = (mm_nt(key, dscores) * SCORE + through).astype(BF16)


def final_body(steps, chunk, place_ref, *refs):
    parts = refs[:steps]
    key_ref, value_ref, sel_ref, sel_t_ref, feat_ref, gk_in_ref, gv_in_ref, back_ref = refs[steps : steps + 8]
    rest = refs[steps + 8 :]
    length = value_ref.shape[0]
    per = parts[0].shape[0] // ROWS
    cut = length - WINDOW
    sel = sel_ref[...]
    sel_t = sel_t_ref[...]
    ones = jnp.where(iota((8, length), 0) < 2, 1.0, 0.0).astype(BF16)
    if chunk + 1 < CHUNKS:
        gwk_in_ref, gk_ref, gv_ref, gwk_ref = rest
        gwk_ref[:cut, :] = gwk_in_ref[:cut, :].astype(BF16)
        gwk_ref[cut:, :] = (gwk_in_ref[cut:, :] + back_ref[:WINDOW, :].astype(F32)).astype(BF16)
        base = 0
    else:
        gk_before, gv_before, gk_ref, gv_ref = rest
        base = chunk * per
        gk_ref[: base * FEAT, :] = gk_before[...]
        gv_ref[:, : base * HEAD_DIM] = gv_before[...]
    for h in range(per):
        whole = chunk * per + h
        columns = span(whole, HEAD_DIM)
        state = None
        for step, part in enumerate(parts):
            block = part[span(h, ROWS), :].astype(F32) * taken(place_ref, step, True)
            state = block if state is None else state + block
        high, low = halves(state)
        value = value_ref[:, columns]
        grad_value = gv_in_ref[:, columns] + (mm(feat_ref[whole], high) + mm(feat_ref[whole], low))
        out_columns = span(base + h, HEAD_DIM)
        gv_ref[:cut, out_columns] = grad_value[:cut].astype(BF16)
        gv_ref[cut:, out_columns] = (grad_value[cut:] + back_ref[WINDOW:, columns].astype(F32)).astype(BF16)
        norm = mm_tn(stack8(list(split(tile_norm(state[CONST:])))), ones)
        upstream = mm_nt(high, value) + mm_nt(low, value) - norm
        through = pull_back(upstream, key_ref[span(whole, FEAT), :], sel, sel_t)
        gk_ref[span(base + h, FEAT), :] = (gk_in_ref[span(whole, FEAT), :] + through).astype(BF16)


def call(body, outs, *args, place=None, hbm=0, copies=0):
    vmem = pl.BlockSpec(memory_space=pltpu.VMEM)
    specs = [pl.BlockSpec(memory_space=pltpu.HBM)] * hbm + [vmem] * (len(args) - hbm)
    args = tuple(pltpu.with_memory_space_constraint(a, pltpu.HBM) if i < hbm else a for i, a in enumerate(args))
    if place is not None:
        specs = [pl.BlockSpec(memory_space=pltpu.SMEM)] + specs
        args = (place,) + args
    return pl.pallas_call(
        body,
        out_shape=[jax.ShapeDtypeStruct(shape, dtype) for shape, dtype in outs],
        in_specs=specs,
        out_specs=[vmem] * len(outs),
        scratch_shapes=[pltpu.SemaphoreType.DMA((copies,))] if copies else [],
        compiler_params=pltpu.CompilerParams(vmem_limit_bytes=VMEM_LIMIT),
    )(*args)


def exchanged(states, add, after_first):
    count = lax.axis_size("seq")
    states = list(states)
    parts = [[] for _ in states]
    extra = None
    step = 1
    while step < count:
        pairs = [(i, i ^ step) for i in range(count)]
        for c, state in enumerate(states):
            parts[c].append(lax.ppermute(state, "seq", pairs))
        if extra is None:
            extra = after_first()
        step *= 2
        if step < count:
            for c, state in enumerate(states):
                (states[c],) = call(add, [(state.shape, BF16)], state, parts[c][-1])
    return parts, states, extra


def shards(query, key, value, window_query, window_key, gain, cotangent):
    length, width = value.shape
    heads = width // HEAD_DIM
    per = heads // CHUNKS
    count = lax.axis_size("seq")
    full_width = HEADS * HEAD_DIM
    place = lax.axis_index("seq").astype(jnp.int32).reshape(1)
    gain_row = gain.reshape(1, width)
    query_t, key_t = query.T, key.T
    state_shape = ((per * ROWS, HEAD_DIM), BF16)
    wide = ((length, width), F32)
    wide_narrow = ((length, width), BF16)
    tables = feature_tables()

    *states, rim, key_v, value_v, sel, sel_t, rows = call(
        state_body,
        [state_shape] * CHUNKS
        + [((2 * WINDOW, width), BF16), (key_t.shape, BF16), wide_narrow]
        + [(t.shape, t.dtype) for t in tables],
        key_t, value, window_key, *tables, hbm=6, copies=7,
    )

    def early():
        rim_in = lax.ppermute(rim, "seq", [(i, i + 1) for i in range(count - 1)])
        local = call(
            local_body,
            [wide, ((length, 128), F32), ((heads, length, ROWS), BF16), ((heads * ROWS, length), BF16), ((heads, length, ROWS), BF16),
             (query_t.shape, BF16), wide_narrow, wide_narrow, wide_narrow, (gain_row.shape, F32)],
            query_t, window_query, window_key, cotangent, gain_row, key_v, value_v, sel, sel_t, rows, hbm=5, copies=5,
        )
        return rim_in, local

    parts, _, (rim_in, local) = exchanged(states, add_about_body, early)
    numer, denom, featq, featq_t, featk, query_v, wquery, wkey, cot, gain_v = local
    window_out, weights = call(
        window_body, [wide, ((heads, length, 2 * WINDOW), F32)], wquery, wkey, value_v, rim_in, place=place
    )
    steps = len(parts[0])
    half = ((length, per * HEAD_DIM), F32)
    square = ((length, 128), F32)
    merged, linear, inverse, prefix, norm, before = [], [], [], [], [], []
    for c in range(CHUNKS):
        tail = [((8, length), F32)] if c + 1 == CHUNKS else [square, square]
        out = call(
            lambda *refs, c=c: merge_body(steps, c, *refs),
            [half, half, square, ((per * ROWS, HEAD_DIM), F32), ((per * 8, ROWS), F32)] + tail,
            *parts[c], featq, numer, denom, window_out, gain_v, cot, *before, place=place,
        )
        for held, item in zip((merged, linear, inverse, prefix, norm), out):
            held.append(item)
        before = out[5:]
    (stats,) = before
    ring = lax.axis_size("head")
    step = 1
    while step < ring:
        stats = stats + lax.ppermute(stats, "head", [(i, i ^ step) for i in range(ring)])
        step *= 2
    *terms, grad, cols, ratios = call(
        lambda *refs: grad_body(float(full_width), *refs),
        [state_shape] * CHUNKS + [wide, square, ((8, length), F32)],
        stats, *merged, *linear, *inverse, gain_v, cot, featq_t,
    )

    def middle():
        grad_wquery, wkey_part, value_part, back = call(
            window_back_body,
            [wide_narrow, wide, wide, ((2 * WINDOW, width), BF16)],
            wquery, wkey, value_v, rim_in, weights, grad,
        )
        back = lax.ppermute(back, "seq", [(i + 1, i) for i in range(count - 1)])
        return grad_wquery, wkey_part, value_part, back

    parts, _, (grad_wquery, wkey_part, value_part, back) = exchanged(terms, add_body, middle)
    grad_query, key_part, value_part, normed = call(
        local_back_body,
        [(query_t.shape, BF16), (key_t.shape, F32), wide, wide_narrow],
        query_v, key_v, value_v, sel, sel_t, grad, cols, ratios, value_part, gain_v, *merged, *inverse, *prefix, *norm,
    )
    common = (key_v, value_v, sel, sel_t, featk, key_part, value_part, back)
    grad_key, grad_value, grad_wkey = call(
        lambda *refs: final_body(steps, 0, *refs),
        [((per * FEAT, length), BF16), ((length, per * HEAD_DIM), BF16), wide_narrow],
        *parts[0], *common, wkey_part, place=place,
    )
    grad_key, grad_value = call(
        lambda *refs: final_body(steps, 1, *refs),
        [(key_t.shape, BF16), wide_narrow],
        *parts[1], *common, grad_key, grad_value, place=place,
    )
    return (normed, grad_query.T, grad_key.T, grad_value, grad_wquery, grad_wkey)


def solution(mesh):
    placed = P("seq", "head")
    return jax.shard_map(
        shards,
        mesh=mesh,
        in_specs=(placed, placed, placed, placed, placed, P("head"), placed),
        out_specs=(placed,) * 6,
        check_vma=False,
    )
```

time: 222 us -> 58.9 us (0.27)
  blocking collectives: 81.6 us -> 0 us
  waiting for transfers between devices: 50.4 us -> 14.2 us
  other arithmetic: 27.6 us -> 0.01 us
  matrix products: 19.6 us -> 0 us
  Pallas kernels: 0 us -> 18.6 us
  local copies, waits for them, and re-layouts: 15.2 us -> 0 us
  between operations: 14.7 us -> 0.76 us
  starting transfers between devices: 11.7 us -> 25.1 us
    all_gather x2 -> x0, blocking collectives: 75.9 us -> none  [prefix(): gathered = jax.tree.map(lambda a: lax.all_gather(a, axis), part)]
    all_gather x2 -> x0, waiting for transfers between devices: 50.3 us -> none  [prefix(): gathered = jax.tree.map(lambda a: lax.all_gather(a, axis), part)]
    pallas_call x0 -> x18, Pallas kernels: none -> 18.6 us  [call(): pl.pallas_call(body, out_shape=[jax.ShapeDtypeStruct(shape, dtype) for sh...]
    dot_general x19 -> x0, matrix products: 18.2 us -> none  [the longest x1 3.11 us: shards(): jnp.einsum('the,hed->thd', feat_query_f, prefix_state, precision=HIGHEST)]
    ppermute x4 -> x16, waiting for transfers between devices: 0.01 us -> 14.2 us  [the longest x12 10.9 us: exchanged(): parts[c].append(lax.ppermute(state, 'seq', pairs))]
    ppermute x4 -> x16, starting transfers between devices: 11.7 us -> 25.1 us  [the longest x12 19.2 us: exchanged(): parts[c].append(lax.ppermute(state, 'seq', pairs))]
    add x19 -> x2, other arithmetic: 8.54 us -> 0.01 us  [shards(): stats + lax.ppermute(stats, 'head', [(i, i ^ step) for i in range(ring)])]
    unnamed x87 -> x0, local copies, waits for them, and re-layouts: 7 us -> none
  transfers between devices with their start and end apart: 6 -> 16, of which waited for: 2 -> 7; matrix products, arithmetic and copies ran while one was open for 20% -> 0% of each run, Pallas kernels for 0% -> 21%
where the time goes in v1:
time: 58.9 us; the launch traced here: 58.7 us
  starting transfers between devices  25.1 us (43%)
  Pallas kernels  18.6 us (32%)
  waiting for transfers between devices  14.2 us (24%)
  between operations  0.76 us (1%)
    ppermute x12, starting transfers between devices, exchanged(): parts[c].append(lax.ppermute(state, 'seq', pairs))  19.2 us
    pallas_call x18, Pallas kernels, call(): pl.pallas_call(body, out_shape=[jax.ShapeDtypeStruct(shape, dtype) for sh...  18.6 us
    ppermute x12, waiting for transfers between devices, exchanged(): parts[c].append(lax.ppermute(state, 'seq', pairs))  10.9 us
    ppermute x2, waiting for transfers between devices, shards(): lax.ppermute(stats, 'head', [(i, i ^ step) for i in range(ring)])  3.29 us
    ppermute x1, starting transfers between devices, early(): rim_in = lax.ppermute(rim, 'seq', [(i, i + 1) for i in range(count - 1)])  3.13 us
    ppermute x2, starting transfers between devices, shards(): lax.ppermute(stats, 'head', [(i, i ^ step) for i in range(ring)])  1.56 us
    ppermute x1, starting transfers between devices, middle(): back = lax.ppermute(back, 'seq', [(i + 1, i) for i in range(count - 1)])  1.28 us
  transfers between devices with their start and end apart: 16, of which 7 were waited for; matrix products, arithmetic and copies ran while one was open for 0% of the time, Pallas kernels for 21%

profile of v1, /device:TPU:0, one launch (start us, length us, event | category | flops | bytes accessed | tf_op | source)
XLA Modules:
  0.0 58.7 jit_solution(13536403734850999739)
XLA Ops:
  0.6 2.7 %shard_map.145 = (bf16[320,128]{1,0:T(8,128)(2,1)S(1)}, bf16[320,128]{1,0:T(8,128)(2,1)S(1)}, bf16[128,512]{1,0:T(8,128)(2,1)S(1)}, bf16[64,256]{1,0:T(8,128)(2,...) custom-call(bf16[64,256]{1,0:T(8,128)(2,1)} %bitcast.7, ...), custom_call_target="tpu_custom_call" | custom-call | tf_op jit(solution)/shard_map/pallas_call | solution.py:459
  3.3 3.0 %collective-permute-start.4 = (bf16[320,128]{1,0:T(8,128)(2,1)S(1)}, bf16[320,128]{1,0:T(8,128)(2,1)S(1)}, u32[]{:S(2)}, u32[]{:S(2)}) collective-permute-start(bf16[320,128]{1,0:T(8,128)(2,1)S(1)} %get-tuple-element.73.mine_ref), channel_id=1, source_target_pairs={{0,4},{4,0},{8,12},{12,8},{16,20},{20,16},{24,28},{28,24},{1,5},{5... | collective-permute-start | bytes 245768 | tf_op jit(solution)/shard_map/ppermute | solution.py:478
  6.3 0.1 collective-permute-start
  6.4 2.7 %collective-permute-done.4.theirs_ref.refs_1_ = bf16[320,128]{1,0:T(8,128)(2,1)S(1)} collective-permute-done((bf16[320,128]{1,0:T(8,128)(2,1)S(1)}, bf16[320,128]{1,0:T(8,128)(2,1)S(1)}, u32[]{:S(2)}, u32[]{:S(2)}) %collective-permute-start.4) | collective-permute-done | bytes 81952 | tf_op jit(solution)/shard_map/ppermute | solution.py:478
  9.1 0.2 shard_map.150.mine_ref
  9.3 2.6 %collective-permute-start.5 = (bf16[320,128]{1,0:T(8,128)(2,1)S(1)}, bf16[320,128]{1,0:T(8,128)(2,1)S(1)}, u32[]{:S(2)}, u32[]{:S(2)}) collective-permute-start(bf16[320,128]{1,0:T(8,128)(2,1)S(1)} %shard_map.150.mine_ref), channel_id=1, source_target_pairs={{0,8},{4,12},{8,0},{12,4},{16,24},{20,28},{24,16},{28,20},{1,9},{5... | collective-permute-start | bytes 245768 | tf_op jit(solution)/shard_map/ppermute | solution.py:478
  11.9 0.0 collective-permute-done.theirs_ref.refs_1_
  11.9 0.2 shard_map.147.mine_ref
  12.2 0.7 %collective-permute-start.1 = (bf16[320,128]{1,0:T(8,128)(2,1)S(1)}, bf16[320,128]{1,0:T(8,128)(2,1)S(1)}, u32[]{:S(2)}, u32[]{:S(2)}) collective-permute-start(bf16[320,128]{1,0:T(8,128)(2,1)S(1)} %shard_map.147.mine_ref), channel_id=1, source_target_pairs={{0,8},{4,12},{8,0},{12,4},{16,24},{20,28},{24,16},{28,20},{1,9},{5... | collective-permute-start | bytes 245768 | tf_op jit(solution)/shard_map/ppermute | solution.py:478
  12.9 3.1 %collective-permute-start.3 = (bf16[128,512]{1,0:T(8,128)(2,1)S(1)}, bf16[128,512]{1,0:T(8,128)(2,1)S(1)}, u32[]{:S(2)}, u32[]{:S(2)}) collective-permute-start(bf16[128,512]{1,0:T(8,128)(2,1)S(1)} %get-tuple-element.69), channel_id=1, source_target_pairs={{0,4},{4,8},{8,12},{12,16},{16,20},{20,24},{24,28},{1,5},{5,9},{9,... | collective-permute-start | bytes 393224 | tf_op jit(solution)/shard_map/ppermute | solution.py:511
  16.0 0.0 collective-permute-done.5.theirs_ref.refs_2_
  16.0 0.2 shard_map.151
  16.3 2.7 %collective-permute-start.6 = (bf16[320,128]{1,0:T(8,128)(2,1)S(1)}, bf16[320,128]{1,0:T(8,128)(2,1)S(1)}, u32[]{:S(2)}, u32[]{:S(2)}) collective-permute-start(bf16[320,128]{1,0:T(8,128)(2,1)S(1)} %shard_map.151), channel_id=1, source_target_pairs={{0,16},{4,20},{8,24},{12,28},{16,0},{20,4},{24,8},{28,12},{1,17},{... | collective-permute-start | bytes 245768 | tf_op jit(solution)/shard_map/ppermute | solution.py:478
  18.9 0.0 collective-permute-done.1.theirs_ref.refs_2_
  18.9 0.2 shard_map.148
  19.2 1.0 %collective-permute-start.2 = (bf16[320,128]{1,0:T(8,128)(2,1)S(1)}, bf16[320,128]{1,0:T(8,128)(2,1)S(1)}, u32[]{:S(2)}, u32[]{:S(2)}) collective-permute-start(bf16[320,128]{1,0:T(8,128)(2,1)S(1)} %shard_map.148), channel_id=1, source_target_pairs={{0,16},{4,20},{8,24},{12,28},{16,0},{20,4},{24,8},{28,12},{1,17},{... | collective-permute-start | bytes 245768 | tf_op jit(solution)/shard_map/ppermute | solution.py:478
  20.1 2.2 %shard_map.146 = (f32[256,512]{1,0:T(8,128)S(1)}, f32[256,128]{1,0:T(8,128)S(1)}, bf16[4,256,160]{2,1,0:T(8,128)(2,1)S(1)}, bf16[640,256]{1,0:T(8,128)(2,1)S(1)}...) custom-call(bf16[64,256]{1,0:T(8,128)(2,1)} %bitcast.6, ...), custom_call_target="tpu_custom_call" | custom-call | tf_op jit(solution)/shard_map/pallas_call | solution.py:459
  22.3 0.0 collective-permute-done.3.rim_ref
  22.3 1.6 %shard_map.149 = (f32[256,512]{1,0:T(8,128)S(1)}, f32[4,256,128]{2,1,0:T(8,128)S(1)}) custom-call(s32[1]{0:T(128)} %bitcast.3.place_ref.refs_0_, bf16[256,512]{1,0:T(8,128)(2,1)S(1)} %get-tuple-element.67.wquery_ref, bf16[256,512]{1,0:T(8,128)(2,1)S(1)} %get-tuple-element.68.wkey_ref, bf16[256,512]{1,0:T(8,128)(2,1)S(1)} %get-tuple-element.58.value_ref.refs_5_, ...), custom_call_target="tpu_custom_call" | custom-call | tf_op jit(solution)/shard_map/pallas_call | solution.py:459
  24.0 0.3 collective-permute-done.6.refs_3_
  24.2 0.8 %shard_map.152 = (f32[256,256]{1,0:T(8,128)S(1)}, f32[256,256]{1,0:T(8,128)S(1)}, f32[256,128]{1,0:T(8,128)S(1)}, f32[320,128]{1,0:T(8,128)S(1)}, f32[16,160]{1,...) custom-call(s32[1]{0:T(128)} %bitcast.3.place_ref.refs_0_, ...), custom_call_target="tpu_custom_call" | custom-call | tf_op jit(solution)/shard_map/pallas_call | solution.py:459
  25.0 1.0 %collective-permute-done.2.refs_3_ = bf16[320,128]{1,0:T(8,128)(2,1)S(1)} collective-permute-done((bf16[320,128]{1,0:T(8,128)(2,1)S(1)}, bf16[320,128]{1,0:T(8,128)(2,1)S(1)}, u32[]{:S(2)}, u32[]{:S(2)}) %collective-permute-start.2) | collective-permute-done | bytes 81952 | tf_op jit(solution)/shard_map/ppermute | solution.py:478
  26.0 0.9 %shard_map.153 = (f32[256,256]{1,0:T(8,128)S(1)}, f32[256,256]{1,0:T(8,128)S(1)}, f32[256,128]{1,0:T(8,128)S(1)}, f32[320,128]{1,0:T(8,128)S(1)}, f32[16,160]{1,0:T(8,128)S(1)}, /*index=5*/f32[8,256]{1,0:T(8,128)S(1)}) custom-call(s32[1]{0:T(128)} %bitcast.3.place_ref.refs_0_, bf16[320,128]{1,0:T(8,128)(2,1)S(1)} %collective-permute-done.theirs_ref.refs_1_, ...), custom_call_target="tpu_custom_call" | custom-call | tf_op jit(solution)/shard_map/pallas_call | solution.py:459
  26.9 0.0 collective-permute-start.7
  26.9 1.2 %collective-permute-done.7 = f32[8,256]{1,0:T(8,128)S(1)} collective-permute-done((f32[8,256]{1,0:T(8,128)S(1)}, f32[8,256]{1,0:T(8,128)S(1)}, u32[]{:S(2)}, u32[]{:S(2)}) %collective-permute-start.7) | collective-permute-done | bytes 8224 | tf_op jit(solution)/shard_map/ppermute | solution.py:543
  28.1 1.5 %collective-permute-start.8 = (f32[8,256]{1,0:T(8,128)S(1)}, f32[8,256]{1,0:T(8,128)S(1)}, u32[]{:S(2)}, u32[]{:S(2)}) collective-permute-start(f32[8,256]{1,0:T(8,128)S(1)} %add.6), channel_id=1, source_target_pairs={{0,2},{1,3},{2,0},{3,1},{4,6},{5,7},{6,4},{7,5},{8,10},{9,11},{10,... | collective-permute-start | bytes 24584 | tf_op jit(solution)/shard_map/ppermute | solution.py:543
  29.6 2.1 %collective-permute-done.8 = f32[8,256]{1,0:T(8,128)S(1)} collective-permute-done((f32[8,256]{1,0:T(8,128)S(1)}, f32[8,256]{1,0:T(8,128)S(1)}, u32[]{:S(2)}, u32[]{:S(2)}) %collective-permute-start.8) | collective-permute-done | bytes 8224 | tf_op jit(solution)/shard_map/ppermute | solution.py:543
  31.8 1.1 %shard_map.154 = (bf16[320,128]{1,0:T(8,128)(2,1)S(1)}, bf16[320,128]{1,0:T(8,128)(2,1)S(1)}, f32[256,512]{1,0:T(8,128)S(1)}, f32[256,128]{1,0:T(8,128)S(1)}, f32[8,256]{1,0:T(8,128)S(1)}) custom-call(f32[8,256]{1,0:T(8,128)S(1)} %add.7.refs_0_, f32[256,256]{1,0:T(8,128)S(1)} %get-tuple-element.77.refs_1_.refs_0_, ...), custom_call_target="tpu_custom_call" | custom-call | tf_op jit(solution)/shard_map/pallas_call | solution.py:459
  32.9 1.6 %collective-permute-start.13 = (bf16[320,128]{1,0:T(8,128)(2,1)S(1)}, bf16[320,128]{1,0:T(8,128)(2,1)S(1)}, u32[]{:S(2)}, u32[]{:S(2)}) collective-permute-start(bf16[320,128]{1,0:T(8,128)(2,1)S(1)} %get-tuple-element.100.mine_ref), channel_id=1, source_target_pairs={{0,4},{4,0},{8,12},{12,8},{16,20},{20,16},{24,28},{28,24},{1,5},{5... | collective-permute-start | bytes 245768 | tf_op jit(solution)/shard_map/ppermute | solution.py:478
  34.5 0.5 collective-permute-start.9
  35.0 2.6 %collective-permute-done.13.theirs_ref.refs_1_ = bf16[320,128]{1,0:T(8,128)(2,1)S(1)} collective-permute-done((bf16[320,128]{1,0:T(8,128)(2,1)S(1)}, bf16[320,128]{1,0:T(8,128)(2,1)S(1)}, u32[]{:S(2)}, u32[]{:S(2)}) %collective-permute-start.13) | collective-permute-done | bytes 81952 | tf_op jit(solution)/shard_map/ppermute | solution.py:478
  37.6 1.4 %collective-permute-start.14 = (bf16[320,128]{1,0:T(8,128)(2,1)S(1)}, bf16[320,128]{1,0:T(8,128)(2,1)S(1)}, u32[]{:S(2)}, u32[]{:S(2)}) collective-permute-start(bf16[320,128]{1,0:T(8,128)(2,1)S(1)} %shard_map.159.mine_ref), channel_id=1, source_target_pairs={{0,8},{4,12},{8,0},{12,4},{16,24},{20,28},{24,16},{28,20},{1,9},{5... | collective-permute-start | bytes 245768 | tf_op jit(solution)/shard_map/ppermute | solution.py:478
  39.1 0.0 collective-permute-done.9.theirs_ref.refs_1_
  39.1 1.3 %collective-permute-start.10 = (bf16[320,128]{1,0:T(8,128)(2,1)S(1)}, bf16[320,128]{1,0:T(8,128)(2,1)S(1)}, u32[]{:S(2)}, u32[]{:S(2)}) collective-permute-start(bf16[320,128]{1,0:T(8,128)(2,1)S(1)} %shard_map.157.mine_ref), channel_id=1, source_target_pairs={{0,8},{4,12},{8,0},{12,4},{16,24},{20,28},{24,16},{28,20},{1,9},{5... | collective-permute-start | bytes 245768 | tf_op jit(solution)/shard_map/ppermute | solution.py:478
  40.4 2.2 %shard_map.155 = (bf16[256,512]{1,0:T(8,128)(2,1)}, f32[256,512]{1,0:T(8,128)S(1)}, f32[256,512]{1,0:T(8,128)S(1)}, bf16[128,512]{1,0:T(8,128)(2,1)S(1)}) custom-call(bf16[256,512]{1,0:T(8,128)(2,1)S(1)} %get-tuple-element.67.wquery_ref, bf16[256,512]{1,0:T(8,128)(2,1)S(1)} %get-tuple-element.68.wkey_ref, ...), custom_call_target="tpu_custom_call" | custom-call | tf_op jit(solution)/shard_map/pallas_call | solution.py:459
  42.6 1.3 %collective-permute-start.12 = (bf16[128,512]{1,0:T(8,128)(2,1)S(1)}, bf16[128,512]{1,0:T(8,128)(2,1)S(1)}, u32[]{:S(2)}, u32[]{:S(2)}) collective-permute-start(bf16[128,512]{1,0:T(8,128)(2,1)S(1)} %get-tuple-element.99), channel_id=1, source_target_pairs={{4,0},{8,4},{12,8},{16,12},{20,16},{24,20},{28,24},{5,1},{9,5},{13... | collective-permute-start | bytes 393224 | tf_op jit(solution)/shard_map/ppermute | solution.py:557
  43.9 0.0 collective-permute-done.14.theirs_ref.refs_2_
  43.9 4.2 %collective-permute-start.15 = (bf16[320,128]{1,0:T(8,128)(2,1)S(1)}, bf16[320,128]{1,0:T(8,128)(2,1)S(1)}, u32[]{:S(2)}, u32[]{:S(2)}) collective-permute-start(bf16[320,128]{1,0:T(8,128)(2,1)S(1)} %shard_map.160), channel_id=1, source_target_pairs={{0,16},{4,20},{8,24},{12,28},{16,0},{20,4},{24,8},{28,12},{1,17},{... | collective-permute-start | bytes 245768 | tf_op jit(solution)/shard_map/ppermute | solution.py:478
  48.1 0.0 collective-permute-done.10.theirs_ref.refs_2_
  48.1 0.1 collective-permute-start.11
  48.2 3.2 %shard_map.156 = (bf16[64,256]{1,0:T(8,128)(2,1)}, f32[64,256]{1,0:T(8,128)S(1)}, f32[256,512]{1,0:T(8,128)S(1)}, bf16[256,512]{1,0:T(8,128)(2,1)}) custom-call(bf16[64,256]{1,0:T(8,128)(2,1)S(1)} %get-tuple-element.62.query_ref, bf16[64,256]{1,0:T(8,128)(2,1)S(1)} %get-tuple-element.57.key_ref.refs_4_, ...), custom_call_target="tpu_custom_call" | custom-call | tf_op jit(solution)/shard_map/pallas_call | solution.py:459
  51.4 0.0 collective-permute-done.12.refs_11_
  51.4 4.3 %collective-permute-done.15.refs_3_ = bf16[320,128]{1,0:T(8,128)(2,1)S(1)} collective-permute-done((bf16[320,128]{1,0:T(8,128)(2,1)S(1)}, bf16[320,128]{1,0:T(8,128)(2,1)S(1)}, u32[]{:S(2)}, u32[]{:S(2)}) %collective-permute-start.15) | collective-permute-done | bytes 81952 | tf_op jit(solution)/shard_map/ppermute | solution.py:478
  55.7 1.5 %shard_map.161 = (bf16[32,256]{1,0:T(8,128)(2,1)S(1)}, bf16[256,256]{1,0:T(8,128)(2,1)S(1)}, bf16[256,512]{1,0:T(8,128)(2,1)}) custom-call(s32[1]{0:T(128)} %bitcast.3.place_ref.refs_0_, bf16[320,128]{1,0:T(8,128)(2,1)S(1)} %collective-permute-done.13.theirs_ref.refs_1_, bf16[320,128]{1,0:T(8,128)(2,1)S(1)} %collective-permute-done.14.theirs_ref.refs_2_, ...), custom_call_target="tpu_custom_call" | custom-call | tf_op jit(solution)/shard_map/pallas_call | solution.py:459
  57.2 0.0 collective-permute-done.11.refs_3_
  57.2 1.5 %shard_map.162 = (bf16[64,256]{1,0:T(8,128)(2,1)}, bf16[256,512]{1,0:T(8,128)(2,1)}) custom-call(s32[1]{0:T(128)} %bitcast.3.place_ref.refs_0_, bf16[320,128]{1,0:T(8,128)(2,1)S(1)} %collective-permute-done.9.theirs_ref.refs_1_, bf16[320,128]{1,0:T(8,128)(2,1)S(1)} %collective-permute-done.10.theirs_ref.refs_2_, ...), custom_call_target="tpu_custom_call" | custom-call | tf_op jit(solution)/shard_map/pallas_call | solution.py:459
  (6 shorter events, 0.2 us)
Async XLA Ops:
  3.3 5.8 %collective-permute-start.4 = (bf16[320,128]{1,0:T(8,128)(2,1)S(1)}, bf16[320,128]{1,0:T(8,128)(2,1)S(1)}, u32[]{:S(2)}, u32[]{:S(2)}) collective-permute-start(bf16[320,128]{1,0:T(8,128)(2,1)S(1)} %get-tuple-element.73.mine_ref), channel_id=1, source_target_pairs={{0,4},{4,0},{8,12},{12,8},{16,20},{20,16},{24,28},{28,24},{1,5},{5... | collective-permute-start | bytes 245768 | tf_op jit(solution)/shard_map/ppermute | solution.py:478
  6.3 5.6 %collective-permute-start = (bf16[320,128]{1,0:T(8,128)(2,1)S(1)}, bf16[320,128]{1,0:T(8,128)(2,1)S(1)}, u32[]{:S(2)}, u32[]{:S(2)}) collective-permute-start(bf16[320,128]{1,0:T(8,128)(2,1)S(1)} %get-tuple-element.63.mine_ref), channel_id=1, source_target_pairs={{0,4},{4,0},{8,12},{12,8},{16,20},{20,16},{24,28},{28,24},{1,5},{5... | collective-permute-start | bytes 245768 | tf_op jit(solution)/shard_map/ppermute | solution.py:478
  9.3 6.7 %collective-permute-start.5 = (bf16[320,128]{1,0:T(8,128)(2,1)S(1)}, bf16[320,128]{1,0:T(8,128)(2,1)S(1)}, u32[]{:S(2)}, u32[]{:S(2)}) collective-permute-start(bf16[320,128]{1,0:T(8,128)(2,1)S(1)} %shard_map.150.mine_ref), channel_id=1, source_target_pairs={{0,8},{4,12},{8,0},{12,4},{16,24},{20,28},{24,16},{28,20},{1,9},{5... | collective-permute-start | bytes 245768 | tf_op jit(solution)/shard_map/ppermute | solution.py:478
  12.2 6.8 %collective-permute-start.1 = (bf16[320,128]{1,0:T(8,128)(2,1)S(1)}, bf16[320,128]{1,0:T(8,128)(2,1)S(1)}, u32[]{:S(2)}, u32[]{:S(2)}) collective-permute-start(bf16[320,128]{1,0:T(8,128)(2,1)S(1)} %shard_map.147.mine_ref), channel_id=1, source_target_pairs={{0,8},{4,12},{8,0},{12,4},{16,24},{20,28},{24,16},{28,20},{1,9},{5... | collective-permute-start | bytes 245768 | tf_op jit(solution)/shard_map/ppermute | solution.py:478
  12.9 9.4 %collective-permute-start.3 = (bf16[128,512]{1,0:T(8,128)(2,1)S(1)}, bf16[128,512]{1,0:T(8,128)(2,1)S(1)}, u32[]{:S(2)}, u32[]{:S(2)}) collective-permute-start(bf16[128,512]{1,0:T(8,128)(2,1)S(1)} %get-tuple-element.69), channel_id=1, source_target_pairs={{0,4},{4,8},{8,12},{12,16},{16,20},{20,24},{24,28},{1,5},{5,9},{9,... | collective-permute-start | bytes 393224 | tf_op jit(solution)/shard_map/ppermute | solution.py:511
  16.3 8.0 %collective-permute-start.6 = (bf16[320,128]{1,0:T(8,128)(2,1)S(1)}, bf16[320,128]{1,0:T(8,128)(2,1)S(1)}, u32[]{:S(2)}, u32[]{:S(2)}) collective-permute-start(bf16[320,128]{1,0:T(8,128)(2,1)S(1)} %shard_map.151), channel_id=1, source_target_pairs={{0,16},{4,20},{8,24},{12,28},{16,0},{20,4},{24,8},{28,12},{1,17},{... | collective-permute-start | bytes 245768 | tf_op jit(solution)/shard_map/ppermute | solution.py:478
  19.2 6.8 %collective-permute-start.2 = (bf16[320,128]{1,0:T(8,128)(2,1)S(1)}, bf16[320,128]{1,0:T(8,128)(2,1)S(1)}, u32[]{:S(2)}, u32[]{:S(2)}) collective-permute-start(bf16[320,128]{1,0:T(8,128)(2,1)S(1)} %shard_map.148), channel_id=1, source_target_pairs={{0,16},{4,20},{8,24},{12,28},{16,0},{20,4},{24,8},{28,12},{1,17},{... | collective-permute-start | bytes 245768 | tf_op jit(solution)/shard_map/ppermute | solution.py:478
  26.9 1.2 %collective-permute-start.7 = (f32[8,256]{1,0:T(8,128)S(1)}, f32[8,256]{1,0:T(8,128)S(1)}, u32[]{:S(2)}, u32[]{:S(2)}) collective-permute-start(f32[8,256]{1,0:T(8,128)S(1)} %get-tuple-element.76), channel_id=1, source_target_pairs={{0,1},{1,0},{2,3},{3,2},{4,5},{5,4},{6,7},{7,6},{8,9},{9,8},{10,11... | collective-permute-start | bytes 24584 | tf_op jit(solution)/shard_map/ppermute | solution.py:543
  28.1 3.7 %collective-permute-start.8 = (f32[8,256]{1,0:T(8,128)S(1)}, f32[8,256]{1,0:T(8,128)S(1)}, u32[]{:S(2)}, u32[]{:S(2)}) collective-permute-start(f32[8,256]{1,0:T(8,128)S(1)} %add.6), channel_id=1, source_target_pairs={{0,2},{1,3},{2,0},{3,1},{4,6},{5,7},{6,4},{7,5},{8,10},{9,11},{10,... | collective-permute-start | bytes 24584 | tf_op jit(solution)/shard_map/ppermute | solution.py:543
  32.9 4.7 %collective-permute-start.13 = (bf16[320,128]{1,0:T(8,128)(2,1)S(1)}, bf16[320,128]{1,0:T(8,128)(2,1)S(1)}, u32[]{:S(2)}, u32[]{:S(2)}) collective-permute-start(bf16[320,128]{1,0:T(8,128)(2,1)S(1)} %get-tuple-element.100.mine_ref), channel_id=1, source_target_pairs={{0,4},{4,0},{8,12},{12,8},{16,20},{20,16},{24,28},{28,24},{1,5},{5... | collective-permute-start | bytes 245768 | tf_op jit(solution)/shard_map/ppermute | solution.py:478
  34.5 4.6 %collective-permute-start.9 = (bf16[320,128]{1,0:T(8,128)(2,1)S(1)}, bf16[320,128]{1,0:T(8,128)(2,1)S(1)}, u32[]{:S(2)}, u32[]{:S(2)}) collective-permute-start(bf16[320,128]{1,0:T(8,128)(2,1)S(1)} %get-tuple-element.95.mine_ref), channel_id=1, source_target_pairs={{0,4},{4,0},{8,12},{12,8},{16,20},{20,16},{24,28},{28,24},{1,5},{5... | collective-permute-start | bytes 245768 | tf_op jit(solution)/shard_map/ppermute | solution.py:478
  37.6 6.2 %collective-permute-start.14 = (bf16[320,128]{1,0:T(8,128)(2,1)S(1)}, bf16[320,128]{1,0:T(8,128)(2,1)S(1)}, u32[]{:S(2)}, u32[]{:S(2)}) collective-permute-start(bf16[320,128]{1,0:T(8,128)(2,1)S(1)} %shard_map.159.mine_ref), channel_id=1, source_target_pairs={{0,8},{4,12},{8,0},{12,4},{16,24},{20,28},{24,16},{28,20},{1,9},{5... | collective-permute-start | bytes 245768 | tf_op jit(solution)/shard_map/ppermute | solution.py:478
  39.1 9.0 %collective-permute-start.10 = (bf16[320,128]{1,0:T(8,128)(2,1)S(1)}, bf16[320,128]{1,0:T(8,128)(2,1)S(1)}, u32[]{:S(2)}, u32[]{:S(2)}) collective-permute-start(bf16[320,128]{1,0:T(8,128)(2,1)S(1)} %shard_map.157.mine_ref), channel_id=1, source_target_pairs={{0,8},{4,12},{8,0},{12,4},{16,24},{20,28},{24,16},{28,20},{1,9},{5... | collective-permute-start | bytes 245768 | tf_op jit(solution)/shard_map/ppermute | solution.py:478
  42.6 8.8 %collective-permute-start.12 = (bf16[128,512]{1,0:T(8,128)(2,1)S(1)}, bf16[128,512]{1,0:T(8,128)(2,1)S(1)}, u32[]{:S(2)}, u32[]{:S(2)}) collective-permute-start(bf16[128,512]{1,0:T(8,128)(2,1)S(1)} %get-tuple-element.99), channel_id=1, source_target_pairs={{4,0},{8,4},{12,8},{16,12},{20,16},{24,20},{28,24},{5,1},{9,5},{13... | collective-permute-start | bytes 393224 | tf_op jit(solution)/shard_map/ppermute | solution.py:557
  43.9 11.8 %collective-permute-start.15 = (bf16[320,128]{1,0:T(8,128)(2,1)S(1)}, bf16[320,128]{1,0:T(8,128)(2,1)S(1)}, u32[]{:S(2)}, u32[]{:S(2)}) collective-permute-start(bf16[320,128]{1,0:T(8,128)(2,1)S(1)} %shard_map.160), channel_id=1, source_target_pairs={{0,16},{4,20},{8,24},{12,28},{16,0},{20,4},{24,8},{28,12},{1,17},{... | collective-permute-start | bytes 245768 | tf_op jit(solution)/shard_map/ppermute | solution.py:478
  48.1 9.0 %collective-permute-start.11 = (bf16[320,128]{1,0:T(8,128)(2,1)S(1)}, bf16[320,128]{1,0:T(8,128)(2,1)S(1)}, u32[]{:S(2)}, u32[]{:S(2)}) collective-permute-start(bf16[320,128]{1,0:T(8,128)(2,1)S(1)} %shard_map.158), channel_id=1, source_target_pairs={{0,16},{4,20},{8,24},{12,28},{16,0},{20,4},{24,8},{28,12},{1,17},{... | collective-permute-start | bytes 245768 | tf_op jit(solution)/shard_map/ppermute | solution.py:478

commit v2 on v1

v2 whole, which is shorter than its diff:
```python
import math

import jax
import jax.numpy as jnp
import numpy as np
from jax import lax
from jax.experimental import pallas as pl
from jax.experimental.pallas import tpu as pltpu
from jax.sharding import PartitionSpec as P

HEADS = 16
HEAD_DIM = 128
FEAT = 16
WINDOW = 64
CHUNKS = 2

QUAD = FEAT * (FEAT + 1) // 2
LINEAR = QUAD
CONST = QUAD + FEAT
ROWS = 160
ROOT_HALF = float(np.float32(math.sqrt(0.5)))
SCORE = 1.0 / math.sqrt(FEAT)

F32 = jnp.float32
BF16 = jnp.bfloat16
VMEM_LIMIT = 24 * 1024 * 1024


def feature_tables():
    first = np.zeros((ROWS, FEAT), np.float32)
    second = np.zeros((ROWS, FEAT), np.float32)
    rows = np.zeros((8, ROWS), np.float32)
    scale = FEAT ** (-0.25)
    place = 0
    for distance in range(FEAT // 2 + 1):
        for i in range(FEAT if distance < FEAT // 2 else FEAT // 2):
            first[place, i] = scale
            second[place, (i + distance) % FEAT] = scale
            rows[2, place] = ROOT_HALF * (1.0 if distance == 0 else 2.0)
            place += 1
    for i in range(FEAT):
        first[LINEAR + i, i] = scale
    rows[1, LINEAR:CONST] = 1.0
    rows[0:2, CONST] = 1.0
    rows[2, LINEAR : CONST + 1] = 1.0
    sel = np.concatenate([first, second], axis=0)
    sel_t = np.concatenate([first.T, second.T], axis=0)
    return jnp.asarray(sel, BF16), jnp.asarray(sel_t, BF16), jnp.asarray(rows)


def mm(a, b):
    return lax.dot_general(a, b, (((1,), (0,)), ((), ())), preferred_element_type=F32)


def mm_nt(a, b):
    return lax.dot_general(a, b, (((1,), (1,)), ((), ())), preferred_element_type=F32)


def mm_tn(a, b):
    return lax.dot_general(a, b, (((0,), (0,)), ((), ())), preferred_element_type=F32)


def halves(x):
    high = x.astype(BF16)
    return high, (x - high.astype(F32)).astype(BF16)


def lane_sum(x):
    return jnp.sum(x, axis=1, keepdims=True)


def span(h, size):
    return slice(h * size, (h + 1) * size)


def iota(shape, axis):
    return lax.broadcasted_iota(jnp.int32, shape, axis)


def stack8(lines):
    count = -(-len(lines) // 8) * 8
    place = iota((count, lines[0].shape[1]), 0)
    out = jnp.zeros(place.shape, F32)
    for i, line in enumerate(lines):
        out = jnp.where(place == i, line, out)
    return out.astype(BF16)


def split(x):
    high = x.astype(BF16).astype(F32)
    return high, (x - high).astype(BF16).astype(F32)


def feature_rows(inputs_t, sel):
    a = mm(sel[:ROWS], inputs_t)
    b = mm(sel[ROWS : ROWS + QUAD], inputs_t)
    tail = (iota((ROWS - CONST, inputs_t.shape[1]), 0) == 0).astype(F32)
    return jnp.concatenate([a[:QUAD] * b * ROOT_HALF, a[LINEAR:CONST], tail], axis=0).astype(BF16)


def weighted_features(inputs_t, sel_t, rows):
    a = mm_tn(inputs_t, sel_t[:FEAT]) + rows[0:1]
    b = mm_tn(inputs_t, sel_t[FEAT:]) + rows[1:2]
    return (a * b * rows[2:3]).astype(BF16)


def pull_back(upstreams, inputs_t, sel, sel_t):
    firsts = [mm(sel[:QUAD], x) for x in inputs_t]
    seconds = [mm(sel[ROWS : ROWS + QUAD], x) for x in inputs_t]
    first_t = sel_t[:FEAT, :CONST]
    second_t = sel_t[FEAT:, :QUAD]
    sides = []
    for upstream, a, b in zip(upstreams, firsts, seconds):
        squares = upstream[:FEAT] * ROOT_HALF
        others = upstream[FEAT:QUAD] * (2.0 * ROOT_HALF)
        on_first = jnp.concatenate([squares * b[:FEAT], others * b[FEAT:], upstream[LINEAR:CONST]], axis=0)
        on_second = jnp.concatenate([squares * a[:FEAT], others * a[FEAT:]], axis=0)
        sides.append(halves(on_first) + halves(on_second))
    return [
        (mm(first_t, p_high) + mm(second_t, q_high)) + (mm(first_t, p_low) + mm(second_t, q_low))
        for p_high, p_low, q_high, q_low in sides
    ]


def norm_tile(norm):
    high, low = split(norm)
    pad = jnp.zeros((1, 256 - ROWS), F32)
    row = iota((8, 128), 0)
    out = jnp.where(row == 1, high[:, :128], 0.0)
    out = jnp.where(row == 2, jnp.concatenate([high[:, 128:], pad], axis=1), out)
    out = jnp.where(row == 3, low[:, :128], out)
    return jnp.where(row == 4, jnp.concatenate([low[:, 128:], pad], axis=1), out)


def tile_norm(tile):
    return jnp.concatenate([tile[1:2] + tile[3:4], (tile[2:3] + tile[4:5])[:, : ROWS - 128]], axis=1)


def outer(pairs):
    left, right = [], []
    for a, b in pairs:
        a_high, a_low = split(a)
        b_high, b_low = split(b)
        left += [a_high, a_low, a_high]
        right += [b_high, b_high, b_low]
    return mm_tn(stack8(left), stack8(right))


def store_state(out_ref, head, state, tile):
    row = iota((8, 128), 0)
    last = jnp.where(row == 0, state[CONST:], tile)
    out_ref[span(head, ROWS), :] = jnp.concatenate([state[:CONST], last], axis=0).astype(BF16)


def causal_mask(length):
    return iota((length, length), 0) >= iota((length, length), 1)


def state_body(key_hbm, value_hbm, wkey_hbm, sel_hbm, sel_t_hbm, rows_hbm, *refs):
    states = refs[:CHUNKS]
    rim_ref, key_ref, value_ref, sel_ref, sel_t_ref, rows_ref, sems = refs[CHUNKS:]
    length, width = value_ref.shape
    heads = width // HEAD_DIM
    cut = length - WINDOW
    pairs = [
        (key_hbm, key_ref),
        (sel_hbm, sel_ref),
        (value_hbm, value_ref),
        (wkey_hbm.at[cut:length, :], rim_ref.at[0:WINDOW, :]),
        (value_hbm.at[cut:length, :], rim_ref.at[WINDOW : 2 * WINDOW, :]),
        (sel_t_hbm, sel_t_ref),
        (rows_hbm, rows_ref),
    ]
    copies = [pltpu.make_async_copy(a, b, sems.at[i]) for i, (a, b) in enumerate(pairs)]
    for copy in copies:
        copy.start()
    for copy in copies[:3]:
        copy.wait()
    sel = sel_ref[...]
    ones = jnp.ones((8, length), BF16)
    place = iota((8, 128), 0)
    feats = [feature_rows(key_ref[span(h, FEAT), :], sel) for h in range(heads)]
    norms = [mm_nt(ones, feat)[0:1] for feat in feats]
    sums = [mm(feat, value_ref[:, span(h, HEAD_DIM)]) for h, feat in enumerate(feats)]
    middles = [(state[CONST : CONST + 1] * (1.0 / length)).astype(BF16).astype(F32) for state in sums]
    moved = [mm_tn(stack8(list(split(norm))), stack8([middle, middle])) for norm, middle in zip(norms, middles)]
    tiles = [jnp.where(place == 5, middle, norm_tile(norm)) for norm, middle in zip(norms, middles)]
    per = heads // CHUNKS
    for h in range(heads):
        store_state(states[h // per], h % per, sums[h] - moved[h], tiles[h])
    for copy in copies[3:]:
        copy.wait()


def add_about_body(mine_ref, theirs_ref, out_ref):
    place = iota((8, 128), 0)
    totals, tiles, moves = [], [], []
    for h in range(mine_ref.shape[0] // ROWS):
        mine = mine_ref[span(h, ROWS), :].astype(F32)
        theirs = theirs_ref[span(h, ROWS), :].astype(F32)
        mine_tile, their_tile = mine[CONST:], theirs[CONST:]
        mine_norm, their_norm = tile_norm(mine_tile), tile_norm(their_tile)
        mine_middle, their_middle = mine_tile[5:6], their_tile[5:6]
        middle = (0.5 * (mine_middle + their_middle)).astype(BF16).astype(F32)
        moves.append(outer([(mine_norm, mine_middle - middle), (their_norm, their_middle - middle)]))
        tiles.append(jnp.where(place == 5, middle, norm_tile(mine_norm + their_norm)))
        totals.append(mine + theirs)
    for h, total in enumerate(totals):
        store_state(out_ref, h, total + moves[h], tiles[h])


def add_body(mine_ref, theirs_ref, out_ref):
    for h in range(mine_ref.shape[0] // ROWS):
        total = mine_ref[span(h, ROWS), :].astype(F32) + theirs_ref[span(h, ROWS), :].astype(F32)
        store_state(out_ref, h, total, norm_tile(tile_norm(total[CONST:])))


def gather_about_body(bits, ahead, place_ref, *refs):
    parts, mine_ref, out_ref = refs[: len(bits)], refs[-2], refs[-1]
    place = iota((8, 128), 0)
    weights = [taken(place_ref, bit, False) for bit in bits] + [taken(place_ref, ahead, True)]
    totals, tiles, moves = [], [], []
    for h in range(mine_ref.shape[0] // ROWS):
        blocks = [ref[span(h, ROWS), :].astype(F32) for ref in parts + (mine_ref,)]
        middles = [block[CONST + 5 : CONST + 6] for block in blocks]
        norms = [tile_norm(block[CONST:]) * weight for block, weight in zip(blocks, weights)]
        norm = sum(norms)
        sizes = [n[:, CONST : CONST + 1] for n in norms]
        middle = sum(size * m for size, m in zip(sizes, middles)) * (1.0 / jnp.maximum(sum(sizes), 1.0))
        middle = middle.astype(BF16).astype(F32)
        moves.append(outer([(n, m - middle) for n, m in zip(norms, middles)]))
        tiles.append(jnp.where(place == 5, middle, norm_tile(norm)))
        totals.append(sum(block * weight for block, weight in zip(blocks, weights)))
    for h, total in enumerate(totals):
        store_state(out_ref, h, total + moves[h], tiles[h])


def gather_body(bits, ahead, place_ref, *refs):
    parts, mine_ref, out_ref = refs[: len(bits)], refs[-2], refs[-1]
    weights = [taken(place_ref, bit, True) for bit in bits] + [taken(place_ref, ahead, False)]
    for h in range(mine_ref.shape[0] // ROWS):
        total = sum(ref[span(h, ROWS), :].astype(F32) * weight for ref, weight in zip(parts + (mine_ref,), weights))
        store_state(out_ref, h, total, norm_tile(tile_norm(total[CONST:])))


def local_body(query_hbm, key_ref, value_ref, sel_ref, sel_t_ref, rows_ref,
               numer_ref, denom_ref, featq_ref, featq_t_ref, query_ref, sems):
    copy = pltpu.make_async_copy(query_hbm, query_ref, sems.at[0])
    copy.start()
    length = value_ref.shape[0]
    heads = value_ref.shape[1] // HEAD_DIM
    sel = sel_ref[...]
    sel_t = sel_t_ref[...]
    rows = rows_ref[...]
    keys = [key_ref[span(h, FEAT), :] for h in range(heads)]
    copy.wait()
    causal = causal_mask(length)
    lane = iota((length, 128), 1)
    queries = [query_ref[span(h, FEAT), :] for h in range(heads)]
    scores = [mm_tn(query, key) * SCORE for query, key in zip(queries, keys)]
    columns = [feature_rows(query, sel) for query in queries]
    features = [weighted_features(query, sel_t, rows) for query in queries]
    kernels = [jnp.where(causal, 1.0 + score + 0.5 * score * score, 0.0) for score in scores]
    numers = [mm(kernel.astype(BF16), value_ref[:, span(h, HEAD_DIM)]) for h, kernel in enumerate(kernels)]
    denoms = jnp.zeros((length, 128), F32)
    for h in range(heads):
        denoms = jnp.where(lane == h, lane_sum(kernels[h]), denoms)
    for h in range(heads):
        featq_t_ref[span(h, ROWS), :] = columns[h]
        featq_ref[h] = features[h]
        numer_ref[:, span(h, HEAD_DIM)] = numers[h]
    denom_ref[...] = denoms


def window_body(place_ref, wquery_hbm, wkey_hbm, cot_hbm, gain_hbm, value_ref, rim_ref,
                out_ref, weights_ref, wquery_ref, wkey_ref, cot_ref, gain_ref, sems):
    pairs = [(wquery_hbm, wquery_ref), (wkey_hbm, wkey_ref), (cot_hbm, cot_ref), (gain_hbm, gain_ref)]
    copies = [pltpu.make_async_copy(a, b, sems.at[i]) for i, (a, b) in enumerate(pairs)]
    for copy in copies:
        copy.start()
    length = wquery_ref.shape[0]
    heads = value_ref.shape[1] // HEAD_DIM
    live = place_ref[0] > 0
    row = iota((WINDOW, 2 * WINDOW), 0)
    col = iota((WINDOW, 2 * WINDOW), 1)
    inside = (col > row) & (col <= row + WINDOW)
    edge = inside & ((col >= WINDOW) | live)
    starts = range(0, length, WINDOW)
    allowed = jnp.concatenate([edge] + [inside] * (len(starts) - 1), axis=0)
    copies[0].wait()
    copies[1].wait()
    for h in range(heads):
        columns = span(h, HEAD_DIM)
        keys = jnp.concatenate([rim_ref[:WINDOW, columns], wkey_ref[:, columns]], axis=0)
        values = jnp.concatenate([rim_ref[WINDOW:, columns], value_ref[:, columns]], axis=0)
        query = wquery_ref[:, columns]
        logits = jnp.concatenate([mm_nt(query[s : s + WINDOW], keys[s : s + 2 * WINDOW]) for s in starts], axis=0)
        masked = jnp.where(allowed, logits * (1.0 / math.sqrt(HEAD_DIM)), -1e30)
        exponent = jnp.where(allowed, jnp.exp(masked - jnp.max(masked, axis=1, keepdims=True)), 0.0)
        weights = exponent * (1.0 / lane_sum(exponent))
        weights_ref[h] = weights
        narrow = weights.astype(BF16)
        out_ref[:, columns] = jnp.concatenate([mm(narrow[s : s + WINDOW], values[s : s + 2 * WINDOW]) for s in starts], axis=0)
    copies[2].wait()
    copies[3].wait()


def taken(place_ref, bit, later):
    if bit is None:
        return 1.0
    side = (place_ref[0] >> bit) & 1
    return (1 - side if later else side).astype(F32)


def merge_body(bits, chunk, place_ref, *refs):
    steps = len(bits)
    parts = refs[:steps]
    feat_ref, numer_ref, denom_ref, window_ref, gain_ref, cot_ref = refs[steps : steps + 6]
    before = refs[steps + 6 : steps + 6 + (2 if chunk else 0)]
    outs = refs[steps + 6 + len(before) :]
    merged_ref, linear_ref, inverse_ref, prefix_ref, norm_ref = outs[:5]
    length = numer_ref.shape[0]
    per = merged_ref.shape[1] // HEAD_DIM
    lane = iota((length, 128), 1)
    inverses = jnp.zeros((length, 128), F32)
    squares = before[0][...] if chunk else jnp.zeros((length, HEAD_DIM), F32)
    crosses = before[1][...] if chunk else jnp.zeros((length, HEAD_DIM), F32)
    states, norms, lefts, rights = [], [], [], []
    for h in range(per):
        state = norm = None
        left, right = [], []
        for bit, part in zip(bits, parts):
            block = part[span(h, ROWS), :].astype(F32)
            middle = block[CONST + 5 : CONST + 6]
            block = block * taken(place_ref, bit, False)
            block_norm = tile_norm(block[CONST:])
            left += list(split(block_norm))
            right += [middle, middle]
            state = block if state is None else state + block
            norm = block_norm if norm is None else norm + block_norm
        states.append(state)
        norms.append(norm)
        lefts.append(stack8(left))
        rights.append(stack8(right))
    moved = [mm_tn(left, right) for left, right in zip(lefts, rights)]
    states = [state + move for state, move in zip(states, moved)]
    parted = [halves(state) for state in states]
    wholes = [chunk * per + h for h in range(per)]
    feats = [feat_ref[whole] for whole in wholes]
    extras = [mm_nt(feat, stack8(list(split(norm)))) for feat, norm in zip(feats, norms)]
    reads = [mm(feat, high) + mm(feat, low) for feat, (high, low) in zip(feats, parted)]
    linears, mergeds = [], []
    for h, whole in enumerate(wholes):
        columns = span(whole, HEAD_DIM)
        inverse = 1.0 / (denom_ref[:, whole : whole + 1] + (extras[h][:, 0:1] + extras[h][:, 1:2]))
        inverses = jnp.where(lane == h, inverse, inverses)
        linear = (numer_ref[:, columns] + reads[h]) * inverse
        merged = linear + window_ref[:, columns]
        squares = squares + merged * merged
        scaled_cot = cot_ref[:, columns].astype(F32) * gain_ref[0:1, columns]
        crosses = crosses + scaled_cot * merged
        linears.append(linear)
        mergeds.append(merged)
    for h in range(per):
        linear_ref[:, span(h, HEAD_DIM)] = linears[h]
        merged_ref[:, span(h, HEAD_DIM)] = mergeds[h]
        prefix_ref[span(h, ROWS), :] = states[h]
        norm_ref[span(h, 8), :] = jnp.broadcast_to(norms[h], (8, ROWS))
    inverse_ref[...] = inverses
    if chunk + 1 < CHUNKS:
        outs[5][...] = squares
        outs[6][...] = crosses
    else:
        stats = jnp.where(lane == 0, lane_sum(squares), jnp.where(lane == 1, lane_sum(crosses), 0.0))
        outs[5][...] = jnp.transpose(stats)[:8]


def grad_body(width, sources, *refs):
    stats_refs, refs = refs[:sources], refs[sources:]
    merged_refs, linear_refs, inverse_refs = refs[:CHUNKS], refs[CHUNKS : 2 * CHUNKS], refs[2 * CHUNKS : 3 * CHUNKS]
    gain_ref, cot_ref, feat_t_ref = refs[3 * CHUNKS : 3 * CHUNKS + 3]
    terms = refs[3 * CHUNKS + 3 : 4 * CHUNKS + 3]
    grad_ref, cols_ref, ratios_ref = refs[4 * CHUNKS + 3 :]
    length = grad_ref.shape[0]
    heads = grad_ref.shape[1] // HEAD_DIM
    per = heads // CHUNKS
    stats = stats_refs[0][...]
    for ref in stats_refs[1:]:
        stats = stats + ref[...]
    sums = jnp.transpose(jnp.concatenate([stats, jnp.zeros((120, length), F32)], axis=0))
    mean = sums[:, 0:1] / width + 1e-6
    inv_rms = 1.0 / jnp.sqrt(mean)
    pull = sums[:, 1:2] / (width * mean)
    lane = iota((length, 128), 1)
    cols = jnp.where(lane == heads, inv_rms, 0.0)
    grads, narrows = [], []
    for h in range(heads):
        chunk, local = h // per, span(h % per, HEAD_DIM)
        inverse = inverse_refs[chunk][:, h % per : h % per + 1]
        scaled_cot = cot_ref[:, span(h, HEAD_DIM)].astype(F32) * gain_ref[0:1, span(h, HEAD_DIM)]
        grad = (scaled_cot - merged_refs[chunk][:, local] * pull) * inv_rms
        grads.append(grad)
        narrows.append((grad * inverse).astype(BF16))
        cols = jnp.where(lane == h, lane_sum(grad * linear_refs[chunk][:, local]) * inverse, cols)
    feats = [feat_t_ref[span(h, ROWS), :] for h in range(heads)]
    sums = [mm(feat, narrow) for feat, narrow in zip(feats, narrows)]
    ratios = jnp.transpose(cols)[:8]
    norms = [mm_nt(stack8(list(split(ratios[h : h + 1]))), feats[h]) for h in range(heads)]
    for h in range(heads):
        store_state(terms[h // per], h % per, sums[h], norm_tile(norms[h][0:1] + norms[h][1:2]))
        grad_ref[:, span(h, HEAD_DIM)] = grads[h]
    cols_ref[...] = cols
    ratios_ref[...] = ratios


def window_back_body(wquery_ref, wkey_ref, value_ref, rim_ref, weights_ref, grad_ref, gwq_ref, gwk_ref, gv_ref, back_ref):
    length = wquery_ref.shape[0]
    heads = value_ref.shape[1] // HEAD_DIM
    root = 1.0 / math.sqrt(HEAD_DIM)
    starts = range(0, length, WINDOW)
    pad = jnp.zeros((WINDOW, HEAD_DIM), F32)
    for h in range(heads):
        columns = span(h, HEAD_DIM)
        keys = jnp.concatenate([rim_ref[:WINDOW, columns], wkey_ref[:, columns]], axis=0)
        values = jnp.concatenate([rim_ref[WINDOW:, columns], value_ref[:, columns]], axis=0)
        grad = grad_ref[:, columns].astype(BF16)
        query = wquery_ref[:, columns]
        weights = weights_ref[h]
        narrow = weights.astype(BF16)
        dprob = jnp.concatenate([mm_nt(grad[s : s + WINDOW], values[s : s + 2 * WINDOW]) for s in starts], axis=0)
        dlogits = (weights * (dprob - lane_sum(weights * dprob))).astype(BF16)
        grads = [mm(dlogits[s : s + WINDOW], keys[s : s + 2 * WINDOW]) for s in starts]
        gwq_ref[:, columns] = (jnp.concatenate(grads, axis=0) * root).astype(BF16)
        key_parts = [mm_tn(dlogits[s : s + WINDOW], query[s : s + WINDOW]) for s in starts]
        value_parts = [mm_tn(narrow[s : s + WINDOW], grad[s : s + WINDOW]) for s in starts]
        back_ref[:WINDOW, columns] = (key_parts[0][:WINDOW] * root).astype(BF16)
        back_ref[WINDOW:, columns] = value_parts[0][:WINDOW].astype(BF16)
        key_sum = [a[WINDOW:] + b[:WINDOW] for a, b in zip(key_parts, key_parts[1:] + [pad])]
        value_sum = [a[WINDOW:] + b[:WINDOW] for a, b in zip(value_parts, value_parts[1:] + [pad])]
        gwk_ref[:, columns] = jnp.concatenate(key_sum, axis=0) * root
        gv_ref[:, columns] = jnp.concatenate(value_sum, axis=0)


def local_back_body(query_ref, key_ref, value_ref, sel_ref, sel_t_ref, rows_ref, grad_ref, cols_ref, ratios_ref, gv_in_ref, gain_ref, *refs):
    merged_refs, inverse_refs = refs[:CHUNKS], refs[CHUNKS : 2 * CHUNKS]
    prefix_refs, norm_refs = refs[2 * CHUNKS : 3 * CHUNKS], refs[3 * CHUNKS : 4 * CHUNKS]
    gq_ref, gk_ref, gv_ref, normed_ref, feat_ref = refs[4 * CHUNKS :]
    length = value_ref.shape[0]
    heads = value_ref.shape[1] // HEAD_DIM
    per = heads // CHUNKS
    sel = sel_ref[...]
    sel_t = sel_t_ref[...]
    causal = causal_mask(length)
    inv_rms = cols_ref[:, heads : heads + 1]
    queries = [query_ref[span(h, FEAT), :] for h in range(heads)]
    keys = [key_ref[span(h, FEAT), :] for h in range(heads)]
    scaled = [grad_ref[:, span(h, HEAD_DIM)] * inverse_refs[h // per][:, h % per : h % per + 1] for h in range(heads)]
    parted = [halves(x) for x in scaled]
    scores = [mm_tn(query, key) * SCORE for query, key in zip(queries, keys)]
    probs = [mm_nt(narrow, value_ref[:, span(h, HEAD_DIM)]) for h, (narrow, _) in enumerate(parted)]
    kernels = [jnp.where(causal, 1.0 + score + 0.5 * score * score, 0.0).astype(BF16) for score in scores]
    values = [mm_tn(kernel, narrow) for kernel, (narrow, _) in zip(kernels, parted)]
    dscores = [
        jnp.where(causal, (probs[h] - cols_ref[:, h : h + 1]) * (1.0 + scores[h]), 0.0).astype(BF16) for h in range(heads)
    ]
    by_query = [mm_nt(key, dscore) * SCORE for key, dscore in zip(keys, dscores)]
    by_key = [mm(query, dscore) * SCORE for query, dscore in zip(queries, dscores)]
    states = [halves(prefix_refs[h // per][span(h % per, ROWS), :]) for h in range(heads)]
    upstreams = [
        mm_nt(high, narrow) + (mm_nt(low, narrow) + mm_nt(high, rest))
        for (high, low), (narrow, rest) in zip(states, parted)
    ]
    drops = [
        outer([(norm_refs[h // per][h % per * 8 : h % per * 8 + 1, :], ratios_ref[h : h + 1, :])]) for h in range(heads)
    ]
    through = pull_back([up - drop for up, drop in zip(upstreams, drops)], queries, sel, sel_t)
    rows = rows_ref[...]
    features = [weighted_features(key, sel_t, rows) for key in keys]
    for h in range(heads):
        columns = span(h, HEAD_DIM)
        merged = merged_refs[h // per][:, span(h % per, HEAD_DIM)]
        normed_ref[:, columns] = (merged * inv_rms * gain_ref[0:1, columns]).astype(BF16)
        feat_ref[h] = features[h]
        gk_ref[span(h, FEAT), :] = by_key[h]
        gv_ref[:, columns] = gv_in_ref[:, columns] + values[h]
        gq_ref[span(h, FEAT), :] = (by_query[h] + through[h]).astype(BF16)


def final_body(bits, chunk, place_ref, *refs):
    steps = len(bits)
    parts = refs[:steps]
    key_ref, value_ref, sel_ref, sel_t_ref, feat_ref, gk_in_ref, gv_in_ref, back_ref = refs[steps : steps + 8]
    rest = refs[steps + 8 :]
    length = value_ref.shape[0]
    per = parts[0].shape[0] // ROWS
    cut = length - WINDOW
    sel = sel_ref[...]
    sel_t = sel_t_ref[...]
    ones = jnp.where(iota((8, length), 0) < 2, 1.0, 0.0).astype(BF16)
    if chunk + 1 < CHUNKS:
        gwk_in_ref, gk_ref, gv_ref, gwk_ref = rest
        gwk_ref[:cut, :] = gwk_in_ref[:cut, :].astype(BF16)
        gwk_ref[cut:, :] = (gwk_in_ref[cut:, :] + back_ref[:WINDOW, :].astype(F32)).astype(BF16)
        base = 0
    else:
        gk_before, gv_before, gk_ref, gv_ref = rest
        base = chunk * per
        gk_ref[: base * FEAT, :] = gk_before[...]
        gv_ref[:, : base * HEAD_DIM] = gv_before[...]
    wholes = [chunk * per + h for h in range(per)]
    states = []
    for h in range(per):
        state = None
        for bit, part in zip(bits, parts):
            block = part[span(h, ROWS), :].astype(F32) * taken(place_ref, bit, True)
            state = block if state is None else state + block
        states.append(state)
    parted = [halves(state) for state in states]
    values = [value_ref[:, span(whole, HEAD_DIM)] for whole in wholes]
    upstreams = [mm_nt(high, value) + mm_nt(low, value) for (high, low), value in zip(parted, values)]
    norms = [mm_tn(stack8(list(split(tile_norm(state[CONST:])))), ones) for state in states]
    reads = [mm(feat_ref[whole], high) + mm(feat_ref[whole], low) for whole, (high, low) in zip(wholes, parted)]
    keys = [key_ref[span(whole, FEAT), :] for whole in wholes]
    through = pull_back([up - norm for up, norm in zip(upstreams, norms)], keys, sel, sel_t)
    for h, whole in enumerate(wholes):
        columns = span(whole, HEAD_DIM)
        grad_value = gv_in_ref[:, columns] + reads[h]
        out_columns = span(base + h, HEAD_DIM)
        gv_ref[:cut, out_columns] = grad_value[:cut].astype(BF16)
        gv_ref[cut:, out_columns] = (grad_value[cut:] + back_ref[WINDOW:, columns].astype(F32)).astype(BF16)
        gk_ref[span(base + h, FEAT), :] = (gk_in_ref[span(whole, FEAT), :] + through[h]).astype(BF16)


def call(body, outs, *args, place=None, hbm=0, copies=0, results=(), ties=()):
    vmem = pl.BlockSpec(memory_space=pltpu.VMEM)
    specs = [pl.BlockSpec(memory_space=pltpu.HBM)] * hbm + [vmem] * (len(args) - hbm)
    args = tuple(
        pltpu.with_memory_space_constraint(a, pltpu.HBM if i < hbm else pltpu.VMEM) for i, a in enumerate(args)
    )
    if place is not None:
        specs = [pl.BlockSpec(memory_space=pltpu.SMEM)] + specs
        args = (place,) + args
    given = len(args)
    if ties:
        specs = specs + [pl.BlockSpec(memory_space=pl.ANY)] * len(ties)
        args = args + tuple(ties)
    return pl.pallas_call(
        body if not ties else lambda *refs: body(*refs[:given], *refs[given + len(ties) :]),
        out_shape=[
            jax.ShapeDtypeStruct(shape, dtype) if i in results else pltpu.VMEM(shape, dtype)
            for i, (shape, dtype) in enumerate(outs)
        ],
        in_specs=specs,
        out_specs=[vmem] * len(outs),
        scratch_shapes=[pltpu.SemaphoreType.DMA((copies,))] if copies else [],
        compiler_params=pltpu.CompilerParams(vmem_limit_bytes=VMEM_LIMIT),
    )(*args)


def exchanged(states, add, gather, place, after_first):
    count = lax.axis_size("seq")
    bits = list(range(count.bit_length() - 1))
    orders = [bits if c % 2 == 0 else bits[::-1] for c in range(len(states))]
    held = list(states)
    parts = [[] for _ in states]
    extra, ties = None, []
    for step in range(len(bits)):
        for c, order in enumerate(orders):
            pairs = [(i, i ^ (1 << order[step])) for i in range(count)]
            parts[c].append(lax.ppermute(held[c], "seq", pairs))
        if extra is None:
            extra, ties = after_first()
        if step + 1 == len(bits):
            break
        for c, order in enumerate(orders):
            tie = ties.pop(0) if c == 0 and ties else ()
            shape = [(held[c].shape, BF16)]
            if c % 2:
                counts = order[:1] + [None] * step
                (held[c],) = call(
                    lambda *refs: gather(counts, order[step + 1], *refs), shape, *parts[c], states[c], place=place, ties=tie
                )
            else:
                (held[c],) = call(add, shape, held[c], parts[c][-1], ties=tie)
    takes = [order[:1] + [None] * (len(bits) - 1) if c % 2 else order for c, order in enumerate(orders)]
    return parts, takes, extra


def shards(query, key, value, window_query, window_key, gain, cotangent):
    length, width = value.shape
    heads = width // HEAD_DIM
    per = heads // CHUNKS
    count = lax.axis_size("seq")
    full_width = HEADS * HEAD_DIM
    place = lax.axis_index("seq").astype(jnp.int32).reshape(1)
    gain_row = gain.reshape(1, width)
    query_t, key_t = query.T, key.T
    state_shape = ((per * ROWS, HEAD_DIM), BF16)
    wide = ((length, width), F32)
    wide_narrow = ((length, width), BF16)
    tables = feature_tables()

    *states, rim, key_v, value_v, sel, sel_t, rows = call(
        state_body,
        [state_shape] * CHUNKS
        + [((2 * WINDOW, width), BF16), (key_t.shape, BF16), wide_narrow]
        + [(t.shape, t.dtype) for t in tables],
        key_t, value, window_key, *tables, hbm=6, copies=7,
    )

    def early():
        rim_in = lax.ppermute(rim, "seq", [(i, (i + 1) % count) for i in range(count)])
        local = call(
            local_body,
            [wide, ((length, 128), F32), ((heads, length, ROWS), BF16), ((heads * ROWS, length), BF16), (query_t.shape, BF16)],
            query_t, key_v, value_v, sel, sel_t, rows, hbm=1, copies=1,
        )
        return (rim_in, local), [(local[1],), (rim_in,)]

    parts, takes, (rim_in, local) = exchanged(states, add_about_body, gather_about_body, place, early)
    numer, denom, featq, featq_t, query_v = local
    window_out, weights, wquery, wkey, cot, gain_v = call(
        window_body,
        [wide, ((heads, length, 2 * WINDOW), F32), wide_narrow, wide_narrow, wide_narrow, (gain_row.shape, F32)],
        window_query, window_key, cotangent, gain_row, value_v, rim_in, place=place, hbm=4, copies=4,
    )
    half = ((length, per * HEAD_DIM), F32)
    square = ((length, 128), F32)
    merged, linear, inverse, prefix, norm, before = [], [], [], [], [], []
    for c in range(CHUNKS):
        tail = [((8, length), F32)] if c + 1 == CHUNKS else [square, square]
        out = call(
            lambda *refs, c=c: merge_body(takes[c], c, *refs),
            [half, half, square, ((per * ROWS, HEAD_DIM), F32), ((per * 8, ROWS), F32)] + tail,
            *parts[c], featq, numer, denom, window_out, gain_v, cot, *before, place=place,
        )
        for held, item in zip((merged, linear, inverse, prefix, norm), out):
            held.append(item)
        before = out[5:]
    (stats,) = before
    ring = lax.axis_size("head")
    stats = [stats] + [lax.ppermute(stats, "head", [(i, i ^ s) for i in range(ring)]) for s in range(1, ring)]
    *terms, grad, cols, ratios = call(
        lambda *refs: grad_body(float(full_width), ring, *refs),
        [state_shape] * CHUNKS + [wide, square, ((8, length), F32)],
        *stats, *merged, *linear, *inverse, gain_v, cot, featq_t,
    )

    def middle():
        grad_wquery, wkey_part, value_part, back = call(
            window_back_body,
            [wide_narrow, wide, wide, ((2 * WINDOW, width), BF16)],
            wquery, wkey, value_v, rim_in, weights, grad, results=(0,),
        )
        back = lax.ppermute(back, "seq", [((i + 1) % count, i) for i in range(count)])
        return (grad_wquery, wkey_part, value_part, back), [(wkey_part,)]

    parts, takes, (grad_wquery, wkey_part, value_part, back) = exchanged(terms, add_body, gather_body, place, middle)
    grad_query, key_part, value_part, normed, featk = call(
        local_back_body,
        [(query_t.shape, BF16), (key_t.shape, F32), wide, wide_narrow, ((heads, length, ROWS), BF16)],
        query_v, key_v, value_v, sel, sel_t, rows, grad, cols, ratios, value_part, gain_v, *merged, *inverse, *prefix, *norm, results=(0, 3),
    )
    common = (key_v, value_v, sel, sel_t, featk, key_part, value_part, back)
    grad_key, grad_value, grad_wkey = call(
        lambda *refs: final_body(takes[0], 0, *refs),
        [((per * FEAT, length), BF16), ((length, per * HEAD_DIM), BF16), wide_narrow],
        *parts[0], *common, wkey_part, place=place, results=(2,),
    )
    grad_key, grad_value = call(
        lambda *refs: final_body(takes[1], 1, *refs),
        [(key_t.shape, BF16), wide_narrow],
        *parts[1], *common, grad_key, grad_value, place=place, results=(0, 1),
    )
    return (normed, grad_query.T, grad_key.T, grad_value, grad_wquery, grad_wkey)


def solution(mesh):
    placed = P("seq", "head")
    return jax.shard_map(
        shards,
        mesh=mesh,
        in_specs=(placed, placed, placed, placed, placed, P("head"), placed),
        out_specs=(placed,) * 6,
        check_vma=False,
    )
```

time: 58.9 us -> 50.6 us (0.86)
  starting transfers between devices: 25.1 us -> 21 us
  waiting for transfers between devices: 14.2 us -> 11.4 us
  Pallas kernels: 18.6 us -> 17.2 us
    ppermute x16 -> x17, starting transfers between devices: 25.1 us -> 21 us  [the longest x12 16.8 us: exchanged(): parts[c].append(lax.ppermute(held[c], 'seq', pairs))]
    ppermute x16 -> x17, waiting for transfers between devices: 14.2 us -> 11.4 us  [the longest x12 5.85 us: exchanged(): parts[c].append(lax.ppermute(held[c], 'seq', pairs))]
    pallas_call x18, Pallas kernels: 18.6 us -> 17.2 us  [call(): pl.pallas_call(body if not ties else lambda *refs: body(*refs[:given], *r...]
  transfers between devices with their start and end apart: 16 -> 17, of which waited for: 7 -> 6; matrix products, arithmetic and copies ran while one was open for 0% -> 0% of each run, Pallas kernels for 21% -> 24%
where the time goes in v2:
time: 50.6 us; the launch traced here: 50.4 us
  starting transfers between devices  21 us (42%)
  Pallas kernels  17.2 us (34%)
  waiting for transfers between devices  11.4 us (23%)
  between operations  0.75 us (1%)
    pallas_call x18, Pallas kernels, call(): pl.pallas_call(body if not ties else lambda *refs: body(*refs[:given], *r...  17.2 us
    ppermute x12, starting transfers between devices, exchanged(): parts[c].append(lax.ppermute(held[c], 'seq', pairs))  16.8 us
    ppermute x12, waiting for transfers between devices, exchanged(): parts[c].append(lax.ppermute(held[c], 'seq', pairs))  5.85 us
    ppermute x1, waiting for transfers between devices, early(): lax.ppermute(rim, 'seq', [(i, (i + 1) % count) for i in range(count)])  3.69 us
    ppermute x3, starting transfers between devices, shards(): lax.ppermute(stats, 'head', [(i, i ^ s) for i in range(ring)])  1.89 us
    ppermute x3, waiting for transfers between devices, shards(): lax.ppermute(stats, 'head', [(i, i ^ s) for i in range(ring)])  1.87 us
    ppermute x1, starting transfers between devices, middle(): lax.ppermute(back, 'seq', [((i + 1) % count, i) for i in range(count)])  1.86 us
  transfers between devices with their start and end apart: 17, of which 6 were waited for; matrix products, arithmetic and copies ran while one was open for 0% of the time, Pallas kernels for 24%

profile of v2, /device:TPU:0, one launch (start us, length us, event | category | flops | bytes accessed | tf_op | source)
XLA Modules:
  0.0 50.4 jit_solution(8731451822530152869)
XLA Ops:
  0.6 1.8 %shard_map.145 = (bf16[320,128]{1,0:T(8,128)(2,1)S(1)}, bf16[320,128]{1,0:T(8,128)(2,1)S(1)}, bf16[128,512]{1,0:T(8,128)(2,1)S(1)}, bf16[64,256]{1,0:T(8,128)(2,...) custom-call(bf16[64,256]{1,0:T(8,128)(2,1)} %bitcast.7, ...), custom_call_target="tpu_custom_call" | custom-call | tf_op jit(solution)/shard_map/pallas_call | solution.py:547
  2.4 3.0 %collective-permute-start.4 = (bf16[320,128]{1,0:T(8,128)(2,1)S(1)}, bf16[320,128]{1,0:T(8,128)(2,1)S(1)}, u32[]{:S(2)}, u32[]{:S(2)}) collective-permute-start(bf16[320,128]{1,0:T(8,128)(2,1)S(1)} %get-tuple-element.71.refs_0_), channel_id=1, source_target_pairs={{0,4},{4,0},{8,12},{12,8},{16,20},{20,16},{24,28},{28,24},{1,5},{5... | collective-permute-start | bytes 245768 | tf_op jit(solution)/shard_map/ppermute | solution.py:570
  5.4 2.6 %collective-permute-start = (bf16[320,128]{1,0:T(8,128)(2,1)S(1)}, bf16[320,128]{1,0:T(8,128)(2,1)S(1)}, u32[]{:S(2)}, u32[]{:S(2)}) collective-permute-start(bf16[320,128]{1,0:T(8,128)(2,1)S(1)} %get-tuple-element.63.refs_2_.refs_3_), channel_id=1, source_target_pairs={{0,16},{4,20},{8,24},{12,28},{16,0},{20,4},{24,8},{28,12},{1,17},{... | collective-permute-start | bytes 245768 | tf_op jit(solution)/shard_map/ppermute | solution.py:570
  8.0 0.5 %collective-permute-start.3 = (bf16[128,512]{1,0:T(8,128)(2,1)S(1)}, bf16[128,512]{1,0:T(8,128)(2,1)S(1)}, u32[]{:S(2)}, u32[]{:S(2)}) collective-permute-start(bf16[128,512]{1,0:T(8,128)(2,1)S(1)} %get-tuple-element.67), channel_id=1, source_target_pairs={{0,4},{4,8},{8,12},{12,16},{16,20},{20,24},{24,28},{28,0},{1,5},{5... | collective-permute-start | bytes 393224 | tf_op jit(solution)/shard_map/ppermute | solution.py:612
  8.5 1.7 %shard_map.146 = (f32[256,512]{1,0:T(8,128)S(1)}, f32[256,128]{1,0:T(8,128)S(1)}, bf16[4,256,160]{2,1,0:T(8,128)(2,1)S(1)}, bf16[640,256]{1,0:T(8,128)(2,1)S(1)}, bf16[64,256]{1,0:T(8,128)(2,1)S(1)}) custom-call(bf16[64,256]{1,0:T(8,128)(2,1)} %bitcast.6, bf16[64,256]{1,0:T(8,128)(2,1)S(1)} %get-tuple-element.57.key_ref.refs_4_, ...), custom_call_target="tpu_custom_call" | custom-call | tf_op jit(solution)/shard_map/pallas_call | solution.py:547
  10.2 0.0 collective-permute-done.4.refs_1_
  10.3 0.2 shard_map.150.refs_0_
  10.5 1.6 %collective-permute-start.5 = (bf16[320,128]{1,0:T(8,128)(2,1)S(1)}, bf16[320,128]{1,0:T(8,128)(2,1)S(1)}, u32[]{:S(2)}, u32[]{:S(2)}) collective-permute-start(bf16[320,128]{1,0:T(8,128)(2,1)S(1)} %shard_map.150.refs_0_), channel_id=1, source_target_pairs={{0,8},{4,12},{8,0},{12,4},{16,24},{20,28},{24,16},{28,20},{1,9},{5... | collective-permute-start | bytes 245768 | tf_op jit(solution)/shard_map/ppermute | solution.py:570
  12.1 0.0 collective-permute-done.refs_1_
  12.1 0.2 shard_map.147
  12.4 0.6 %collective-permute-start.1 = (bf16[320,128]{1,0:T(8,128)(2,1)S(1)}, bf16[320,128]{1,0:T(8,128)(2,1)S(1)}, u32[]{:S(2)}, u32[]{:S(2)}) collective-permute-start(bf16[320,128]{1,0:T(8,128)(2,1)S(1)} %shard_map.147), channel_id=1, source_target_pairs={{0,8},{4,12},{8,0},{12,4},{16,24},{20,28},{24,16},{28,20},{1,9},{5... | collective-permute-start | bytes 245768 | tf_op jit(solution)/shard_map/ppermute | solution.py:570
  13.0 3.7 %collective-permute-done.3.rim_ref.refs_2_ = bf16[128,512]{1,0:T(8,128)(2,1)S(1)} collective-permute-done((bf16[128,512]{1,0:T(8,128)(2,1)S(1)}, bf16[128,512]{1,0:T(8,128)(2,1)S(1)}, u32[]{:S(2)}, u32[]{:S(2)}) %collective-permute-start.3) | collective-permute-done | bytes 131104 | tf_op jit(solution)/shard_map/ppermute | solution.py:612
  16.6 0.0 collective-permute-done.5.refs_1_.refs_2_
  16.6 0.2 shard_map.151
  16.9 0.7 %collective-permute-start.6 = (bf16[320,128]{1,0:T(8,128)(2,1)S(1)}, bf16[320,128]{1,0:T(8,128)(2,1)S(1)}, u32[]{:S(2)}, u32[]{:S(2)}) collective-permute-start(bf16[320,128]{1,0:T(8,128)(2,1)S(1)} %shard_map.151), channel_id=1, source_target_pairs={{0,16},{4,20},{8,24},{12,28},{16,0},{20,4},{24,8},{28,12},{1,17},{... | collective-permute-start | bytes 245768 | tf_op jit(solution)/shard_map/ppermute | solution.py:570
  17.6 0.0 collective-permute-done.1.refs_2_
  17.6 0.2 shard_map.148
  17.9 2.2 %collective-permute-start.2 = (bf16[320,128]{1,0:T(8,128)(2,1)S(1)}, bf16[320,128]{1,0:T(8,128)(2,1)S(1)}, u32[]{:S(2)}, u32[]{:S(2)}) collective-permute-start(bf16[320,128]{1,0:T(8,128)(2,1)S(1)} %shard_map.148), channel_id=1, source_target_pairs={{0,4},{4,0},{8,12},{12,8},{16,20},{20,16},{24,28},{28,24},{1,5},{5... | collective-permute-start | bytes 245768 | tf_op jit(solution)/shard_map/ppermute | solution.py:570
  20.0 2.7 %shard_map.149 = (f32[256,512]{1,0:T(8,128)S(1)}, f32[4,256,128]{2,1,0:T(8,128)S(1)}, bf16[256,512]{1,0:T(8,128)(2,1)S(1)}, bf16[256,512]{1,0:T(8,128)(2,1)S(1)}...) custom-call(s32[1]{0:T(128)} %bitcast.2.refs_0_.place_ref, bf16[256,512]{1,0:T(8,128)(2,1)} %wquery_hbm.1, ...), custom_call_target="tpu_custom_call" | custom-call | tf_op jit(solution)/shard_map/pallas_call | solution.py:547
  22.7 0.0 collective-permute-done.6.refs_3_
  22.8 0.5 %shard_map.152 = (f32[256,256]{1,0:T(8,128)S(1)}, f32[256,256]{1,0:T(8,128)S(1)}, f32[256,128]{1,0:T(8,128)S(1)}, f32[320,128]{1,0:T(8,128)S(1)}, f32[16,160]{1,...) custom-call(s32[1]{0:T(128)} %bitcast.2.refs_0_.place_ref, ...), custom_call_target="tpu_custom_call" | custom-call | tf_op jit(solution)/shard_map/pallas_call | solution.py:547
  23.3 0.0 collective-permute-done.2.refs_3_
  23.3 0.7 %shard_map.153 = (f32[256,256]{1,0:T(8,128)S(1)}, f32[256,256]{1,0:T(8,128)S(1)}, f32[256,128]{1,0:T(8,128)S(1)}, f32[320,128]{1,0:T(8,128)S(1)}, f32[16,160]{1,0:T(8,128)S(1)}, /*index=5*/f32[8,256]{1,0:T(8,128)S(1)}) custom-call(s32[1]{0:T(128)} %bitcast.2.refs_0_.place_ref, bf16[320,128]{1,0:T(8,128)(2,1)S(1)} %collective-permute-done.refs_1_, ...), custom_call_target="tpu_custom_call" | custom-call | tf_op jit(solution)/shard_map/pallas_call | solution.py:547
  24.0 0.0 collective-permute-start.9
  24.1 1.6 %collective-permute-start.8 = (f32[8,256]{1,0:T(8,128)S(1)}, f32[8,256]{1,0:T(8,128)S(1)}, u32[]{:S(2)}, u32[]{:S(2)}) collective-permute-start(f32[8,256]{1,0:T(8,128)S(1)} %get-tuple-element.74.refs_0_), channel_id=1, source_target_pairs={{0,2},{1,3},{2,0},{3,1},{4,6},{5,7},{6,4},{7,5},{8,10},{9,11},{10,... | collective-permute-start | bytes 24584 | tf_op jit(solution)/shard_map/ppermute | solution.py:642
  25.6 0.3 collective-permute-start.7
  25.9 1.2 %collective-permute-done.9.refs_3_ = f32[8,256]{1,0:T(8,128)S(1)} collective-permute-done((f32[8,256]{1,0:T(8,128)S(1)}, f32[8,256]{1,0:T(8,128)S(1)}, u32[]{:S(2)}, u32[]{:S(2)}) %collective-permute-start.9) | collective-permute-done | bytes 8224 | tf_op jit(solution)/shard_map/ppermute | solution.py:642
  27.1 0.6 %collective-permute-done.8.refs_2_ = f32[8,256]{1,0:T(8,128)S(1)} collective-permute-done((f32[8,256]{1,0:T(8,128)S(1)}, f32[8,256]{1,0:T(8,128)S(1)}, u32[]{:S(2)}, u32[]{:S(2)}) %collective-permute-start.8) | collective-permute-done | bytes 8224 | tf_op jit(solution)/shard_map/ppermute | solution.py:642
  27.8 0.0 collective-permute-done.7.refs_1_
  27.8 1.1 %shard_map.154 = (bf16[320,128]{1,0:T(8,128)(2,1)S(1)}, bf16[320,128]{1,0:T(8,128)(2,1)S(1)}, f32[256,512]{1,0:T(8,128)S(1)}, f32[256,128]{1,0:T(8,128)S(1)}, f32[8,256]{1,0:T(8,128)S(1)}) custom-call(f32[8,256]{1,0:T(8,128)S(1)} %get-tuple-element.74.refs_0_, f32[8,256]{1,0:T(8,128)S(1)} %collective-permute-done.7.refs_1_, ...), custom_call_target="tpu_custom_call" | custom-call | tf_op jit(solution)/shard_map/pallas_call | solution.py:547
  28.9 1.9 %collective-permute-start.14 = (bf16[320,128]{1,0:T(8,128)(2,1)S(1)}, bf16[320,128]{1,0:T(8,128)(2,1)S(1)}, u32[]{:S(2)}, u32[]{:S(2)}) collective-permute-start(bf16[320,128]{1,0:T(8,128)(2,1)S(1)} %get-tuple-element.100.refs_0_), channel_id=1, source_target_pairs={{0,4},{4,0},{8,12},{12,8},{16,20},{20,16},{24,28},{28,24},{1,5},{5... | collective-permute-start | bytes 245768 | tf_op jit(solution)/shard_map/ppermute | solution.py:570
  30.8 1.5 %collective-permute-start.10 = (bf16[320,128]{1,0:T(8,128)(2,1)S(1)}, bf16[320,128]{1,0:T(8,128)(2,1)S(1)}, u32[]{:S(2)}, u32[]{:S(2)}) collective-permute-start(bf16[320,128]{1,0:T(8,128)(2,1)S(1)} %get-tuple-element.95.refs_2_.refs_3_), channel_id=1, source_target_pairs={{0,16},{4,20},{8,24},{12,28},{16,0},{20,4},{24,8},{28,12},{1,17},{... | collective-permute-start | bytes 245768 | tf_op jit(solution)/shard_map/ppermute | solution.py:570
  32.3 2.2 %shard_map.155 = (bf16[256,512]{1,0:T(8,128)(2,1)}, f32[256,512]{1,0:T(8,128)S(1)}, f32[256,512]{1,0:T(8,128)S(1)}, bf16[128,512]{1,0:T(8,128)(2,1)S(1)}) custom-call(bf16[256,512]{1,0:T(8,128)(2,1)S(1)} %get-tuple-element.85.wquery_ref, bf16[256,512]{1,0:T(8,128)(2,1)S(1)} %get-tuple-element.86.wkey_ref, ...), custom_call_target="tpu_custom_call" | custom-call | tf_op jit(solution)/shard_map/pallas_call | solution.py:547
  34.5 0.0 collective-permute-done.14.refs_1_
  34.5 1.1 %collective-permute-start.15 = (bf16[320,128]{1,0:T(8,128)(2,1)S(1)}, bf16[320,128]{1,0:T(8,128)(2,1)S(1)}, u32[]{:S(2)}, u32[]{:S(2)}) collective-permute-start(bf16[320,128]{1,0:T(8,128)(2,1)S(1)} %shard_map.159.mine_ref), channel_id=1, source_target_pairs={{0,8},{4,12},{8,0},{12,4},{16,24},{20,28},{24,16},{28,20},{1,9},{5... | collective-permute-start | bytes 245768 | tf_op jit(solution)/shard_map/ppermute | solution.py:570
  35.6 2.4 %collective-permute-done.10.refs_1_ = bf16[320,128]{1,0:T(8,128)(2,1)S(1)} collective-permute-done((bf16[320,128]{1,0:T(8,128)(2,1)S(1)}, bf16[320,128]{1,0:T(8,128)(2,1)S(1)}, u32[]{:S(2)}, u32[]{:S(2)}) %collective-permute-start.10) | collective-permute-done | bytes 81952 | tf_op jit(solution)/shard_map/ppermute | solution.py:570
  38.1 0.1 collective-permute-start.11
  38.1 1.9 %collective-permute-start.13 = (bf16[128,512]{1,0:T(8,128)(2,1)S(1)}, bf16[128,512]{1,0:T(8,128)(2,1)S(1)}, u32[]{:S(2)}, u32[]{:S(2)}) collective-permute-start(bf16[128,512]{1,0:T(8,128)(2,1)S(1)} %get-tuple-element.99), channel_id=1, source_target_pairs={{4,0},{8,4},{12,8},{16,12},{20,16},{24,20},{28,24},{0,28},{5,1},{9... | collective-permute-start | bytes 393224 | tf_op jit(solution)/shard_map/ppermute | solution.py:655
  40.0 0.0 collective-permute-done.15.theirs_ref.refs_2_
  40.0 1.4 %collective-permute-start.16 = (bf16[320,128]{1,0:T(8,128)(2,1)S(1)}, bf16[320,128]{1,0:T(8,128)(2,1)S(1)}, u32[]{:S(2)}, u32[]{:S(2)}) collective-permute-start(bf16[320,128]{1,0:T(8,128)(2,1)S(1)} %shard_map.160), channel_id=1, source_target_pairs={{0,16},{4,20},{8,24},{12,28},{16,0},{20,4},{24,8},{28,12},{1,17},{... | collective-permute-start | bytes 245768 | tf_op jit(solution)/shard_map/ppermute | solution.py:570
  41.5 2.3 %collective-permute-done.11.refs_2_ = bf16[320,128]{1,0:T(8,128)(2,1)S(1)} collective-permute-done((bf16[320,128]{1,0:T(8,128)(2,1)S(1)}, bf16[320,128]{1,0:T(8,128)(2,1)S(1)}, u32[]{:S(2)}, u32[]{:S(2)}) %collective-permute-start.11) | collective-permute-done | bytes 81952 | tf_op jit(solution)/shard_map/ppermute | solution.py:570
  43.7 0.1 shard_map.158
  43.8 0.1 collective-permute-start.12
  43.9 2.8 %shard_map.156 = (bf16[64,256]{1,0:T(8,128)(2,1)}, f32[64,256]{1,0:T(8,128)S(1)}, f32[256,512]{1,0:T(8,128)S(1)}, bf16[256,512]{1,0:T(8,128)(2,1)}, bf16[4,256,160]{2,1,0:T(8,128)(2,1)S(1)}) custom-call(bf16[64,256]{1,0:T(8,128)(2,1)S(1)} %get-tuple-element.62.query_ref, bf16[64,256]{1,0:T(8,128)(2,1)S(1)} %get-tuple-element.57.key_ref.refs_4_, ...), custom_call_target="tpu_custom_call" | custom-call | tf_op jit(solution)/shard_map/pallas_call | solution.py:547
  46.6 0.0 collective-permute-done.13.refs_11_
  46.6 1.2 %collective-permute-done.16.refs_3_ = bf16[320,128]{1,0:T(8,128)(2,1)S(1)} collective-permute-done((bf16[320,128]{1,0:T(8,128)(2,1)S(1)}, bf16[320,128]{1,0:T(8,128)(2,1)S(1)}, u32[]{:S(2)}, u32[]{:S(2)}) %collective-permute-start.16) | collective-permute-done | bytes 81952 | tf_op jit(solution)/shard_map/ppermute | solution.py:570
  47.8 1.3 %shard_map.161 = (bf16[32,256]{1,0:T(8,128)(2,1)S(1)}, bf16[256,256]{1,0:T(8,128)(2,1)S(1)}, bf16[256,512]{1,0:T(8,128)(2,1)}) custom-call(s32[1]{0:T(128)} %bitcast.2.refs_0_.place_ref, bf16[320,128]{1,0:T(8,128)(2,1)S(1)} %collective-permute-done.14.refs_1_, bf16[320,128]{1,0:T(8,128)(2,1)S(1)} %collective-permute-done.15.theirs_ref.refs_2_, ...), custom_call_target="tpu_custom_call" | custom-call | tf_op jit(solution)/shard_map/pallas_call | solution.py:547
  49.1 0.0 collective-permute-done.12.refs_3_
  49.1 1.3 %shard_map.162 = (bf16[64,256]{1,0:T(8,128)(2,1)}, bf16[256,512]{1,0:T(8,128)(2,1)}) custom-call(s32[1]{0:T(128)} %bitcast.2.refs_0_.place_ref, bf16[320,128]{1,0:T(8,128)(2,1)S(1)} %collective-permute-done.10.refs_1_, bf16[320,128]{1,0:T(8,128)(2,1)S(1)} %collective-permute-done.11.refs_2_, bf16[320,128]{1,0:T(8,128)(2,1)S(1)} %collective-permute-done.12.refs_3_, ...), custom_call_target="tpu_custom_call" | custom-call | tf_op jit(solution)/shard_map/pallas_call | solution.py:547
  (3 shorter events, 0.1 us)
Async XLA Ops:
  2.4 7.9 %collective-permute-start.4 = (bf16[320,128]{1,0:T(8,128)(2,1)S(1)}, bf16[320,128]{1,0:T(8,128)(2,1)S(1)}, u32[]{:S(2)}, u32[]{:S(2)}) collective-permute-start(bf16[320,128]{1,0:T(8,128)(2,1)S(1)} %get-tuple-element.71.refs_0_), channel_id=1, source_target_pairs={{0,4},{4,0},{8,12},{12,8},{16,20},{20,16},{24,28},{28,24},{1,5},{5... | collective-permute-start | bytes 245768 | tf_op jit(solution)/shard_map/ppermute | solution.py:570
  5.4 6.7 %collective-permute-start = (bf16[320,128]{1,0:T(8,128)(2,1)S(1)}, bf16[320,128]{1,0:T(8,128)(2,1)S(1)}, u32[]{:S(2)}, u32[]{:S(2)}) collective-permute-start(bf16[320,128]{1,0:T(8,128)(2,1)S(1)} %get-tuple-element.63.refs_2_.refs_3_), channel_id=1, source_target_pairs={{0,16},{4,20},{8,24},{12,28},{16,0},{20,4},{24,8},{28,12},{1,17},{... | collective-permute-start | bytes 245768 | tf_op jit(solution)/shard_map/ppermute | solution.py:570
  8.0 8.6 %collective-permute-start.3 = (bf16[128,512]{1,0:T(8,128)(2,1)S(1)}, bf16[128,512]{1,0:T(8,128)(2,1)S(1)}, u32[]{:S(2)}, u32[]{:S(2)}) collective-permute-start(bf16[128,512]{1,0:T(8,128)(2,1)S(1)} %get-tuple-element.67), channel_id=1, source_target_pairs={{0,4},{4,8},{8,12},{12,16},{16,20},{20,24},{24,28},{28,0},{1,5},{5... | collective-permute-start | bytes 393224 | tf_op jit(solution)/shard_map/ppermute | solution.py:612
  10.5 6.2 %collective-permute-start.5 = (bf16[320,128]{1,0:T(8,128)(2,1)S(1)}, bf16[320,128]{1,0:T(8,128)(2,1)S(1)}, u32[]{:S(2)}, u32[]{:S(2)}) collective-permute-start(bf16[320,128]{1,0:T(8,128)(2,1)S(1)} %shard_map.150.refs_0_), channel_id=1, source_target_pairs={{0,8},{4,12},{8,0},{12,4},{16,24},{20,28},{24,16},{28,20},{1,9},{5... | collective-permute-start | bytes 245768 | tf_op jit(solution)/shard_map/ppermute | solution.py:570
  12.4 5.3 %collective-permute-start.1 = (bf16[320,128]{1,0:T(8,128)(2,1)S(1)}, bf16[320,128]{1,0:T(8,128)(2,1)S(1)}, u32[]{:S(2)}, u32[]{:S(2)}) collective-permute-start(bf16[320,128]{1,0:T(8,128)(2,1)S(1)} %shard_map.147), channel_id=1, source_target_pairs={{0,8},{4,12},{8,0},{12,4},{16,24},{20,28},{24,16},{28,20},{1,9},{5... | collective-permute-start | bytes 245768 | tf_op jit(solution)/shard_map/ppermute | solution.py:570
  16.9 5.9 %collective-permute-start.6 = (bf16[320,128]{1,0:T(8,128)(2,1)S(1)}, bf16[320,128]{1,0:T(8,128)(2,1)S(1)}, u32[]{:S(2)}, u32[]{:S(2)}) collective-permute-start(bf16[320,128]{1,0:T(8,128)(2,1)S(1)} %shard_map.151), channel_id=1, source_target_pairs={{0,16},{4,20},{8,24},{12,28},{16,0},{20,4},{24,8},{28,12},{1,17},{... | collective-permute-start | bytes 245768 | tf_op jit(solution)/shard_map/ppermute | solution.py:570
  17.9 5.4 %collective-permute-start.2 = (bf16[320,128]{1,0:T(8,128)(2,1)S(1)}, bf16[320,128]{1,0:T(8,128)(2,1)S(1)}, u32[]{:S(2)}, u32[]{:S(2)}) collective-permute-start(bf16[320,128]{1,0:T(8,128)(2,1)S(1)} %shard_map.148), channel_id=1, source_target_pairs={{0,4},{4,0},{8,12},{12,8},{16,20},{20,16},{24,28},{28,24},{1,5},{5... | collective-permute-start | bytes 245768 | tf_op jit(solution)/shard_map/ppermute | solution.py:570
  24.0 3.1 %collective-permute-start.9 = (f32[8,256]{1,0:T(8,128)S(1)}, f32[8,256]{1,0:T(8,128)S(1)}, u32[]{:S(2)}, u32[]{:S(2)}) collective-permute-start(f32[8,256]{1,0:T(8,128)S(1)} %get-tuple-element.74.refs_0_), channel_id=1, source_target_pairs={{0,3},{1,2},{2,1},{3,0},{4,7},{5,6},{6,5},{7,4},{8,11},{9,10},{10,... | collective-permute-start | bytes 24584 | tf_op jit(solution)/shard_map/ppermute | solution.py:642
  24.1 3.7 %collective-permute-start.8 = (f32[8,256]{1,0:T(8,128)S(1)}, f32[8,256]{1,0:T(8,128)S(1)}, u32[]{:S(2)}, u32[]{:S(2)}) collective-permute-start(f32[8,256]{1,0:T(8,128)S(1)} %get-tuple-element.74.refs_0_), channel_id=1, source_target_pairs={{0,2},{1,3},{2,0},{3,1},{4,6},{5,7},{6,4},{7,5},{8,10},{9,11},{10,... | collective-permute-start | bytes 24584 | tf_op jit(solution)/shard_map/ppermute | solution.py:642
  25.6 2.1 %collective-permute-start.7 = (f32[8,256]{1,0:T(8,128)S(1)}, f32[8,256]{1,0:T(8,128)S(1)}, u32[]{:S(2)}, u32[]{:S(2)}) collective-permute-start(f32[8,256]{1,0:T(8,128)S(1)} %get-tuple-element.74.refs_0_), channel_id=1, source_target_pairs={{0,1},{1,0},{2,3},{3,2},{4,5},{5,4},{6,7},{7,6},{8,9},{9,8},{10,11... | collective-permute-start | bytes 24584 | tf_op jit(solution)/shard_map/ppermute | solution.py:642
  28.9 5.6 %collective-permute-start.14 = (bf16[320,128]{1,0:T(8,128)(2,1)S(1)}, bf16[320,128]{1,0:T(8,128)(2,1)S(1)}, u32[]{:S(2)}, u32[]{:S(2)}) collective-permute-start(bf16[320,128]{1,0:T(8,128)(2,1)S(1)} %get-tuple-element.100.refs_0_), channel_id=1, source_target_pairs={{0,4},{4,0},{8,12},{12,8},{16,20},{20,16},{24,28},{28,24},{1,5},{5... | collective-permute-start | bytes 245768 | tf_op jit(solution)/shard_map/ppermute | solution.py:570
  30.8 7.2 %collective-permute-start.10 = (bf16[320,128]{1,0:T(8,128)(2,1)S(1)}, bf16[320,128]{1,0:T(8,128)(2,1)S(1)}, u32[]{:S(2)}, u32[]{:S(2)}) collective-permute-start(bf16[320,128]{1,0:T(8,128)(2,1)S(1)} %get-tuple-element.95.refs_2_.refs_3_), channel_id=1, source_target_pairs={{0,16},{4,20},{8,24},{12,28},{16,0},{20,4},{24,8},{28,12},{1,17},{... | collective-permute-start | bytes 245768 | tf_op jit(solution)/shard_map/ppermute | solution.py:570
  34.5 5.5 %collective-permute-start.15 = (bf16[320,128]{1,0:T(8,128)(2,1)S(1)}, bf16[320,128]{1,0:T(8,128)(2,1)S(1)}, u32[]{:S(2)}, u32[]{:S(2)}) collective-permute-start(bf16[320,128]{1,0:T(8,128)(2,1)S(1)} %shard_map.159.mine_ref), channel_id=1, source_target_pairs={{0,8},{4,12},{8,0},{12,4},{16,24},{20,28},{24,16},{28,20},{1,9},{5... | collective-permute-start | bytes 245768 | tf_op jit(solution)/shard_map/ppermute | solution.py:570
  38.1 5.7 %collective-permute-start.11 = (bf16[320,128]{1,0:T(8,128)(2,1)S(1)}, bf16[320,128]{1,0:T(8,128)(2,1)S(1)}, u32[]{:S(2)}, u32[]{:S(2)}) collective-permute-start(bf16[320,128]{1,0:T(8,128)(2,1)S(1)} %shard_map.157), channel_id=1, source_target_pairs={{0,8},{4,12},{8,0},{12,4},{16,24},{20,28},{24,16},{28,20},{1,9},{5... | collective-permute-start | bytes 245768 | tf_op jit(solution)/shard_map/ppermute | solution.py:570
  38.1 8.5 %collective-permute-start.13 = (bf16[128,512]{1,0:T(8,128)(2,1)S(1)}, bf16[128,512]{1,0:T(8,128)(2,1)S(1)}, u32[]{:S(2)}, u32[]{:S(2)}) collective-permute-start(bf16[128,512]{1,0:T(8,128)(2,1)S(1)} %get-tuple-element.99), channel_id=1, source_target_pairs={{4,0},{8,4},{12,8},{16,12},{20,16},{24,20},{28,24},{0,28},{5,1},{9... | collective-permute-start | bytes 393224 | tf_op jit(solution)/shard_map/ppermute | solution.py:655
  40.0 7.8 %collective-permute-start.16 = (bf16[320,128]{1,0:T(8,128)(2,1)S(1)}, bf16[320,128]{1,0:T(8,128)(2,1)S(1)}, u32[]{:S(2)}, u32[]{:S(2)}) collective-permute-start(bf16[320,128]{1,0:T(8,128)(2,1)S(1)} %shard_map.160), channel_id=1, source_target_pairs={{0,16},{4,20},{8,24},{12,28},{16,0},{20,4},{24,8},{28,12},{1,17},{... | collective-permute-start | bytes 245768 | tf_op jit(solution)/shard_map/ppermute | solution.py:570
  43.8 5.3 %collective-permute-start.12 = (bf16[320,128]{1,0:T(8,128)(2,1)S(1)}, bf16[320,128]{1,0:T(8,128)(2,1)S(1)}, u32[]{:S(2)}, u32[]{:S(2)}) collective-permute-start(bf16[320,128]{1,0:T(8,128)(2,1)S(1)} %shard_map.158), channel_id=1, source_target_pairs={{0,4},{4,0},{8,12},{12,8},{16,20},{20,16},{24,28},{28,24},{1,5},{5... | collective-permute-start | bytes 245768 | tf_op jit(solution)/shard_map/ppermute | solution.py:570

commit v3 on v2

--- a/solution.py
+++ b/solution.py
@@ -174,13 +174,14 @@
     copies = [pltpu.make_async_copy(a, b, sems.at[i]) for i, (a, b) in enumerate(pairs)]
     for copy in copies:
         copy.start()
-    for copy in copies[:3]:
-        copy.wait()
+    copies[0].wait()
+    copies[1].wait()
     sel = sel_ref[...]
     ones = jnp.ones((8, length), BF16)
     place = iota((8, 128), 0)
     feats = [feature_rows(key_ref[span(h, FEAT), :], sel) for h in range(heads)]
     norms = [mm_nt(ones, feat)[0:1] for feat in feats]
+    copies[2].wait()
     sums = [mm(feat, value_ref[:, span(h, HEAD_DIM)]) for h, feat in enumerate(feats)]
     middles = [(state[CONST : CONST + 1] * (1.0 / length)).astype(BF16).astype(F32) for state in sums]
     moved = [mm_tn(stack8(list(split(norm))), stack8([middle, middle])) for norm, middle in zip(norms, middles)]
@@ -243,17 +244,19 @@
         store_state(out_ref, h, total, norm_tile(tile_norm(total[CONST:])))
 
 
-def local_body(query_hbm, key_ref, value_ref, sel_ref, sel_t_ref, rows_ref,
-               numer_ref, denom_ref, featq_ref, featq_t_ref, query_ref, sems):
-    copy = pltpu.make_async_copy(query_hbm, query_ref, sems.at[0])
-    copy.start()
+def local_body(query_hbm, wquery_hbm, wkey_hbm, key_ref, value_ref, sel_ref, sel_t_ref, rows_ref,
+               numer_ref, denom_ref, featq_ref, featq_t_ref, query_ref, wquery_ref, wkey_ref, sems):
+    pairs = [(query_hbm, query_ref), (wquery_hbm, wquery_ref), (wkey_hbm, wkey_ref)]
+    copies = [pltpu.make_async_copy(a, b, sems.at[i]) for i, (a, b) in enumerate(pairs)]
+    for copy in copies:
+        copy.start()
     length = value_ref.shape[0]
     heads = value_ref.shape[1] // HEAD_DIM
     sel = sel_ref[...]
     sel_t = sel_t_ref[...]
     rows = rows_ref[...]
     keys = [key_ref[span(h, FEAT), :] for h in range(heads)]
-    copy.wait()
+    copies[0].wait()
     causal = causal_mask(length)
     lane = iota((length, 128), 1)
     queries = [query_ref[span(h, FEAT), :] for h in range(heads)]
@@ -270,11 +273,13 @@
         featq_ref[h] = features[h]
         numer_ref[:, span(h, HEAD_DIM)] = numers[h]
     denom_ref[...] = denoms
-
-
-def window_body(place_ref, wquery_hbm, wkey_hbm, cot_hbm, gain_hbm, value_ref, rim_ref,
-                out_ref, weights_ref, wquery_ref, wkey_ref, cot_ref, gain_ref, sems):
-    pairs = [(wquery_hbm, wquery_ref), (wkey_hbm, wkey_ref), (cot_hbm, cot_ref), (gain_hbm, gain_ref)]
+    copies[1].wait()
+    copies[2].wait()
+
+
+def window_body(place_ref, cot_hbm, gain_hbm, wquery_ref, wkey_ref, value_ref, rim_ref,
+                out_ref, weights_ref, cot_ref, gain_ref, sems):
+    pairs = [(cot_hbm, cot_ref), (gain_hbm, gain_ref)]
     copies = [pltpu.make_async_copy(a, b, sems.at[i]) for i, (a, b) in enumerate(pairs)]
     for copy in copies:
         copy.start()
@@ -287,8 +292,6 @@
     edge = inside & ((col >= WINDOW) | live)
     starts = range(0, length, WINDOW)
     allowed = jnp.concatenate([edge] + [inside] * (len(starts) - 1), axis=0)
-    copies[0].wait()
-    copies[1].wait()
     for h in range(heads):
         columns = span(h, HEAD_DIM)
         keys = jnp.concatenate([rim_ref[:WINDOW, columns], wkey_ref[:, columns]], axis=0)
@@ -301,8 +304,8 @@
         weights_ref[h] = weights
         narrow = weights.astype(BF16)
         out_ref[:, columns] = jnp.concatenate([mm(narrow[s : s + WINDOW], values[s : s + 2 * WINDOW]) for s in starts], axis=0)
-    copies[2].wait()
-    copies[3].wait()
+    copies[0].wait()
+    copies[1].wait()
 
 
 def taken(place_ref, bit, later):
@@ -413,14 +416,19 @@
     ratios_ref[...] = ratios
 
 
-def window_back_body(wquery_ref, wkey_ref, value_ref, rim_ref, weights_ref, grad_ref, gwq_ref, gwk_ref, gv_ref, back_ref):
+def window_back_body(wquery_ref, wkey_ref, value_ref, rim_ref, weights_ref, grad_ref, cols_ref, gain_ref, *refs):
+    merged_refs, (gwq_ref, gwk_ref, gv_ref, back_ref, normed_ref) = refs[:CHUNKS], refs[CHUNKS:]
     length = wquery_ref.shape[0]
     heads = value_ref.shape[1] // HEAD_DIM
     root = 1.0 / math.sqrt(HEAD_DIM)
     starts = range(0, length, WINDOW)
     pad = jnp.zeros((WINDOW, HEAD_DIM), F32)
+    inv_rms = cols_ref[:, heads : heads + 1]
+    per = heads // CHUNKS
     for h in range(heads):
         columns = span(h, HEAD_DIM)
+        merged = merged_refs[h // per][:, span(h % per, HEAD_DIM)]
+        normed_ref[:, columns] = (merged * inv_rms * gain_ref[0:1, columns]).astype(BF16)
         keys = jnp.concatenate([rim_ref[:WINDOW, columns], wkey_ref[:, columns]], axis=0)
         values = jnp.concatenate([rim_ref[WINDOW:, columns], value_ref[:, columns]], axis=0)
         grad = grad_ref[:, columns].astype(BF16)
@@ -441,17 +449,15 @@
         gv_ref[:, columns] = jnp.concatenate(value_sum, axis=0)
 
 
-def local_back_body(query_ref, key_ref, value_ref, sel_ref, sel_t_ref, rows_ref, grad_ref, cols_ref, ratios_ref, gv_in_ref, gain_ref, *refs):
-    merged_refs, inverse_refs = refs[:CHUNKS], refs[CHUNKS : 2 * CHUNKS]
-    prefix_refs, norm_refs = refs[2 * CHUNKS : 3 * CHUNKS], refs[3 * CHUNKS : 4 * CHUNKS]
-    gq_ref, gk_ref, gv_ref, normed_ref, feat_ref = refs[4 * CHUNKS :]
+def local_back_body(query_ref, key_ref, value_ref, sel_ref, sel_t_ref, rows_ref, grad_ref, cols_ref, ratios_ref, gv_in_ref, *refs):
+    inverse_refs, prefix_refs, norm_refs = refs[:CHUNKS], refs[CHUNKS : 2 * CHUNKS], refs[2 * CHUNKS : 3 * CHUNKS]
+    gq_ref, gk_ref, gv_ref, feat_ref = refs[3 * CHUNKS :]
     length = value_ref.shape[0]
     heads = value_ref.shape[1] // HEAD_DIM
     per = heads // CHUNKS
     sel = sel_ref[...]
     sel_t = sel_t_ref[...]
     causal = causal_mask(length)
-    inv_rms = cols_ref[:, heads : heads + 1]
     queries = [query_ref[span(h, FEAT), :] for h in range(heads)]
     keys = [key_ref[span(h, FEAT), :] for h in range(heads)]
     scaled = [grad_ref[:, span(h, HEAD_DIM)] * inverse_refs[h // per][:, h % per : h % per + 1] for h in range(heads)]
@@ -478,8 +484,6 @@
     features = [weighted_features(key, sel_t, rows) for key in keys]
     for h in range(heads):
         columns = span(h, HEAD_DIM)
-        merged = merged_refs[h // per][:, span(h % per, HEAD_DIM)]
-        normed_ref[:, columns] = (merged * inv_rms * gain_ref[0:1, columns]).astype(BF16)
         feat_ref[h] = features[h]
         gk_ref[span(h, FEAT), :] = by_key[h]
         gv_ref[:, columns] = gv_in_ref[:, columns] + values[h]
@@ -501,12 +505,22 @@
         gwk_in_ref, gk_ref, gv_ref, gwk_ref = rest
         gwk_ref[:cut, :] = gwk_in_ref[:cut, :].astype(BF16)
         gwk_ref[cut:, :] = (gwk_in_ref[cut:, :] + back_ref[:WINDOW, :].astype(F32)).astype(BF16)
-        base = 0
     else:
-        gk_before, gv_before, gk_ref, gv_ref = rest
-        base = chunk * per
-        gk_ref[: base * FEAT, :] = gk_before[...]
-        gv_ref[:, : base * HEAD_DIM] = gv_before[...]
+        gwk_in, gq_in, gk_before, gv_before, gwk_out, gq_out, gk_out, gv_out, gk_ref, gv_ref, sems = rest
+        own, other = chunk * per, (1 - chunk) * per
+        early = [
+            (gwk_in, gwk_out),
+            (gv_before, gv_out.at[:, other * HEAD_DIM : (other + per) * HEAD_DIM]),
+            (gk_before, gk_out.at[other * FEAT : (other + per) * FEAT, :]),
+            (gq_in, gq_out),
+        ]
+        late = [
+            (gv_ref, gv_out.at[:, own * HEAD_DIM : (own + per) * HEAD_DIM]),
+            (gk_ref, gk_out.at[own * FEAT : (own + per) * FEAT, :]),
+        ]
+        copies = [pltpu.make_async_copy(a, b, sems.at[i]) for i, (a, b) in enumerate(early + late)]
+        for copy in copies[: len(early)]:
+            copy.start()
     wholes = [chunk * per + h for h in range(per)]
     states = []
     for h in range(per):
@@ -525,13 +539,19 @@
     for h, whole in enumerate(wholes):
         columns = span(whole, HEAD_DIM)
         grad_value = gv_in_ref[:, columns] + reads[h]
-        out_columns = span(base + h, HEAD_DIM)
-        gv_ref[:cut, out_columns] = grad_value[:cut].astype(BF16)
-        gv_ref[cut:, out_columns] = (grad_value[cut:] + back_ref[WINDOW:, columns].astype(F32)).astype(BF16)
-        gk_ref[span(base + h, FEAT), :] = (gk_in_ref[span(whole, FEAT), :] + through[h]).astype(BF16)
-
-
-def call(body, outs, *args, place=None, hbm=0, copies=0, results=(), ties=()):
+        gv_ref[:cut, span(h, HEAD_DIM)] = grad_value[:cut].astype(BF16)
+        gv_ref[cut:, span(h, HEAD_DIM)] = (grad_value[cut:] + back_ref[WINDOW:, columns].astype(F32)).astype(BF16)
+    if chunk + 1 == CHUNKS:
+        copies[-2].start()
+    for h, whole in enumerate(wholes):
+        gk_ref[span(h, FEAT), :] = (gk_in_ref[span(whole, FEAT), :] + through[h]).astype(BF16)
+    if chunk + 1 == CHUNKS:
+        copies[-1].start()
+        for copy in copies:
+            copy.wait()
+
+
+def call(body, outs, *args, place=None, hbm=0, copies=0, results=(), ties=(), held=None):
     vmem = pl.BlockSpec(memory_space=pltpu.VMEM)
     specs = [pl.BlockSpec(memory_space=pltpu.HBM)] * hbm + [vmem] * (len(args) - hbm)
     args = tuple(
@@ -547,12 +567,15 @@
     return pl.pallas_call(
         body if not ties else lambda *refs: body(*refs[:given], *refs[given + len(ties) :]),
         out_shape=[
-            jax.ShapeDtypeStruct(shape, dtype) if i in results else pltpu.VMEM(shape, dtype)
+            pltpu.HBM(shape, dtype) if i in results else pltpu.VMEM(shape, dtype)
             for i, (shape, dtype) in enumerate(outs)
         ],
         in_specs=specs,
-        out_specs=[vmem] * len(outs),
-        scratch_shapes=[pltpu.SemaphoreType.DMA((copies,))] if copies else [],
+        out_specs=[
+            pl.BlockSpec(memory_space=pltpu.HBM) if held and i in results else vmem for i in range(len(outs))
+        ],
+        scratch_shapes=[pltpu.VMEM(shape, dtype) for shape, dtype in held or ()]
+        + ([pltpu.SemaphoreType.DMA((copies,))] if copies else []),
         compiler_params=pltpu.CompilerParams(vmem_limit_bytes=VMEM_LIMIT),
     )(*args)
 
@@ -563,7 +586,7 @@
     orders = [bits if c % 2 == 0 else bits[::-1] for c in range(len(states))]
     held = list(states)
     parts = [[] for _ in states]
-    extra, ties = None, []
+    extra, ties = None, {}
     for step in range(len(bits)):
         for c, order in enumerate(orders):
             pairs = [(i, i ^ (1 << order[step])) for i in range(count)]
@@ -573,7 +596,7 @@
         if step + 1 == len(bits):
             break
         for c, order in enumerate(orders):
-            tie = ties.pop(0) if c == 0 and ties else ()
+            tie = ties.get((step, c), ())
             shape = [(held[c].shape, BF16)]
             if c % 2:
                 counts = order[:1] + [None] * step
@@ -612,17 +635,18 @@
         rim_in = lax.ppermute(rim, "seq", [(i, (i + 1) % count) for i in range(count)])
         local = call(
             local_body,
-            [wide, ((length, 128), F32), ((heads, length, ROWS), BF16), ((heads * ROWS, length), BF16), (query_t.shape, BF16)],
-            query_t, key_v, value_v, sel, sel_t, rows, hbm=1, copies=1,
+            [wide, ((length, 128), F32), ((heads, length, ROWS), BF16), ((heads * ROWS, length), BF16), (query_t.shape, BF16),
+             wide_narrow, wide_narrow],
+            query_t, window_query, window_key, key_v, value_v, sel, sel_t, rows, hbm=3, copies=3,
         )
-        return (rim_in, local), [(local[1],), (rim_in,)]
+        return (rim_in, local), {(0, 1): (local[1],), (1, 1): (rim_in,)}
 
     parts, takes, (rim_in, local) = exchanged(states, add_about_body, gather_about_body, place, early)
-    numer, denom, featq, featq_t, query_v = local
-    window_out, weights, wquery, wkey, cot, gain_v = call(
+    numer, denom, featq, featq_t, query_v, wquery, wkey = local
+    window_out, weights, cot, gain_v = call(
         window_body,
-        [wide, ((heads, length, 2 * WINDOW), F32), wide_narrow, wide_narrow, wide_narrow, (gain_row.shape, F32)],
-        window_query, window_key, cotangent, gain_row, value_v, rim_in, place=place, hbm=4, copies=4,
+        [wide, ((heads, length, 2 * WINDOW), F32), wide_narrow, (gain_row.shape, F32)],
+        cotangent, gain_row, wquery, wkey, value_v, rim_in, place=place, hbm=2, copies=2,
     )
     half = ((length, per * HEAD_DIM), F32)
     square = ((length, 128), F32)
@@ -647,30 +671,31 @@
     )
 
     def middle():
-        grad_wquery, wkey_part, value_part, back = call(
+        grad_wquery, wkey_part, value_part, back, normed = call(
             window_back_body,
-            [wide_narrow, wide, wide, ((2 * WINDOW, width), BF16)],
-            wquery, wkey, value_v, rim_in, weights, grad, results=(0,),
+            [wide_narrow, wide, wide, ((2 * WINDOW, width), BF16), wide_narrow],
+            wquery, wkey, value_v, rim_in, weights, grad, cols, gain_v, *merged, results=(0, 4),
         )
         back = lax.ppermute(back, "seq", [((i + 1) % count, i) for i in range(count)])
-        return (grad_wquery, wkey_part, value_part, back), [(wkey_part,)]
-
-    parts, takes, (grad_wquery, wkey_part, value_part, back) = exchanged(terms, add_body, gather_body, place, middle)
-    grad_query, key_part, value_part, normed, featk = call(
+        return (grad_wquery, wkey_part, value_part, back, normed), {(0, 0): (wkey_part,)}
+
+    parts, takes, (grad_wquery, wkey_part, value_part, back, normed) = exchanged(terms, add_body, gather_body, place, middle)
+    grad_query, key_part, value_part, featk = call(
         local_back_body,
-        [(query_t.shape, BF16), (key_t.shape, F32), wide, wide_narrow, ((heads, length, ROWS), BF16)],
-        query_v, key_v, value_v, sel, sel_t, rows, grad, cols, ratios, value_part, gain_v, *merged, *inverse, *prefix, *norm, results=(0, 3),
+        [(query_t.shape, BF16), (key_t.shape, F32), wide, ((heads, length, ROWS), BF16)],
+        query_v, key_v, value_v, sel, sel_t, rows, grad, cols, ratios, value_part, *inverse, *prefix, *norm,
     )
     common = (key_v, value_v, sel, sel_t, featk, key_part, value_part, back)
     grad_key, grad_value, grad_wkey = call(
         lambda *refs: final_body(takes[0], 0, *refs),
         [((per * FEAT, length), BF16), ((length, per * HEAD_DIM), BF16), wide_narrow],
-        *parts[0], *common, wkey_part, place=place, results=(2,),
+        *parts[0], *common, wkey_part, place=place,
     )
-    grad_key, grad_value = call(
+    grad_wkey, grad_query, grad_key, grad_value = call(
         lambda *refs: final_body(takes[1], 1, *refs),
-        [(key_t.shape, BF16), wide_narrow],
-        *parts[1], *common, grad_key, grad_value, place=place, results=(0, 1),
+        [wide_narrow, (query_t.shape, BF16), (key_t.shape, BF16), wide_narrow],
+        *parts[1], *common, grad_wkey, grad_query, grad_key, grad_value, place=place, results=(0, 1, 2, 3), copies=6,
+        held=[((per * FEAT, length), BF16), ((length, per * HEAD_DIM), BF16)],
     )
     return (normed, grad_query.T, grad_key.T, grad_value, grad_wquery, grad_wkey)
 

time: 50.6 us -> 49.7 us (0.982)
  starting transfers between devices: 21 us -> 24.4 us
  Pallas kernels: 17.2 us -> 15.1 us
  waiting for transfers between devices: 11.4 us -> 9.34 us
    ppermute x1, waiting for transfers between devices: 3.69 us -> 0.01 us  [early(): lax.ppermute(rim, 'seq', [(i, (i + 1) % count) for i in range(count)])]
    ppermute x12, starting transfers between devices: 16.8 us -> 19.7 us  [exchanged(): parts[c].append(lax.ppermute(held[c], 'seq', pairs))]
    pallas_call x18, Pallas kernels: 17.2 us -> 15.1 us  [call(): pl.pallas_call(body if not ties else lambda *refs: body(*refs[:given], *r...]
    ppermute x12, waiting for transfers between devices: 5.85 us -> 7.47 us  [exchanged(): parts[c].append(lax.ppermute(held[c], 'seq', pairs))]
  transfers between devices with their start and end apart: 17 -> 17, of which waited for: 6 -> 8; matrix products, arithmetic and copies ran while one was open for 0% -> 0% of each run, Pallas kernels for 24% -> 20%
where the time goes in v3:
time: 49.7 us; the launch traced here: 49.6 us
  starting transfers between devices  24.4 us (49%)
  Pallas kernels  15.1 us (30%)
  waiting for transfers between devices  9.34 us (19%)
  between operations  0.75 us (2%)
    ppermute x12, starting transfers between devices, exchanged(): parts[c].append(lax.ppermute(held[c], 'seq', pairs))  19.7 us
    pallas_call x18, Pallas kernels, call(): pl.pallas_call(body if not ties else lambda *refs: body(*refs[:given], *r...  15.1 us
    ppermute x12, waiting for transfers between devices, exchanged(): parts[c].append(lax.ppermute(held[c], 'seq', pairs))  7.47 us
    ppermute x1, starting transfers between devices, middle(): lax.ppermute(back, 'seq', [((i + 1) % count, i) for i in range(count)])  2.26 us
    ppermute x3, starting transfers between devices, shards(): lax.ppermute(stats, 'head', [(i, i ^ s) for i in range(ring)])  1.9 us
    ppermute x3, waiting for transfers between devices, shards(): lax.ppermute(stats, 'head', [(i, i ^ s) for i in range(ring)])  1.87 us
  transfers between devices with their start and end apart: 17, of which 8 were waited for; matrix products, arithmetic and copies ran while one was open for 0% of the time, Pallas kernels for 20%

profile of v3, /device:TPU:0, one launch (start us, length us, event | category | flops | bytes accessed | tf_op | source)
XLA Modules:
  0.0 49.6 jit_solution(14815611006138111403)
XLA Ops:
  0.6 1.8 %shard_map.145 = (bf16[320,128]{1,0:T(8,128)(2,1)S(1)}, bf16[320,128]{1,0:T(8,128)(2,1)S(1)}, bf16[128,512]{1,0:T(8,128)(2,1)S(1)}, bf16[64,256]{1,0:T(8,128)(2,...) custom-call(bf16[64,256]{1,0:T(8,128)(2,1)} %bitcast.6, ...), custom_call_target="tpu_custom_call" | custom-call | tf_op jit(solution)/shard_map/pallas_call | solution.py:567
  2.4 3.0 %collective-permute-start.4 = (bf16[320,128]{1,0:T(8,128)(2,1)S(1)}, bf16[320,128]{1,0:T(8,128)(2,1)S(1)}, u32[]{:S(2)}, u32[]{:S(2)}) collective-permute-start(bf16[320,128]{1,0:T(8,128)(2,1)S(1)} %get-tuple-element.75.mine_ref), channel_id=1, source_target_pairs={{0,4},{4,0},{8,12},{12,8},{16,20},{20,16},{24,28},{28,24},{1,5},{5... | collective-permute-start | bytes 245768 | tf_op jit(solution)/shard_map/ppermute | solution.py:593
  5.4 2.6 %collective-permute-start.1 = (bf16[320,128]{1,0:T(8,128)(2,1)S(1)}, bf16[320,128]{1,0:T(8,128)(2,1)S(1)}, u32[]{:S(2)}, u32[]{:S(2)}) collective-permute-start(bf16[320,128]{1,0:T(8,128)(2,1)S(1)} %get-tuple-element.68.refs_2_.refs_3_), channel_id=1, source_target_pairs={{0,16},{4,20},{8,24},{12,28},{16,0},{20,4},{24,8},{28,12},{1,17},{... | collective-permute-start | bytes 245768 | tf_op jit(solution)/shard_map/ppermute | solution.py:593
  8.0 0.5 %collective-permute-start = (bf16[128,512]{1,0:T(8,128)(2,1)S(1)}, bf16[128,512]{1,0:T(8,128)(2,1)S(1)}, u32[]{:S(2)}, u32[]{:S(2)}) collective-permute-start(bf16[128,512]{1,0:T(8,128)(2,1)S(1)} %get-tuple-element.66), channel_id=1, source_target_pairs={{0,4},{4,8},{8,12},{12,16},{16,20},{20,24},{24,28},{28,0},{1,5},{5... | collective-permute-start | bytes 393224 | tf_op jit(solution)/shard_map/ppermute | solution.py:635
  8.6 0.0 collective-permute-done.4.theirs_ref.refs_1_
  8.6 0.2 shard_map.150.mine_ref
  8.8 1.6 %collective-permute-start.5 = (bf16[320,128]{1,0:T(8,128)(2,1)S(1)}, bf16[320,128]{1,0:T(8,128)(2,1)S(1)}, u32[]{:S(2)}, u32[]{:S(2)}) collective-permute-start(bf16[320,128]{1,0:T(8,128)(2,1)S(1)} %shard_map.150.mine_ref), channel_id=1, source_target_pairs={{0,8},{4,12},{8,0},{12,4},{16,24},{20,28},{24,16},{28,20},{1,9},{5... | collective-permute-start | bytes 245768 | tf_op jit(solution)/shard_map/ppermute | solution.py:593
  10.4 1.7 %shard_map.146 = (f32[256,512]{1,0:T(8,128)S(1)}, f32[256,128]{1,0:T(8,128)S(1)}, bf16[4,256,160]{2,1,0:T(8,128)(2,1)S(1)}, bf16[640,256]{1,0:T(8,128)(2,1)S(1)}...) custom-call(bf16[64,256]{1,0:T(8,128)(2,1)} %bitcast.7, ...), custom_call_target="tpu_custom_call" | custom-call | tf_op jit(solution)/shard_map/pallas_call | solution.py:567
  12.2 0.0 collective-permute-done.1.refs_1_
  12.2 0.2 shard_map.148
  12.4 0.5 %collective-permute-start.2 = (bf16[320,128]{1,0:T(8,128)(2,1)S(1)}, bf16[320,128]{1,0:T(8,128)(2,1)S(1)}, u32[]{:S(2)}, u32[]{:S(2)}) collective-permute-start(bf16[320,128]{1,0:T(8,128)(2,1)S(1)} %shard_map.148), channel_id=1, source_target_pairs={{0,8},{4,12},{8,0},{12,4},{16,24},{20,28},{24,16},{28,20},{1,9},{5... | collective-permute-start | bytes 245768 | tf_op jit(solution)/shard_map/ppermute | solution.py:593
  13.0 0.3 collective-permute-done.5.theirs_ref.refs_2_
  13.3 0.2 shard_map.151
  13.5 3.2 %collective-permute-start.6 = (bf16[320,128]{1,0:T(8,128)(2,1)S(1)}, bf16[320,128]{1,0:T(8,128)(2,1)S(1)}, u32[]{:S(2)}, u32[]{:S(2)}) collective-permute-start(bf16[320,128]{1,0:T(8,128)(2,1)S(1)} %shard_map.151), channel_id=1, source_target_pairs={{0,16},{4,20},{8,24},{12,28},{16,0},{20,4},{24,8},{28,12},{1,17},{... | collective-permute-start | bytes 245768 | tf_op jit(solution)/shard_map/ppermute | solution.py:593
  16.7 0.0 collective-permute-done.rim_ref.refs_4_
  16.7 0.6 %collective-permute-done.2.refs_2_ = bf16[320,128]{1,0:T(8,128)(2,1)S(1)} collective-permute-done((bf16[320,128]{1,0:T(8,128)(2,1)S(1)}, bf16[320,128]{1,0:T(8,128)(2,1)S(1)}, u32[]{:S(2)}, u32[]{:S(2)}) %collective-permute-start.2) | collective-permute-done | bytes 81952 | tf_op jit(solution)/shard_map/ppermute | solution.py:593
  17.3 0.2 shard_map.149
  17.6 2.0 %collective-permute-start.3 = (bf16[320,128]{1,0:T(8,128)(2,1)S(1)}, bf16[320,128]{1,0:T(8,128)(2,1)S(1)}, u32[]{:S(2)}, u32[]{:S(2)}) collective-permute-start(bf16[320,128]{1,0:T(8,128)(2,1)S(1)} %shard_map.149), channel_id=1, source_target_pairs={{0,4},{4,0},{8,12},{12,8},{16,20},{20,16},{24,28},{28,24},{1,5},{5... | collective-permute-start | bytes 245768 | tf_op jit(solution)/shard_map/ppermute | solution.py:593
  19.6 1.7 %shard_map.147 = (f32[256,512]{1,0:T(8,128)S(1)}, f32[4,256,128]{2,1,0:T(8,128)S(1)}, bf16[256,512]{1,0:T(8,128)(2,1)S(1)}, f32[1,512]{1,0:T(1,128)S(1)}) custom-call(s32[1]{0:T(128)} %bitcast.2.place_ref.refs_0_, bf16[256,512]{1,0:T(8,128)(2,1)} %cot_hbm.1, f32[1,512]{1,0:T(1,128)} %bitcast.8, bf16[256,512]{1,0:T(8,128)(2,1)S(1)} %get-tuple-element.64.wquery_ref, ...), custom_call_target="tpu_custom_call" | custom-call | tf_op jit(solution)/shard_map/pallas_call | solution.py:567
  21.2 0.0 collective-permute-done.6.refs_3_
  21.3 0.5 %shard_map.152 = (f32[256,256]{1,0:T(8,128)S(1)}, f32[256,256]{1,0:T(8,128)S(1)}, f32[256,128]{1,0:T(8,128)S(1)}, f32[320,128]{1,0:T(8,128)S(1)}, f32[16,160]{1,...) custom-call(s32[1]{0:T(128)} %bitcast.2.place_ref.refs_0_, ...), custom_call_target="tpu_custom_call" | custom-call | tf_op jit(solution)/shard_map/pallas_call | solution.py:567
  21.8 0.3 collective-permute-done.3.refs_3_
  22.1 0.7 %shard_map.153 = (f32[256,256]{1,0:T(8,128)S(1)}, f32[256,256]{1,0:T(8,128)S(1)}, f32[256,128]{1,0:T(8,128)S(1)}, f32[320,128]{1,0:T(8,128)S(1)}, f32[16,160]{1,0:T(8,128)S(1)}, /*index=5*/f32[8,256]{1,0:T(8,128)S(1)}) custom-call(s32[1]{0:T(128)} %bitcast.2.place_ref.refs_0_, bf16[320,128]{1,0:T(8,128)(2,1)S(1)} %collective-permute-done.1.refs_1_, ...), custom_call_target="tpu_custom_call" | custom-call | tf_op jit(solution)/shard_map/pallas_call | solution.py:567
  22.7 0.1 collective-permute-start.9
  22.9 1.5 %collective-permute-start.8 = (f32[8,256]{1,0:T(8,128)S(1)}, f32[8,256]{1,0:T(8,128)S(1)}, u32[]{:S(2)}, u32[]{:S(2)}) collective-permute-start(f32[8,256]{1,0:T(8,128)S(1)} %get-tuple-element.78.refs_0_), channel_id=1, source_target_pairs={{0,2},{1,3},{2,0},{3,1},{4,6},{5,7},{6,4},{7,5},{8,10},{9,11},{10,... | collective-permute-start | bytes 24584 | tf_op jit(solution)/shard_map/ppermute | solution.py:666
  24.4 0.3 collective-permute-start.7
  24.6 1.2 %collective-permute-done.9.refs_3_ = f32[8,256]{1,0:T(8,128)S(1)} collective-permute-done((f32[8,256]{1,0:T(8,128)S(1)}, f32[8,256]{1,0:T(8,128)S(1)}, u32[]{:S(2)}, u32[]{:S(2)}) %collective-permute-start.9) | collective-permute-done | bytes 8224 | tf_op jit(solution)/shard_map/ppermute | solution.py:666
  25.9 0.6 %collective-permute-done.8.refs_2_ = f32[8,256]{1,0:T(8,128)S(1)} collective-permute-done((f32[8,256]{1,0:T(8,128)S(1)}, f32[8,256]{1,0:T(8,128)S(1)}, u32[]{:S(2)}, u32[]{:S(2)}) %collective-permute-start.8) | collective-permute-done | bytes 8224 | tf_op jit(solution)/shard_map/ppermute | solution.py:666
  26.5 0.0 collective-permute-done.7.refs_1_
  26.5 1.1 %shard_map.154 = (bf16[320,128]{1,0:T(8,128)(2,1)S(1)}, bf16[320,128]{1,0:T(8,128)(2,1)S(1)}, f32[256,512]{1,0:T(8,128)S(1)}, f32[256,128]{1,0:T(8,128)S(1)}, f32[8,256]{1,0:T(8,128)S(1)}) custom-call(f32[8,256]{1,0:T(8,128)S(1)} %get-tuple-element.78.refs_0_, f32[8,256]{1,0:T(8,128)S(1)} %collective-permute-done.7.refs_1_, ...), custom_call_target="tpu_custom_call" | custom-call | tf_op jit(solution)/shard_map/pallas_call | solution.py:567
  27.7 2.8 %collective-permute-start.14 = (bf16[320,128]{1,0:T(8,128)(2,1)S(1)}, bf16[320,128]{1,0:T(8,128)(2,1)S(1)}, u32[]{:S(2)}, u32[]{:S(2)}) collective-permute-start(bf16[320,128]{1,0:T(8,128)(2,1)S(1)} %get-tuple-element.101.refs_0_), channel_id=1, source_target_pairs={{0,4},{4,0},{8,12},{12,8},{16,20},{20,16},{24,28},{28,24},{1,5},{5... | collective-permute-start | bytes 245768 | tf_op jit(solution)/shard_map/ppermute | solution.py:593
  30.5 1.7 %collective-permute-start.10 = (bf16[320,128]{1,0:T(8,128)(2,1)S(1)}, bf16[320,128]{1,0:T(8,128)(2,1)S(1)}, u32[]{:S(2)}, u32[]{:S(2)}) collective-permute-start(bf16[320,128]{1,0:T(8,128)(2,1)S(1)} %get-tuple-element.89.refs_2_.refs_3_), channel_id=1, source_target_pairs={{0,16},{4,20},{8,24},{12,28},{16,0},{20,4},{24,8},{28,12},{1,17},{... | collective-permute-start | bytes 245768 | tf_op jit(solution)/shard_map/ppermute | solution.py:593
  32.1 2.3 %shard_map.155 = (bf16[256,512]{1,0:T(8,128)(2,1)}, f32[256,512]{1,0:T(8,128)S(1)}, f32[256,512]{1,0:T(8,128)S(1)}, bf16[128,512]{1,0:T(8,128)(2,1)S(1)}, bf16[256,512]{1,0:T(8,128)(2,1)}) custom-call(bf16[256,512]{1,0:T(8,128)(2,1)S(1)} %get-tuple-element.64.wquery_ref, bf16[256,512]{1,0:T(8,128)(2,1)S(1)} %get-tuple-element.65.wkey_ref, ...), custom_call_target="tpu_custom_call" | custom-call | tf_op jit(solution)/shard_map/pallas_call | solution.py:567
  34.4 0.0 collective-permute-done.14.refs_1_
  34.5 1.1 %collective-permute-start.15 = (bf16[320,128]{1,0:T(8,128)(2,1)S(1)}, bf16[320,128]{1,0:T(8,128)(2,1)S(1)}, u32[]{:S(2)}, u32[]{:S(2)}) collective-permute-start(bf16[320,128]{1,0:T(8,128)(2,1)S(1)} %shard_map.159.mine_ref), channel_id=1, source_target_pairs={{0,8},{4,12},{8,0},{12,4},{16,24},{20,28},{24,16},{28,20},{1,9},{5... | collective-permute-start | bytes 245768 | tf_op jit(solution)/shard_map/ppermute | solution.py:593
  35.5 2.1 %collective-permute-done.10.refs_1_ = bf16[320,128]{1,0:T(8,128)(2,1)S(1)} collective-permute-done((bf16[320,128]{1,0:T(8,128)(2,1)S(1)}, bf16[320,128]{1,0:T(8,128)(2,1)S(1)}, u32[]{:S(2)}, u32[]{:S(2)}) %collective-permute-start.10) | collective-permute-done | bytes 81952 | tf_op jit(solution)/shard_map/ppermute | solution.py:593
  37.7 0.1 collective-permute-start.11
  37.8 2.3 %collective-permute-start.13 = (bf16[128,512]{1,0:T(8,128)(2,1)S(1)}, bf16[128,512]{1,0:T(8,128)(2,1)S(1)}, u32[]{:S(2)}, u32[]{:S(2)}) collective-permute-start(bf16[128,512]{1,0:T(8,128)(2,1)S(1)} %get-tuple-element.100), channel_id=1, source_target_pairs={{4,0},{8,4},{12,8},{16,12},{20,16},{24,20},{28,24},{0,28},{5,1},{9... | collective-permute-start | bytes 393224 | tf_op jit(solution)/shard_map/ppermute | solution.py:679
  40.1 0.0 collective-permute-done.15.theirs_ref.refs_2_
  40.1 1.1 %collective-permute-start.16 = (bf16[320,128]{1,0:T(8,128)(2,1)S(1)}, bf16[320,128]{1,0:T(8,128)(2,1)S(1)}, u32[]{:S(2)}, u32[]{:S(2)}) collective-permute-start(bf16[320,128]{1,0:T(8,128)(2,1)S(1)} %shard_map.160), channel_id=1, source_target_pairs={{0,16},{4,20},{8,24},{12,28},{16,0},{20,4},{24,8},{28,12},{1,17},{... | collective-permute-start | bytes 245768 | tf_op jit(solution)/shard_map/ppermute | solution.py:593
  41.2 2.0 %collective-permute-done.11.refs_2_ = bf16[320,128]{1,0:T(8,128)(2,1)S(1)} collective-permute-done((bf16[320,128]{1,0:T(8,128)(2,1)S(1)}, bf16[320,128]{1,0:T(8,128)(2,1)S(1)}, u32[]{:S(2)}, u32[]{:S(2)}) %collective-permute-start.11) | collective-permute-done | bytes 81952 | tf_op jit(solution)/shard_map/ppermute | solution.py:593
  43.1 0.1 shard_map.157
  43.2 0.1 collective-permute-start.12
  43.3 2.1 %shard_map.158 = (bf16[64,256]{1,0:T(8,128)(2,1)S(1)}, f32[64,256]{1,0:T(8,128)S(1)}, f32[256,512]{1,0:T(8,128)S(1)}, bf16[4,256,160]{2,1,0:T(8,128)(2,1)S(1)}) custom-call(bf16[64,256]{1,0:T(8,128)(2,1)S(1)} %get-tuple-element.90.query_ref, bf16[64,256]{1,0:T(8,128)(2,1)S(1)} %get-tuple-element.59.key_ref.refs_4_, ...), custom_call_target="tpu_custom_call" | custom-call | tf_op jit(solution)/shard_map/pallas_call | solution.py:567
  45.3 0.0 collective-permute-done.13.refs_11_
  45.3 2.2 %collective-permute-done.16.refs_3_ = bf16[320,128]{1,0:T(8,128)(2,1)S(1)} collective-permute-done((bf16[320,128]{1,0:T(8,128)(2,1)S(1)}, bf16[320,128]{1,0:T(8,128)(2,1)S(1)}, u32[]{:S(2)}, u32[]{:S(2)}) %collective-permute-start.16) | collective-permute-done | bytes 81952 | tf_op jit(solution)/shard_map/ppermute | solution.py:593
  47.5 0.7 %shard_map.161 = (bf16[32,256]{1,0:T(8,128)(2,1)S(1)}, bf16[256,256]{1,0:T(8,128)(2,1)S(1)}, bf16[256,512]{1,0:T(8,128)(2,1)S(1)}) custom-call(s32[1]{0:T(128)} %bitcast.2.place_ref.refs_0_, bf16[320,128]{1,0:T(8,128)(2,1)S(1)} %collective-permute-done.14.refs_1_, bf16[320,128]{1,0:T(8,128)(2,1)S(1)} %collective-permute-done.15.theirs_ref.refs_2_, ...), custom_call_target="tpu_custom_call" | custom-call | tf_op jit(solution)/shard_map/pallas_call | solution.py:567
  48.2 0.0 collective-permute-done.12.refs_3_
  48.2 1.4 %shard_map.162 = (bf16[256,512]{1,0:T(8,128)(2,1)}, bf16[64,256]{1,0:T(8,128)(2,1)}, bf16[64,256]{1,0:T(8,128)(2,1)}, bf16[256,512]{1,0:T(8,128)(2,1)}) custom-call(s32[1]{0:T(128)} %bitcast.2.place_ref.refs_0_, bf16[320,128]{1,0:T(8,128)(2,1)S(1)} %collective-permute-done.10.refs_1_, bf16[320,128]{1,0:T(8,128)(2,1)S(1)} %collective-permute-done.11.refs_2_, ...), custom_call_target="tpu_custom_call" | custom-call | tf_op jit(solution)/shard_map/pallas_call | solution.py:567
  (3 shorter events, 0.1 us)
Async XLA Ops:
  2.4 6.1 %collective-permute-start.4 = (bf16[320,128]{1,0:T(8,128)(2,1)S(1)}, bf16[320,128]{1,0:T(8,128)(2,1)S(1)}, u32[]{:S(2)}, u32[]{:S(2)}) collective-permute-start(bf16[320,128]{1,0:T(8,128)(2,1)S(1)} %get-tuple-element.75.mine_ref), channel_id=1, source_target_pairs={{0,4},{4,0},{8,12},{12,8},{16,20},{20,16},{24,28},{28,24},{1,5},{5... | collective-permute-start | bytes 245768 | tf_op jit(solution)/shard_map/ppermute | solution.py:593
  5.4 6.7 %collective-permute-start.1 = (bf16[320,128]{1,0:T(8,128)(2,1)S(1)}, bf16[320,128]{1,0:T(8,128)(2,1)S(1)}, u32[]{:S(2)}, u32[]{:S(2)}) collective-permute-start(bf16[320,128]{1,0:T(8,128)(2,1)S(1)} %get-tuple-element.68.refs_2_.refs_3_), channel_id=1, source_target_pairs={{0,16},{4,20},{8,24},{12,28},{16,0},{20,4},{24,8},{28,12},{1,17},{... | collective-permute-start | bytes 245768 | tf_op jit(solution)/shard_map/ppermute | solution.py:593
  8.0 8.7 %collective-permute-start = (bf16[128,512]{1,0:T(8,128)(2,1)S(1)}, bf16[128,512]{1,0:T(8,128)(2,1)S(1)}, u32[]{:S(2)}, u32[]{:S(2)}) collective-permute-start(bf16[128,512]{1,0:T(8,128)(2,1)S(1)} %get-tuple-element.66), channel_id=1, source_target_pairs={{0,4},{4,8},{8,12},{12,16},{16,20},{20,24},{24,28},{28,0},{1,5},{5... | collective-permute-start | bytes 393224 | tf_op jit(solution)/shard_map/ppermute | solution.py:635
  8.8 4.5 %collective-permute-start.5 = (bf16[320,128]{1,0:T(8,128)(2,1)S(1)}, bf16[320,128]{1,0:T(8,128)(2,1)S(1)}, u32[]{:S(2)}, u32[]{:S(2)}) collective-permute-start(bf16[320,128]{1,0:T(8,128)(2,1)S(1)} %shard_map.150.mine_ref), channel_id=1, source_target_pairs={{0,8},{4,12},{8,0},{12,4},{16,24},{20,28},{24,16},{28,20},{1,9},{5... | collective-permute-start | bytes 245768 | tf_op jit(solution)/shard_map/ppermute | solution.py:593
  12.4 4.9 %collective-permute-start.2 = (bf16[320,128]{1,0:T(8,128)(2,1)S(1)}, bf16[320,128]{1,0:T(8,128)(2,1)S(1)}, u32[]{:S(2)}, u32[]{:S(2)}) collective-permute-start(bf16[320,128]{1,0:T(8,128)(2,1)S(1)} %shard_map.148), channel_id=1, source_target_pairs={{0,8},{4,12},{8,0},{12,4},{16,24},{20,28},{24,16},{28,20},{1,9},{5... | collective-permute-start | bytes 245768 | tf_op jit(solution)/shard_map/ppermute | solution.py:593
  13.5 7.7 %collective-permute-start.6 = (bf16[320,128]{1,0:T(8,128)(2,1)S(1)}, bf16[320,128]{1,0:T(8,128)(2,1)S(1)}, u32[]{:S(2)}, u32[]{:S(2)}) collective-permute-start(bf16[320,128]{1,0:T(8,128)(2,1)S(1)} %shard_map.151), channel_id=1, source_target_pairs={{0,16},{4,20},{8,24},{12,28},{16,0},{20,4},{24,8},{28,12},{1,17},{... | collective-permute-start | bytes 245768 | tf_op jit(solution)/shard_map/ppermute | solution.py:593
  17.6 4.5 %collective-permute-start.3 = (bf16[320,128]{1,0:T(8,128)(2,1)S(1)}, bf16[320,128]{1,0:T(8,128)(2,1)S(1)}, u32[]{:S(2)}, u32[]{:S(2)}) collective-permute-start(bf16[320,128]{1,0:T(8,128)(2,1)S(1)} %shard_map.149), channel_id=1, source_target_pairs={{0,4},{4,0},{8,12},{12,8},{16,20},{20,16},{24,28},{28,24},{1,5},{5... | collective-permute-start | bytes 245768 | tf_op jit(solution)/shard_map/ppermute | solution.py:593
  22.7 3.1 %collective-permute-start.9 = (f32[8,256]{1,0:T(8,128)S(1)}, f32[8,256]{1,0:T(8,128)S(1)}, u32[]{:S(2)}, u32[]{:S(2)}) collective-permute-start(f32[8,256]{1,0:T(8,128)S(1)} %get-tuple-element.78.refs_0_), channel_id=1, source_target_pairs={{0,3},{1,2},{2,1},{3,0},{4,7},{5,6},{6,5},{7,4},{8,11},{9,10},{10,... | collective-permute-start | bytes 24584 | tf_op jit(solution)/shard_map/ppermute | solution.py:666
  22.9 3.7 %collective-permute-start.8 = (f32[8,256]{1,0:T(8,128)S(1)}, f32[8,256]{1,0:T(8,128)S(1)}, u32[]{:S(2)}, u32[]{:S(2)}) collective-permute-start(f32[8,256]{1,0:T(8,128)S(1)} %get-tuple-element.78.refs_0_), channel_id=1, source_target_pairs={{0,2},{1,3},{2,0},{3,1},{4,6},{5,7},{6,4},{7,5},{8,10},{9,11},{10,... | collective-permute-start | bytes 24584 | tf_op jit(solution)/shard_map/ppermute | solution.py:666
  24.4 2.1 %collective-permute-start.7 = (f32[8,256]{1,0:T(8,128)S(1)}, f32[8,256]{1,0:T(8,128)S(1)}, u32[]{:S(2)}, u32[]{:S(2)}) collective-permute-start(f32[8,256]{1,0:T(8,128)S(1)} %get-tuple-element.78.refs_0_), channel_id=1, source_target_pairs={{0,1},{1,0},{2,3},{3,2},{4,5},{5,4},{6,7},{7,6},{8,9},{9,8},{10,11... | collective-permute-start | bytes 24584 | tf_op jit(solution)/shard_map/ppermute | solution.py:666
  27.7 6.8 %collective-permute-start.14 = (bf16[320,128]{1,0:T(8,128)(2,1)S(1)}, bf16[320,128]{1,0:T(8,128)(2,1)S(1)}, u32[]{:S(2)}, u32[]{:S(2)}) collective-permute-start(bf16[320,128]{1,0:T(8,128)(2,1)S(1)} %get-tuple-element.101.refs_0_), channel_id=1, source_target_pairs={{0,4},{4,0},{8,12},{12,8},{16,20},{20,16},{24,28},{28,24},{1,5},{5... | collective-permute-start | bytes 245768 | tf_op jit(solution)/shard_map/ppermute | solution.py:593
  30.5 7.2 %collective-permute-start.10 = (bf16[320,128]{1,0:T(8,128)(2,1)S(1)}, bf16[320,128]{1,0:T(8,128)(2,1)S(1)}, u32[]{:S(2)}, u32[]{:S(2)}) collective-permute-start(bf16[320,128]{1,0:T(8,128)(2,1)S(1)} %get-tuple-element.89.refs_2_.refs_3_), channel_id=1, source_target_pairs={{0,16},{4,20},{8,24},{12,28},{16,0},{20,4},{24,8},{28,12},{1,17},{... | collective-permute-start | bytes 245768 | tf_op jit(solution)/shard_map/ppermute | solution.py:593
  34.5 5.6 %collective-permute-start.15 = (bf16[320,128]{1,0:T(8,128)(2,1)S(1)}, bf16[320,128]{1,0:T(8,128)(2,1)S(1)}, u32[]{:S(2)}, u32[]{:S(2)}) collective-permute-start(bf16[320,128]{1,0:T(8,128)(2,1)S(1)} %shard_map.159.mine_ref), channel_id=1, source_target_pairs={{0,8},{4,12},{8,0},{12,4},{16,24},{20,28},{24,16},{28,20},{1,9},{5... | collective-permute-start | bytes 245768 | tf_op jit(solution)/shard_map/ppermute | solution.py:593
  37.7 5.4 %collective-permute-start.11 = (bf16[320,128]{1,0:T(8,128)(2,1)S(1)}, bf16[320,128]{1,0:T(8,128)(2,1)S(1)}, u32[]{:S(2)}, u32[]{:S(2)}) collective-permute-start(bf16[320,128]{1,0:T(8,128)(2,1)S(1)} %shard_map.156), channel_id=1, source_target_pairs={{0,8},{4,12},{8,0},{12,4},{16,24},{20,28},{24,16},{28,20},{1,9},{5... | collective-permute-start | bytes 245768 | tf_op jit(solution)/shard_map/ppermute | solution.py:593
  37.8 7.5 %collective-permute-start.13 = (bf16[128,512]{1,0:T(8,128)(2,1)S(1)}, bf16[128,512]{1,0:T(8,128)(2,1)S(1)}, u32[]{:S(2)}, u32[]{:S(2)}) collective-permute-start(bf16[128,512]{1,0:T(8,128)(2,1)S(1)} %get-tuple-element.100), channel_id=1, source_target_pairs={{4,0},{8,4},{12,8},{16,12},{20,16},{24,20},{28,24},{0,28},{5,1},{9... | collective-permute-start | bytes 393224 | tf_op jit(solution)/shard_map/ppermute | solution.py:679
  40.1 7.4 %collective-permute-start.16 = (bf16[320,128]{1,0:T(8,128)(2,1)S(1)}, bf16[320,128]{1,0:T(8,128)(2,1)S(1)}, u32[]{:S(2)}, u32[]{:S(2)}) collective-permute-start(bf16[320,128]{1,0:T(8,128)(2,1)S(1)} %shard_map.160), channel_id=1, source_target_pairs={{0,16},{4,20},{8,24},{12,28},{16,0},{20,4},{24,8},{28,12},{1,17},{... | collective-permute-start | bytes 245768 | tf_op jit(solution)/shard_map/ppermute | solution.py:593
  43.2 5.0 %collective-permute-start.12 = (bf16[320,128]{1,0:T(8,128)(2,1)S(1)}, bf16[320,128]{1,0:T(8,128)(2,1)S(1)}, u32[]{:S(2)}, u32[]{:S(2)}) collective-permute-start(bf16[320,128]{1,0:T(8,128)(2,1)S(1)} %shard_map.157), channel_id=1, source_target_pairs={{0,4},{4,0},{8,12},{12,8},{16,20},{20,16},{24,28},{28,24},{1,5},{5... | collective-permute-start | bytes 245768 | tf_op jit(solution)/shard_map/ppermute | solution.py:593

commit v4 on v3

--- a/solution.py
+++ b/solution.py
@@ -67,6 +67,12 @@
 
 def lane_sum(x):
     return jnp.sum(x, axis=1, keepdims=True)
+
+
+def row_sum(x):
+    ones = jnp.ones((8, x.shape[1]), BF16)
+    high, low = halves(x)
+    return mm_nt(ones, high) + mm_nt(ones, low)
 
 
 def span(h, size):
@@ -182,10 +188,11 @@
     feats = [feature_rows(key_ref[span(h, FEAT), :], sel) for h in range(heads)]
     norms = [mm_nt(ones, feat)[0:1] for feat in feats]
     copies[2].wait()
-    sums = [mm(feat, value_ref[:, span(h, HEAD_DIM)]) for h, feat in enumerate(feats)]
-    middles = [(state[CONST : CONST + 1] * (1.0 / length)).astype(BF16).astype(F32) for state in sums]
-    moved = [mm_tn(stack8(list(split(norm))), stack8([middle, middle])) for norm, middle in zip(norms, middles)]
-    tiles = [jnp.where(place == 5, middle, norm_tile(norm)) for norm, middle in zip(norms, middles)]
+    values = [value_ref[:, span(h, HEAD_DIM)] for h in range(heads)]
+    middles = [(jnp.sum(value.astype(F32), axis=0, keepdims=True) * (1.0 / length)).astype(BF16) for value in values]
+    sums = [mm(feat, value) for feat, value in zip(feats, values)]
+    moved = [mm(feat, jnp.broadcast_to(middle, value.shape)) for feat, middle, value in zip(feats, middles, values)]
+    tiles = [jnp.where(place == 5, middle.astype(F32), norm_tile(norm)) for norm, middle in zip(norms, middles)]
     per = heads // CHUNKS
     for h in range(heads):
         store_state(states[h // per], h % per, sums[h] - moved[h], tiles[h])
@@ -374,8 +381,8 @@
         outs[5][...] = squares
         outs[6][...] = crosses
     else:
-        stats = jnp.where(lane == 0, lane_sum(squares), jnp.where(lane == 1, lane_sum(crosses), 0.0))
-        outs[5][...] = jnp.transpose(stats)[:8]
+        place = iota((8, length), 0)
+        outs[5][...] = jnp.where(place == 0, row_sum(squares), jnp.where(place == 1, row_sum(crosses), 0.0))
 
 
 def grad_body(width, sources, *refs):
@@ -395,8 +402,8 @@
     inv_rms = 1.0 / jnp.sqrt(mean)
     pull = sums[:, 1:2] / (width * mean)
     lane = iota((length, 128), 1)
-    cols = jnp.where(lane == heads, inv_rms, 0.0)
-    grads, narrows = [], []
+    cols_ref[...] = jnp.where(lane == heads, inv_rms, 0.0)
+    grads, narrows, ratios = [], [], []
     for h in range(heads):
         chunk, local = h // per, span(h % per, HEAD_DIM)
         inverse = inverse_refs[chunk][:, h % per : h % per + 1]
@@ -404,16 +411,16 @@
         grad = (scaled_cot - merged_refs[chunk][:, local] * pull) * inv_rms
         grads.append(grad)
         narrows.append((grad * inverse).astype(BF16))
-        cols = jnp.where(lane == h, lane_sum(grad * linear_refs[chunk][:, local]) * inverse, cols)
+        ratios.append(row_sum(grad * linear_refs[chunk][:, local] * inverse)[0:1])
     feats = [feat_t_ref[span(h, ROWS), :] for h in range(heads)]
     sums = [mm(feat, narrow) for feat, narrow in zip(feats, narrows)]
-    ratios = jnp.transpose(cols)[:8]
-    norms = [mm_nt(stack8(list(split(ratios[h : h + 1]))), feats[h]) for h in range(heads)]
+    norms = [mm_nt(stack8(list(split(ratio))), feat) for ratio, feat in zip(ratios, feats)]
     for h in range(heads):
         store_state(terms[h // per], h % per, sums[h], norm_tile(norms[h][0:1] + norms[h][1:2]))
         grad_ref[:, span(h, HEAD_DIM)] = grads[h]
-    cols_ref[...] = cols
-    ratios_ref[...] = ratios
+    ratios_ref[...] = jnp.zeros(ratios_ref.shape, F32)
+    for h in range(heads):
+        ratios_ref[h : h + 1, :] = ratios[h]
 
 
 def window_back_body(wquery_ref, wkey_ref, value_ref, rim_ref, weights_ref, grad_ref, cols_ref, gain_ref, *refs):
@@ -449,7 +456,7 @@
         gv_ref[:, columns] = jnp.concatenate(value_sum, axis=0)
 
 
-def local_back_body(query_ref, key_ref, value_ref, sel_ref, sel_t_ref, rows_ref, grad_ref, cols_ref, ratios_ref, gv_in_ref, *refs):
+def local_back_body(query_ref, key_ref, value_ref, sel_ref, sel_t_ref, rows_ref, grad_ref, ratios_ref, gv_in_ref, *refs):
     inverse_refs, prefix_refs, norm_refs = refs[:CHUNKS], refs[CHUNKS : 2 * CHUNKS], refs[2 * CHUNKS : 3 * CHUNKS]
     gq_ref, gk_ref, gv_ref, feat_ref = refs[3 * CHUNKS :]
     length = value_ref.shape[0]
@@ -462,12 +469,13 @@
     keys = [key_ref[span(h, FEAT), :] for h in range(heads)]
     scaled = [grad_ref[:, span(h, HEAD_DIM)] * inverse_refs[h // per][:, h % per : h % per + 1] for h in range(heads)]
     parted = [halves(x) for x in scaled]
+    cols = jnp.transpose(jnp.concatenate([ratios_ref[...], jnp.zeros((120, length), F32)], axis=0))
     scores = [mm_tn(query, key) * SCORE for query, key in zip(queries, keys)]
     probs = [mm_nt(narrow, value_ref[:, span(h, HEAD_DIM)]) for h, (narrow, _) in enumerate(parted)]
     kernels = [jnp.where(causal, 1.0 + score + 0.5 * score * score, 0.0).astype(BF16) for score in scores]
     values = [mm_tn(kernel, narrow) for kernel, (narrow, _) in zip(kernels, parted)]
     dscores = [
-        jnp.where(causal, (probs[h] - cols_ref[:, h : h + 1]) * (1.0 + scores[h]), 0.0).astype(BF16) for h in range(heads)
+        jnp.where(causal, (probs[h] - cols[:, h : h + 1]) * (1.0 + scores[h]), 0.0).astype(BF16) for h in range(heads)
     ]
     by_query = [mm_nt(key, dscore) * SCORE for key, dscore in zip(keys, dscores)]
     by_key = [mm(query, dscore) * SCORE for query, dscore in zip(queries, dscores)]
@@ -683,7 +691,7 @@
     grad_query, key_part, value_part, featk = call(
         local_back_body,
         [(query_t.shape, BF16), (key_t.shape, F32), wide, ((heads, length, ROWS), BF16)],
-        query_v, key_v, value_v, sel, sel_t, rows, grad, cols, ratios, value_part, *inverse, *prefix, *norm,
+        query_v, key_v, value_v, sel, sel_t, rows, grad, ratios, value_part, *inverse, *prefix, *norm,
     )
     common = (key_v, value_v, sel, sel_t, featk, key_part, value_part, back)
     grad_key, grad_value, grad_wkey = call(

time: 49.7 us -> 49.4 us (level)
  no operation moved by 1% of the time
where the time goes in v4:
time: 49.4 us; the launch traced here: 49.3 us
  starting transfers between devices  24.3 us (49%)
  Pallas kernels  14.8 us (30%)
  waiting for transfers between devices  9.38 us (19%)
  between operations  0.75 us (2%)
    ppermute x12, starting transfers between devices, exchanged(): parts[c].append(lax.ppermute(held[c], 'seq', pairs))  19.7 us
    pallas_call x18, Pallas kernels, call(): pl.pallas_call(body if not ties else lambda *refs: body(*refs[:given], *r...  14.8 us
    ppermute x12, waiting for transfers between devices, exchanged(): parts[c].append(lax.ppermute(held[c], 'seq', pairs))  7.51 us
    ppermute x1, starting transfers between devices, middle(): lax.ppermute(back, 'seq', [((i + 1) % count, i) for i in range(count)])  2.2 us
    ppermute x3, starting transfers between devices, shards(): lax.ppermute(stats, 'head', [(i, i ^ s) for i in range(ring)])  1.89 us
    ppermute x3, waiting for transfers between devices, shards(): lax.ppermute(stats, 'head', [(i, i ^ s) for i in range(ring)])  1.86 us
  transfers between devices with their start and end apart: 17, of which 8 were waited for; matrix products, arithmetic and copies ran while one was open for 0% of the time, Pallas kernels for 20%

profile of v4, /device:TPU:0, one launch (start us, length us, event | category | flops | bytes accessed | tf_op | source)
XLA Modules:
  0.0 49.3 jit_solution(6771151677280891038)
XLA Ops:
  0.6 1.7 %shard_map.145 = (bf16[320,128]{1,0:T(8,128)(2,1)S(1)}, bf16[320,128]{1,0:T(8,128)(2,1)S(1)}, bf16[128,512]{1,0:T(8,128)(2,1)S(1)}, bf16[64,256]{1,0:T(8,128)(2,...) custom-call(bf16[64,256]{1,0:T(8,128)(2,1)} %bitcast.6, ...), custom_call_target="tpu_custom_call" | custom-call | tf_op jit(solution)/shard_map/pallas_call | solution.py:575
  2.4 3.0 %collective-permute-start.4 = (bf16[320,128]{1,0:T(8,128)(2,1)S(1)}, bf16[320,128]{1,0:T(8,128)(2,1)S(1)}, u32[]{:S(2)}, u32[]{:S(2)}) collective-permute-start(bf16[320,128]{1,0:T(8,128)(2,1)S(1)} %get-tuple-element.75.mine_ref), channel_id=1, source_target_pairs={{0,4},{4,0},{8,12},{12,8},{16,20},{20,16},{24,28},{28,24},{1,5},{5... | collective-permute-start | bytes 245768 | tf_op jit(solution)/shard_map/ppermute | solution.py:601
  5.4 2.6 %collective-permute-start.1 = (bf16[320,128]{1,0:T(8,128)(2,1)S(1)}, bf16[320,128]{1,0:T(8,128)(2,1)S(1)}, u32[]{:S(2)}, u32[]{:S(2)}) collective-permute-start(bf16[320,128]{1,0:T(8,128)(2,1)S(1)} %get-tuple-element.68.refs_2_.refs_3_), channel_id=1, source_target_pairs={{0,16},{4,20},{8,24},{12,28},{16,0},{20,4},{24,8},{28,12},{1,17},{... | collective-permute-start | bytes 245768 | tf_op jit(solution)/shard_map/ppermute | solution.py:601
  8.0 0.5 %collective-permute-start = (bf16[128,512]{1,0:T(8,128)(2,1)S(1)}, bf16[128,512]{1,0:T(8,128)(2,1)S(1)}, u32[]{:S(2)}, u32[]{:S(2)}) collective-permute-start(bf16[128,512]{1,0:T(8,128)(2,1)S(1)} %get-tuple-element.66), channel_id=1, source_target_pairs={{0,4},{4,8},{8,12},{12,16},{16,20},{20,24},{24,28},{28,0},{1,5},{5... | collective-permute-start | bytes 393224 | tf_op jit(solution)/shard_map/ppermute | solution.py:643
  8.5 0.0 collective-permute-done.4.theirs_ref.refs_1_
  8.5 0.2 shard_map.150.mine_ref
  8.7 1.6 %collective-permute-start.5 = (bf16[320,128]{1,0:T(8,128)(2,1)S(1)}, bf16[320,128]{1,0:T(8,128)(2,1)S(1)}, u32[]{:S(2)}, u32[]{:S(2)}) collective-permute-start(bf16[320,128]{1,0:T(8,128)(2,1)S(1)} %shard_map.150.mine_ref), channel_id=1, source_target_pairs={{0,8},{4,12},{8,0},{12,4},{16,24},{20,28},{24,16},{28,20},{1,9},{5... | collective-permute-start | bytes 245768 | tf_op jit(solution)/shard_map/ppermute | solution.py:601
  10.4 1.7 %shard_map.146 = (f32[256,512]{1,0:T(8,128)S(1)}, f32[256,128]{1,0:T(8,128)S(1)}, bf16[4,256,160]{2,1,0:T(8,128)(2,1)S(1)}, bf16[640,256]{1,0:T(8,128)(2,1)S(1)}...) custom-call(bf16[64,256]{1,0:T(8,128)(2,1)} %bitcast.7, ...), custom_call_target="tpu_custom_call" | custom-call | tf_op jit(solution)/shard_map/pallas_call | solution.py:575
  12.1 0.0 collective-permute-done.1.refs_1_
  12.1 0.2 shard_map.148
  12.4 0.5 %collective-permute-start.2 = (bf16[320,128]{1,0:T(8,128)(2,1)S(1)}, bf16[320,128]{1,0:T(8,128)(2,1)S(1)}, u32[]{:S(2)}, u32[]{:S(2)}) collective-permute-start(bf16[320,128]{1,0:T(8,128)(2,1)S(1)} %shard_map.148), channel_id=1, source_target_pairs={{0,8},{4,12},{8,0},{12,4},{16,24},{20,28},{24,16},{28,20},{1,9},{5... | collective-permute-start | bytes 245768 | tf_op jit(solution)/shard_map/ppermute | solution.py:601
  12.9 0.3 collective-permute-done.5.theirs_ref.refs_2_
  13.2 0.2 shard_map.151
  13.5 3.2 %collective-permute-start.6 = (bf16[320,128]{1,0:T(8,128)(2,1)S(1)}, bf16[320,128]{1,0:T(8,128)(2,1)S(1)}, u32[]{:S(2)}, u32[]{:S(2)}) collective-permute-start(bf16[320,128]{1,0:T(8,128)(2,1)S(1)} %shard_map.151), channel_id=1, source_target_pairs={{0,16},{4,20},{8,24},{12,28},{16,0},{20,4},{24,8},{28,12},{1,17},{... | collective-permute-start | bytes 245768 | tf_op jit(solution)/shard_map/ppermute | solution.py:601
  16.7 0.0 collective-permute-done.rim_ref.refs_4_
  16.7 0.6 %collective-permute-done.2.refs_2_ = bf16[320,128]{1,0:T(8,128)(2,1)S(1)} collective-permute-done((bf16[320,128]{1,0:T(8,128)(2,1)S(1)}, bf16[320,128]{1,0:T(8,128)(2,1)S(1)}, u32[]{:S(2)}, u32[]{:S(2)}) %collective-permute-start.2) | collective-permute-done | bytes 81952 | tf_op jit(solution)/shard_map/ppermute | solution.py:601
  17.3 0.2 shard_map.149
  17.5 2.0 %collective-permute-start.3 = (bf16[320,128]{1,0:T(8,128)(2,1)S(1)}, bf16[320,128]{1,0:T(8,128)(2,1)S(1)}, u32[]{:S(2)}, u32[]{:S(2)}) collective-permute-start(bf16[320,128]{1,0:T(8,128)(2,1)S(1)} %shard_map.149), channel_id=1, source_target_pairs={{0,4},{4,0},{8,12},{12,8},{16,20},{20,16},{24,28},{28,24},{1,5},{5... | collective-permute-start | bytes 245768 | tf_op jit(solution)/shard_map/ppermute | solution.py:601
  19.5 1.7 %shard_map.147 = (f32[256,512]{1,0:T(8,128)S(1)}, f32[4,256,128]{2,1,0:T(8,128)S(1)}, bf16[256,512]{1,0:T(8,128)(2,1)S(1)}, f32[1,512]{1,0:T(1,128)S(1)}) custom-call(s32[1]{0:T(128)} %bitcast.2.place_ref.refs_0_, bf16[256,512]{1,0:T(8,128)(2,1)} %cot_hbm.1, f32[1,512]{1,0:T(1,128)} %bitcast.8, bf16[256,512]{1,0:T(8,128)(2,1)S(1)} %get-tuple-element.64.wquery_ref, ...), custom_call_target="tpu_custom_call" | custom-call | tf_op jit(solution)/shard_map/pallas_call | solution.py:575
  21.2 0.0 collective-permute-done.6.refs_3_
  21.2 0.5 %shard_map.152 = (f32[256,256]{1,0:T(8,128)S(1)}, f32[256,256]{1,0:T(8,128)S(1)}, f32[256,128]{1,0:T(8,128)S(1)}, f32[320,128]{1,0:T(8,128)S(1)}, f32[16,160]{1,...) custom-call(s32[1]{0:T(128)} %bitcast.2.place_ref.refs_0_, ...), custom_call_target="tpu_custom_call" | custom-call | tf_op jit(solution)/shard_map/pallas_call | solution.py:575
  21.7 0.3 collective-permute-done.3.refs_3_
  22.0 0.7 %shard_map.153 = (f32[256,256]{1,0:T(8,128)S(1)}, f32[256,256]{1,0:T(8,128)S(1)}, f32[256,128]{1,0:T(8,128)S(1)}, f32[320,128]{1,0:T(8,128)S(1)}, f32[16,160]{1,0:T(8,128)S(1)}, /*index=5*/f32[8,256]{1,0:T(8,128)S(1)}) custom-call(s32[1]{0:T(128)} %bitcast.2.place_ref.refs_0_, bf16[320,128]{1,0:T(8,128)(2,1)S(1)} %collective-permute-done.1.refs_1_, ...), custom_call_target="tpu_custom_call" | custom-call | tf_op jit(solution)/shard_map/pallas_call | solution.py:575
  22.7 0.1 collective-permute-start.9
  22.8 1.5 %collective-permute-start.8 = (f32[8,256]{1,0:T(8,128)S(1)}, f32[8,256]{1,0:T(8,128)S(1)}, u32[]{:S(2)}, u32[]{:S(2)}) collective-permute-start(f32[8,256]{1,0:T(8,128)S(1)} %get-tuple-element.78.refs_0_), channel_id=1, source_target_pairs={{0,2},{1,3},{2,0},{3,1},{4,6},{5,7},{6,4},{7,5},{8,10},{9,11},{10,... | collective-permute-start | bytes 24584 | tf_op jit(solution)/shard_map/ppermute | solution.py:674
  24.3 0.3 collective-permute-start.7
  24.6 1.2 %collective-permute-done.9.refs_3_ = f32[8,256]{1,0:T(8,128)S(1)} collective-permute-done((f32[8,256]{1,0:T(8,128)S(1)}, f32[8,256]{1,0:T(8,128)S(1)}, u32[]{:S(2)}, u32[]{:S(2)}) %collective-permute-start.9) | collective-permute-done | bytes 8224 | tf_op jit(solution)/shard_map/ppermute | solution.py:674
  25.8 0.6 %collective-permute-done.8.refs_2_ = f32[8,256]{1,0:T(8,128)S(1)} collective-permute-done((f32[8,256]{1,0:T(8,128)S(1)}, f32[8,256]{1,0:T(8,128)S(1)}, u32[]{:S(2)}, u32[]{:S(2)}) %collective-permute-start.8) | collective-permute-done | bytes 8224 | tf_op jit(solution)/shard_map/ppermute | solution.py:674
  26.5 0.0 collective-permute-done.7.refs_1_
  26.5 0.9 %shard_map.154 = (bf16[320,128]{1,0:T(8,128)(2,1)S(1)}, bf16[320,128]{1,0:T(8,128)(2,1)S(1)}, f32[256,512]{1,0:T(8,128)S(1)}, f32[256,128]{1,0:T(8,128)S(1)}, f32[8,256]{1,0:T(8,128)S(1)}) custom-call(f32[8,256]{1,0:T(8,128)S(1)} %get-tuple-element.78.refs_0_, f32[8,256]{1,0:T(8,128)S(1)} %collective-permute-done.7.refs_1_, ...), custom_call_target="tpu_custom_call" | custom-call | tf_op jit(solution)/shard_map/pallas_call | solution.py:575
  27.4 2.8 %collective-permute-start.14 = (bf16[320,128]{1,0:T(8,128)(2,1)S(1)}, bf16[320,128]{1,0:T(8,128)(2,1)S(1)}, u32[]{:S(2)}, u32[]{:S(2)}) collective-permute-start(bf16[320,128]{1,0:T(8,128)(2,1)S(1)} %get-tuple-element.101.refs_0_), channel_id=1, source_target_pairs={{0,4},{4,0},{8,12},{12,8},{16,20},{20,16},{24,28},{28,24},{1,5},{5... | collective-permute-start | bytes 245768 | tf_op jit(solution)/shard_map/ppermute | solution.py:601
  30.2 1.7 %collective-permute-start.10 = (bf16[320,128]{1,0:T(8,128)(2,1)S(1)}, bf16[320,128]{1,0:T(8,128)(2,1)S(1)}, u32[]{:S(2)}, u32[]{:S(2)}) collective-permute-start(bf16[320,128]{1,0:T(8,128)(2,1)S(1)} %get-tuple-element.89.refs_2_.refs_3_), channel_id=1, source_target_pairs={{0,16},{4,20},{8,24},{12,28},{16,0},{20,4},{24,8},{28,12},{1,17},{... | collective-permute-start | bytes 245768 | tf_op jit(solution)/shard_map/ppermute | solution.py:601
  31.8 2.3 %shard_map.155 = (bf16[256,512]{1,0:T(8,128)(2,1)}, f32[256,512]{1,0:T(8,128)S(1)}, f32[256,512]{1,0:T(8,128)S(1)}, bf16[128,512]{1,0:T(8,128)(2,1)S(1)}, bf16[256,512]{1,0:T(8,128)(2,1)}) custom-call(bf16[256,512]{1,0:T(8,128)(2,1)S(1)} %get-tuple-element.64.wquery_ref, bf16[256,512]{1,0:T(8,128)(2,1)S(1)} %get-tuple-element.65.wkey_ref, ...), custom_call_target="tpu_custom_call" | custom-call | tf_op jit(solution)/shard_map/pallas_call | solution.py:575
  34.1 0.0 collective-permute-done.14.refs_1_
  34.2 1.1 %collective-permute-start.15 = (bf16[320,128]{1,0:T(8,128)(2,1)S(1)}, bf16[320,128]{1,0:T(8,128)(2,1)S(1)}, u32[]{:S(2)}, u32[]{:S(2)}) collective-permute-start(bf16[320,128]{1,0:T(8,128)(2,1)S(1)} %shard_map.159.mine_ref), channel_id=1, source_target_pairs={{0,8},{4,12},{8,0},{12,4},{16,24},{20,28},{24,16},{28,20},{1,9},{5... | collective-permute-start | bytes 245768 | tf_op jit(solution)/shard_map/ppermute | solution.py:601
  35.2 2.2 %collective-permute-done.10.refs_1_ = bf16[320,128]{1,0:T(8,128)(2,1)S(1)} collective-permute-done((bf16[320,128]{1,0:T(8,128)(2,1)S(1)}, bf16[320,128]{1,0:T(8,128)(2,1)S(1)}, u32[]{:S(2)}, u32[]{:S(2)}) %collective-permute-start.10) | collective-permute-done | bytes 81952 | tf_op jit(solution)/shard_map/ppermute | solution.py:601
  37.5 0.1 collective-permute-start.11
  37.5 2.2 %collective-permute-start.13 = (bf16[128,512]{1,0:T(8,128)(2,1)S(1)}, bf16[128,512]{1,0:T(8,128)(2,1)S(1)}, u32[]{:S(2)}, u32[]{:S(2)}) collective-permute-start(bf16[128,512]{1,0:T(8,128)(2,1)S(1)} %get-tuple-element.100), channel_id=1, source_target_pairs={{4,0},{8,4},{12,8},{16,12},{20,16},{24,20},{28,24},{0,28},{5,1},{9... | collective-permute-start | bytes 393224 | tf_op jit(solution)/shard_map/ppermute | solution.py:687
  39.7 0.0 collective-permute-done.15.theirs_ref.refs_2_
  39.8 1.1 %collective-permute-start.16 = (bf16[320,128]{1,0:T(8,128)(2,1)S(1)}, bf16[320,128]{1,0:T(8,128)(2,1)S(1)}, u32[]{:S(2)}, u32[]{:S(2)}) collective-permute-start(bf16[320,128]{1,0:T(8,128)(2,1)S(1)} %shard_map.160), channel_id=1, source_target_pairs={{0,16},{4,20},{8,24},{12,28},{16,0},{20,4},{24,8},{28,12},{1,17},{... | collective-permute-start | bytes 245768 | tf_op jit(solution)/shard_map/ppermute | solution.py:601
  40.9 2.0 %collective-permute-done.11.refs_2_ = bf16[320,128]{1,0:T(8,128)(2,1)S(1)} collective-permute-done((bf16[320,128]{1,0:T(8,128)(2,1)S(1)}, bf16[320,128]{1,0:T(8,128)(2,1)S(1)}, u32[]{:S(2)}, u32[]{:S(2)}) %collective-permute-start.11) | collective-permute-done | bytes 81952 | tf_op jit(solution)/shard_map/ppermute | solution.py:601
  42.9 0.1 shard_map.157
  42.9 0.1 collective-permute-start.12
  43.0 2.1 %shard_map.158 = (bf16[64,256]{1,0:T(8,128)(2,1)S(1)}, f32[64,256]{1,0:T(8,128)S(1)}, f32[256,512]{1,0:T(8,128)S(1)}, bf16[4,256,160]{2,1,0:T(8,128)(2,1)S(1)}) custom-call(bf16[64,256]{1,0:T(8,128)(2,1)S(1)} %get-tuple-element.90.query_ref, bf16[64,256]{1,0:T(8,128)(2,1)S(1)} %get-tuple-element.59.key_ref.refs_4_, ...), custom_call_target="tpu_custom_call" | custom-call | tf_op jit(solution)/shard_map/pallas_call | solution.py:575
  45.1 0.0 collective-permute-done.13.refs_11_
  45.1 2.1 %collective-permute-done.16.refs_3_ = bf16[320,128]{1,0:T(8,128)(2,1)S(1)} collective-permute-done((bf16[320,128]{1,0:T(8,128)(2,1)S(1)}, bf16[320,128]{1,0:T(8,128)(2,1)S(1)}, u32[]{:S(2)}, u32[]{:S(2)}) %collective-permute-start.16) | collective-permute-done | bytes 81952 | tf_op jit(solution)/shard_map/ppermute | solution.py:601
  47.2 0.7 %shard_map.161 = (bf16[32,256]{1,0:T(8,128)(2,1)S(1)}, bf16[256,256]{1,0:T(8,128)(2,1)S(1)}, bf16[256,512]{1,0:T(8,128)(2,1)S(1)}) custom-call(s32[1]{0:T(128)} %bitcast.2.place_ref.refs_0_, bf16[320,128]{1,0:T(8,128)(2,1)S(1)} %collective-permute-done.14.refs_1_, bf16[320,128]{1,0:T(8,128)(2,1)S(1)} %collective-permute-done.15.theirs_ref.refs_2_, ...), custom_call_target="tpu_custom_call" | custom-call | tf_op jit(solution)/shard_map/pallas_call | solution.py:575
  47.9 0.0 collective-permute-done.12.refs_3_
  47.9 1.4 %shard_map.162 = (bf16[256,512]{1,0:T(8,128)(2,1)}, bf16[64,256]{1,0:T(8,128)(2,1)}, bf16[64,256]{1,0:T(8,128)(2,1)}, bf16[256,512]{1,0:T(8,128)(2,1)}) custom-call(s32[1]{0:T(128)} %bitcast.2.place_ref.refs_0_, bf16[320,128]{1,0:T(8,128)(2,1)S(1)} %collective-permute-done.10.refs_1_, bf16[320,128]{1,0:T(8,128)(2,1)S(1)} %collective-permute-done.11.refs_2_, ...), custom_call_target="tpu_custom_call" | custom-call | tf_op jit(solution)/shard_map/pallas_call | solution.py:575
  (3 shorter events, 0.1 us)
Async XLA Ops:
  2.4 6.1 %collective-permute-start.4 = (bf16[320,128]{1,0:T(8,128)(2,1)S(1)}, bf16[320,128]{1,0:T(8,128)(2,1)S(1)}, u32[]{:S(2)}, u32[]{:S(2)}) collective-permute-start(bf16[320,128]{1,0:T(8,128)(2,1)S(1)} %get-tuple-element.75.mine_ref), channel_id=1, source_target_pairs={{0,4},{4,0},{8,12},{12,8},{16,20},{20,16},{24,28},{28,24},{1,5},{5... | collective-permute-start | bytes 245768 | tf_op jit(solution)/shard_map/ppermute | solution.py:601
  5.4 6.7 %collective-permute-start.1 = (bf16[320,128]{1,0:T(8,128)(2,1)S(1)}, bf16[320,128]{1,0:T(8,128)(2,1)S(1)}, u32[]{:S(2)}, u32[]{:S(2)}) collective-permute-start(bf16[320,128]{1,0:T(8,128)(2,1)S(1)} %get-tuple-element.68.refs_2_.refs_3_), channel_id=1, source_target_pairs={{0,16},{4,20},{8,24},{12,28},{16,0},{20,4},{24,8},{28,12},{1,17},{... | collective-permute-start | bytes 245768 | tf_op jit(solution)/shard_map/ppermute | solution.py:601
  8.0 8.7 %collective-permute-start = (bf16[128,512]{1,0:T(8,128)(2,1)S(1)}, bf16[128,512]{1,0:T(8,128)(2,1)S(1)}, u32[]{:S(2)}, u32[]{:S(2)}) collective-permute-start(bf16[128,512]{1,0:T(8,128)(2,1)S(1)} %get-tuple-element.66), channel_id=1, source_target_pairs={{0,4},{4,8},{8,12},{12,16},{16,20},{20,24},{24,28},{28,0},{1,5},{5... | collective-permute-start | bytes 393224 | tf_op jit(solution)/shard_map/ppermute | solution.py:643
  8.7 4.5 %collective-permute-start.5 = (bf16[320,128]{1,0:T(8,128)(2,1)S(1)}, bf16[320,128]{1,0:T(8,128)(2,1)S(1)}, u32[]{:S(2)}, u32[]{:S(2)}) collective-permute-start(bf16[320,128]{1,0:T(8,128)(2,1)S(1)} %shard_map.150.mine_ref), channel_id=1, source_target_pairs={{0,8},{4,12},{8,0},{12,4},{16,24},{20,28},{24,16},{28,20},{1,9},{5... | collective-permute-start | bytes 245768 | tf_op jit(solution)/shard_map/ppermute | solution.py:601
  12.4 4.9 %collective-permute-start.2 = (bf16[320,128]{1,0:T(8,128)(2,1)S(1)}, bf16[320,128]{1,0:T(8,128)(2,1)S(1)}, u32[]{:S(2)}, u32[]{:S(2)}) collective-permute-start(bf16[320,128]{1,0:T(8,128)(2,1)S(1)} %shard_map.148), channel_id=1, source_target_pairs={{0,8},{4,12},{8,0},{12,4},{16,24},{20,28},{24,16},{28,20},{1,9},{5... | collective-permute-start | bytes 245768 | tf_op jit(solution)/shard_map/ppermute | solution.py:601
  13.5 7.7 %collective-permute-start.6 = (bf16[320,128]{1,0:T(8,128)(2,1)S(1)}, bf16[320,128]{1,0:T(8,128)(2,1)S(1)}, u32[]{:S(2)}, u32[]{:S(2)}) collective-permute-start(bf16[320,128]{1,0:T(8,128)(2,1)S(1)} %shard_map.151), channel_id=1, source_target_pairs={{0,16},{4,20},{8,24},{12,28},{16,0},{20,4},{24,8},{28,12},{1,17},{... | collective-permute-start | bytes 245768 | tf_op jit(solution)/shard_map/ppermute | solution.py:601
  17.5 4.5 %collective-permute-start.3 = (bf16[320,128]{1,0:T(8,128)(2,1)S(1)}, bf16[320,128]{1,0:T(8,128)(2,1)S(1)}, u32[]{:S(2)}, u32[]{:S(2)}) collective-permute-start(bf16[320,128]{1,0:T(8,128)(2,1)S(1)} %shard_map.149), channel_id=1, source_target_pairs={{0,4},{4,0},{8,12},{12,8},{16,20},{20,16},{24,28},{28,24},{1,5},{5... | collective-permute-start | bytes 245768 | tf_op jit(solution)/shard_map/ppermute | solution.py:601
  22.7 3.1 %collective-permute-start.9 = (f32[8,256]{1,0:T(8,128)S(1)}, f32[8,256]{1,0:T(8,128)S(1)}, u32[]{:S(2)}, u32[]{:S(2)}) collective-permute-start(f32[8,256]{1,0:T(8,128)S(1)} %get-tuple-element.78.refs_0_), channel_id=1, source_target_pairs={{0,3},{1,2},{2,1},{3,0},{4,7},{5,6},{6,5},{7,4},{8,11},{9,10},{10,... | collective-permute-start | bytes 24584 | tf_op jit(solution)/shard_map/ppermute | solution.py:674
  22.8 3.7 %collective-permute-start.8 = (f32[8,256]{1,0:T(8,128)S(1)}, f32[8,256]{1,0:T(8,128)S(1)}, u32[]{:S(2)}, u32[]{:S(2)}) collective-permute-start(f32[8,256]{1,0:T(8,128)S(1)} %get-tuple-element.78.refs_0_), channel_id=1, source_target_pairs={{0,2},{1,3},{2,0},{3,1},{4,6},{5,7},{6,4},{7,5},{8,10},{9,11},{10,... | collective-permute-start | bytes 24584 | tf_op jit(solution)/shard_map/ppermute | solution.py:674
  24.3 2.2 %collective-permute-start.7 = (f32[8,256]{1,0:T(8,128)S(1)}, f32[8,256]{1,0:T(8,128)S(1)}, u32[]{:S(2)}, u32[]{:S(2)}) collective-permute-start(f32[8,256]{1,0:T(8,128)S(1)} %get-tuple-element.78.refs_0_), channel_id=1, source_target_pairs={{0,1},{1,0},{2,3},{3,2},{4,5},{5,4},{6,7},{7,6},{8,9},{9,8},{10,11... | collective-permute-start | bytes 24584 | tf_op jit(solution)/shard_map/ppermute | solution.py:674
  27.4 6.7 %collective-permute-start.14 = (bf16[320,128]{1,0:T(8,128)(2,1)S(1)}, bf16[320,128]{1,0:T(8,128)(2,1)S(1)}, u32[]{:S(2)}, u32[]{:S(2)}) collective-permute-start(bf16[320,128]{1,0:T(8,128)(2,1)S(1)} %get-tuple-element.101.refs_0_), channel_id=1, source_target_pairs={{0,4},{4,0},{8,12},{12,8},{16,20},{20,16},{24,28},{28,24},{1,5},{5... | collective-permute-start | bytes 245768 | tf_op jit(solution)/shard_map/ppermute | solution.py:601
  30.2 7.2 %collective-permute-start.10 = (bf16[320,128]{1,0:T(8,128)(2,1)S(1)}, bf16[320,128]{1,0:T(8,128)(2,1)S(1)}, u32[]{:S(2)}, u32[]{:S(2)}) collective-permute-start(bf16[320,128]{1,0:T(8,128)(2,1)S(1)} %get-tuple-element.89.refs_2_.refs_3_), channel_id=1, source_target_pairs={{0,16},{4,20},{8,24},{12,28},{16,0},{20,4},{24,8},{28,12},{1,17},{... | collective-permute-start | bytes 245768 | tf_op jit(solution)/shard_map/ppermute | solution.py:601
  34.2 5.6 %collective-permute-start.15 = (bf16[320,128]{1,0:T(8,128)(2,1)S(1)}, bf16[320,128]{1,0:T(8,128)(2,1)S(1)}, u32[]{:S(2)}, u32[]{:S(2)}) collective-permute-start(bf16[320,128]{1,0:T(8,128)(2,1)S(1)} %shard_map.159.mine_ref), channel_id=1, source_target_pairs={{0,8},{4,12},{8,0},{12,4},{16,24},{20,28},{24,16},{28,20},{1,9},{5... | collective-permute-start | bytes 245768 | tf_op jit(solution)/shard_map/ppermute | solution.py:601
  37.5 5.4 %collective-permute-start.11 = (bf16[320,128]{1,0:T(8,128)(2,1)S(1)}, bf16[320,128]{1,0:T(8,128)(2,1)S(1)}, u32[]{:S(2)}, u32[]{:S(2)}) collective-permute-start(bf16[320,128]{1,0:T(8,128)(2,1)S(1)} %shard_map.156), channel_id=1, source_target_pairs={{0,8},{4,12},{8,0},{12,4},{16,24},{20,28},{24,16},{28,20},{1,9},{5... | collective-permute-start | bytes 245768 | tf_op jit(solution)/shard_map/ppermute | solution.py:601
  37.5 7.6 %collective-permute-start.13 = (bf16[128,512]{1,0:T(8,128)(2,1)S(1)}, bf16[128,512]{1,0:T(8,128)(2,1)S(1)}, u32[]{:S(2)}, u32[]{:S(2)}) collective-permute-start(bf16[128,512]{1,0:T(8,128)(2,1)S(1)} %get-tuple-element.100), channel_id=1, source_target_pairs={{4,0},{8,4},{12,8},{16,12},{20,16},{24,20},{28,24},{0,28},{5,1},{9... | collective-permute-start | bytes 393224 | tf_op jit(solution)/shard_map/ppermute | solution.py:687
  39.8 7.5 %collective-permute-start.16 = (bf16[320,128]{1,0:T(8,128)(2,1)S(1)}, bf16[320,128]{1,0:T(8,128)(2,1)S(1)}, u32[]{:S(2)}, u32[]{:S(2)}) collective-permute-start(bf16[320,128]{1,0:T(8,128)(2,1)S(1)} %shard_map.160), channel_id=1, source_target_pairs={{0,16},{4,20},{8,24},{12,28},{16,0},{20,4},{24,8},{28,12},{1,17},{... | collective-permute-start | bytes 245768 | tf_op jit(solution)/shard_map/ppermute | solution.py:601
  42.9 5.0 %collective-permute-start.12 = (bf16[320,128]{1,0:T(8,128)(2,1)S(1)}, bf16[320,128]{1,0:T(8,128)(2,1)S(1)}, u32[]{:S(2)}, u32[]{:S(2)}) collective-permute-start(bf16[320,128]{1,0:T(8,128)(2,1)S(1)} %shard_map.157), channel_id=1, source_target_pairs={{0,4},{4,0},{8,12},{12,8},{16,20},{20,16},{24,28},{28,24},{1,5},{5... | collective-permute-start | bytes 245768 | tf_op jit(solution)/shard_map/ppermute | solution.py:601

commit v5 on v4

--- a/solution.py
+++ b/solution.py
@@ -671,7 +671,7 @@
         before = out[5:]
     (stats,) = before
     ring = lax.axis_size("head")
-    stats = [stats] + [lax.ppermute(stats, "head", [(i, i ^ s) for i in range(ring)]) for s in range(1, ring)]
+    stats = [stats] + [lax.ppermute(stats, "head", [(i, (i + s) % ring) for i in range(ring)]) for s in range(1, ring)]
     *terms, grad, cols, ratios = call(
         lambda *refs: grad_body(float(full_width), ring, *refs),
         [state_shape] * CHUNKS + [wide, square, ((8, length), F32)],

time: 49.4 us -> 49 us (level)
  waiting for transfers between devices: 9.38 us -> 8.3 us
  starting transfers between devices: 24.3 us -> 25 us
    ppermute x12, waiting for transfers between devices: 7.51 us -> 5.45 us  [exchanged(): parts[c].append(lax.ppermute(held[c], 'seq', pairs))]
    ppermute x3, waiting for transfers between devices: 1.86 us -> 2.85 us  [shards(): lax.ppermute(stats, 'head', [(i, (i + s) % ring) for i in range(ring)])]
    ppermute x12, starting transfers between devices: 19.7 us -> 20.6 us  [exchanged(): parts[c].append(lax.ppermute(held[c], 'seq', pairs))]
  transfers between devices with their start and end apart: 17 -> 17, of which waited for: 8 -> 9; matrix products, arithmetic and copies ran while one was open for 0% -> 0% of each run, Pallas kernels for 20% -> 21%
where the time goes in v5:
time: 49 us; the launch traced here: 48.8 us
  starting transfers between devices  25 us (51%)
  Pallas kernels  14.8 us (30%)
  waiting for transfers between devices  8.3 us (17%)
  between operations  0.74 us (2%)
    ppermute x12, starting transfers between devices, exchanged(): parts[c].append(lax.ppermute(held[c], 'seq', pairs))  20.6 us
    pallas_call x18, Pallas kernels, call(): pl.pallas_call(body if not ties else lambda *refs: body(*refs[:given], *r...  14.8 us
    ppermute x12, waiting for transfers between devices, exchanged(): parts[c].append(lax.ppermute(held[c], 'seq', pairs))  5.45 us
    ppermute x3, waiting for transfers between devices, shards(): lax.ppermute(stats, 'head', [(i, (i + s) % ring) for i in range(ring)])  2.85 us
    ppermute x1, starting transfers between devices, middle(): lax.ppermute(back, 'seq', [((i + 1) % count, i) for i in range(count)])  2.07 us
    ppermute x3, starting transfers between devices, shards(): lax.ppermute(stats, 'head', [(i, (i + s) % ring) for i in range(ring)])  1.78 us
  transfers between devices with their start and end apart: 17, of which 9 were waited for; matrix products, arithmetic and copies ran while one was open for 0% of the time, Pallas kernels for 21%

profile of v5, /device:TPU:0, one launch (start us, length us, event | category | flops | bytes accessed | tf_op | source)
XLA Modules:
  0.0 48.8 jit_solution(6837459684130942569)
XLA Ops:
  0.6 1.7 %shard_map.145 = (bf16[320,128]{1,0:T(8,128)(2,1)S(1)}, bf16[320,128]{1,0:T(8,128)(2,1)S(1)}, bf16[128,512]{1,0:T(8,128)(2,1)S(1)}, bf16[64,256]{1,0:T(8,128)(2,...) custom-call(bf16[64,256]{1,0:T(8,128)(2,1)} %bitcast.6, ...), custom_call_target="tpu_custom_call" | custom-call | tf_op jit(solution)/shard_map/pallas_call | solution.py:575
  2.4 3.0 %collective-permute-start.4 = (bf16[320,128]{1,0:T(8,128)(2,1)S(1)}, bf16[320,128]{1,0:T(8,128)(2,1)S(1)}, u32[]{:S(2)}, u32[]{:S(2)}) collective-permute-start(bf16[320,128]{1,0:T(8,128)(2,1)S(1)} %get-tuple-element.75.mine_ref), channel_id=1, source_target_pairs={{0,4},{4,0},{8,12},{12,8},{16,20},{20,16},{24,28},{28,24},{1,5},{5... | collective-permute-start | bytes 245768 | tf_op jit(solution)/shard_map/ppermute | solution.py:601
  5.4 2.6 %collective-permute-start.1 = (bf16[320,128]{1,0:T(8,128)(2,1)S(1)}, bf16[320,128]{1,0:T(8,128)(2,1)S(1)}, u32[]{:S(2)}, u32[]{:S(2)}) collective-permute-start(bf16[320,128]{1,0:T(8,128)(2,1)S(1)} %get-tuple-element.68.refs_2_.refs_3_), channel_id=1, source_target_pairs={{0,16},{4,20},{8,24},{12,28},{16,0},{20,4},{24,8},{28,12},{1,17},{... | collective-permute-start | bytes 245768 | tf_op jit(solution)/shard_map/ppermute | solution.py:601
  8.0 0.5 %collective-permute-start = (bf16[128,512]{1,0:T(8,128)(2,1)S(1)}, bf16[128,512]{1,0:T(8,128)(2,1)S(1)}, u32[]{:S(2)}, u32[]{:S(2)}) collective-permute-start(bf16[128,512]{1,0:T(8,128)(2,1)S(1)} %get-tuple-element.66), channel_id=1, source_target_pairs={{0,4},{4,8},{8,12},{12,16},{16,20},{20,24},{24,28},{28,0},{1,5},{5... | collective-permute-start | bytes 393224 | tf_op jit(solution)/shard_map/ppermute | solution.py:643
  8.5 0.0 collective-permute-done.4.theirs_ref.refs_1_
  8.5 0.2 shard_map.150.mine_ref
  8.7 1.6 %collective-permute-start.5 = (bf16[320,128]{1,0:T(8,128)(2,1)S(1)}, bf16[320,128]{1,0:T(8,128)(2,1)S(1)}, u32[]{:S(2)}, u32[]{:S(2)}) collective-permute-start(bf16[320,128]{1,0:T(8,128)(2,1)S(1)} %shard_map.150.mine_ref), channel_id=1, source_target_pairs={{0,8},{4,12},{8,0},{12,4},{16,24},{20,28},{24,16},{28,20},{1,9},{5... | collective-permute-start | bytes 245768 | tf_op jit(solution)/shard_map/ppermute | solution.py:601
  10.4 1.7 %shard_map.146 = (f32[256,512]{1,0:T(8,128)S(1)}, f32[256,128]{1,0:T(8,128)S(1)}, bf16[4,256,160]{2,1,0:T(8,128)(2,1)S(1)}, bf16[640,256]{1,0:T(8,128)(2,1)S(1)}...) custom-call(bf16[64,256]{1,0:T(8,128)(2,1)} %bitcast.7, ...), custom_call_target="tpu_custom_call" | custom-call | tf_op jit(solution)/shard_map/pallas_call | solution.py:575
  12.1 0.0 collective-permute-done.1.refs_1_
  12.1 0.2 shard_map.148
  12.4 0.5 %collective-permute-start.2 = (bf16[320,128]{1,0:T(8,128)(2,1)S(1)}, bf16[320,128]{1,0:T(8,128)(2,1)S(1)}, u32[]{:S(2)}, u32[]{:S(2)}) collective-permute-start(bf16[320,128]{1,0:T(8,128)(2,1)S(1)} %shard_map.148), channel_id=1, source_target_pairs={{0,8},{4,12},{8,0},{12,4},{16,24},{20,28},{24,16},{28,20},{1,9},{5... | collective-permute-start | bytes 245768 | tf_op jit(solution)/shard_map/ppermute | solution.py:601
  12.9 0.3 collective-permute-done.5.theirs_ref.refs_2_
  13.2 0.2 shard_map.151
  13.5 3.2 %collective-permute-start.6 = (bf16[320,128]{1,0:T(8,128)(2,1)S(1)}, bf16[320,128]{1,0:T(8,128)(2,1)S(1)}, u32[]{:S(2)}, u32[]{:S(2)}) collective-permute-start(bf16[320,128]{1,0:T(8,128)(2,1)S(1)} %shard_map.151), channel_id=1, source_target_pairs={{0,16},{4,20},{8,24},{12,28},{16,0},{20,4},{24,8},{28,12},{1,17},{... | collective-permute-start | bytes 245768 | tf_op jit(solution)/shard_map/ppermute | solution.py:601
  16.7 0.0 collective-permute-done.rim_ref.refs_4_
  16.7 0.6 %collective-permute-done.2.refs_2_ = bf16[320,128]{1,0:T(8,128)(2,1)S(1)} collective-permute-done((bf16[320,128]{1,0:T(8,128)(2,1)S(1)}, bf16[320,128]{1,0:T(8,128)(2,1)S(1)}, u32[]{:S(2)}, u32[]{:S(2)}) %collective-permute-start.2) | collective-permute-done | bytes 81952 | tf_op jit(solution)/shard_map/ppermute | solution.py:601
  17.3 0.2 shard_map.149
  17.5 2.0 %collective-permute-start.3 = (bf16[320,128]{1,0:T(8,128)(2,1)S(1)}, bf16[320,128]{1,0:T(8,128)(2,1)S(1)}, u32[]{:S(2)}, u32[]{:S(2)}) collective-permute-start(bf16[320,128]{1,0:T(8,128)(2,1)S(1)} %shard_map.149), channel_id=1, source_target_pairs={{0,4},{4,0},{8,12},{12,8},{16,20},{20,16},{24,28},{28,24},{1,5},{5... | collective-permute-start | bytes 245768 | tf_op jit(solution)/shard_map/ppermute | solution.py:601
  19.5 1.7 %shard_map.147 = (f32[256,512]{1,0:T(8,128)S(1)}, f32[4,256,128]{2,1,0:T(8,128)S(1)}, bf16[256,512]{1,0:T(8,128)(2,1)S(1)}, f32[1,512]{1,0:T(1,128)S(1)}) custom-call(s32[1]{0:T(128)} %bitcast.2.place_ref.refs_0_, bf16[256,512]{1,0:T(8,128)(2,1)} %cot_hbm.1, f32[1,512]{1,0:T(1,128)} %bitcast.8, bf16[256,512]{1,0:T(8,128)(2,1)S(1)} %get-tuple-element.64.wquery_ref, ...), custom_call_target="tpu_custom_call" | custom-call | tf_op jit(solution)/shard_map/pallas_call | solution.py:575
  21.2 0.0 collective-permute-done.6.refs_3_
  21.2 0.5 %shard_map.152 = (f32[256,256]{1,0:T(8,128)S(1)}, f32[256,256]{1,0:T(8,128)S(1)}, f32[256,128]{1,0:T(8,128)S(1)}, f32[320,128]{1,0:T(8,128)S(1)}, f32[16,160]{1,...) custom-call(s32[1]{0:T(128)} %bitcast.2.place_ref.refs_0_, ...), custom_call_target="tpu_custom_call" | custom-call | tf_op jit(solution)/shard_map/pallas_call | solution.py:575
  21.7 0.3 collective-permute-done.3.refs_3_
  22.0 0.7 %shard_map.153 = (f32[256,256]{1,0:T(8,128)S(1)}, f32[256,256]{1,0:T(8,128)S(1)}, f32[256,128]{1,0:T(8,128)S(1)}, f32[320,128]{1,0:T(8,128)S(1)}, f32[16,160]{1,0:T(8,128)S(1)}, /*index=5*/f32[8,256]{1,0:T(8,128)S(1)}) custom-call(s32[1]{0:T(128)} %bitcast.2.place_ref.refs_0_, bf16[320,128]{1,0:T(8,128)(2,1)S(1)} %collective-permute-done.1.refs_1_, ...), custom_call_target="tpu_custom_call" | custom-call | tf_op jit(solution)/shard_map/pallas_call | solution.py:575
  22.7 0.1 collective-permute-start.9
  22.8 1.5 %collective-permute-start.8 = (f32[8,256]{1,0:T(8,128)S(1)}, f32[8,256]{1,0:T(8,128)S(1)}, u32[]{:S(2)}, u32[]{:S(2)}) collective-permute-start(f32[8,256]{1,0:T(8,128)S(1)} %get-tuple-element.78.refs_0_), channel_id=1, source_target_pairs={{0,2},{1,3},{2,0},{3,1},{4,6},{5,7},{6,4},{7,5},{8,10},{9,11},{10,... | collective-permute-start | bytes 24584 | tf_op jit(solution)/shard_map/ppermute | solution.py:674
  24.3 0.2 collective-permute-start.7
  24.5 0.0 collective-permute-done.9.refs_3_
  24.5 2.0 %collective-permute-done.8.refs_2_ = f32[8,256]{1,0:T(8,128)S(1)} collective-permute-done((f32[8,256]{1,0:T(8,128)S(1)}, f32[8,256]{1,0:T(8,128)S(1)}, u32[]{:S(2)}, u32[]{:S(2)}) %collective-permute-start.8) | collective-permute-done | bytes 8224 | tf_op jit(solution)/shard_map/ppermute | solution.py:674
  26.5 0.9 %collective-permute-done.7.refs_1_ = f32[8,256]{1,0:T(8,128)S(1)} collective-permute-done((f32[8,256]{1,0:T(8,128)S(1)}, f32[8,256]{1,0:T(8,128)S(1)}, u32[]{:S(2)}, u32[]{:S(2)}) %collective-permute-start.7) | collective-permute-done | bytes 8224 | tf_op jit(solution)/shard_map/ppermute | solution.py:674
  27.4 0.9 %shard_map.154 = (bf16[320,128]{1,0:T(8,128)(2,1)S(1)}, bf16[320,128]{1,0:T(8,128)(2,1)S(1)}, f32[256,512]{1,0:T(8,128)S(1)}, f32[256,128]{1,0:T(8,128)S(1)}, f32[8,256]{1,0:T(8,128)S(1)}) custom-call(f32[8,256]{1,0:T(8,128)S(1)} %get-tuple-element.78.refs_0_, f32[8,256]{1,0:T(8,128)S(1)} %collective-permute-done.7.refs_1_, ...), custom_call_target="tpu_custom_call" | custom-call | tf_op jit(solution)/shard_map/pallas_call | solution.py:575
  28.3 2.8 %collective-permute-start.14 = (bf16[320,128]{1,0:T(8,128)(2,1)S(1)}, bf16[320,128]{1,0:T(8,128)(2,1)S(1)}, u32[]{:S(2)}, u32[]{:S(2)}) collective-permute-start(bf16[320,128]{1,0:T(8,128)(2,1)S(1)} %get-tuple-element.101.refs_0_), channel_id=1, source_target_pairs={{0,4},{4,0},{8,12},{12,8},{16,20},{20,16},{24,28},{28,24},{1,5},{5... | collective-permute-start | bytes 245768 | tf_op jit(solution)/shard_map/ppermute | solution.py:601
  31.1 1.7 %collective-permute-start.10 = (bf16[320,128]{1,0:T(8,128)(2,1)S(1)}, bf16[320,128]{1,0:T(8,128)(2,1)S(1)}, u32[]{:S(2)}, u32[]{:S(2)}) collective-permute-start(bf16[320,128]{1,0:T(8,128)(2,1)S(1)} %get-tuple-element.89.refs_2_.refs_3_), channel_id=1, source_target_pairs={{0,16},{4,20},{8,24},{12,28},{16,0},{20,4},{24,8},{28,12},{1,17},{... | collective-permute-start | bytes 245768 | tf_op jit(solution)/shard_map/ppermute | solution.py:601
  32.7 2.3 %shard_map.155 = (bf16[256,512]{1,0:T(8,128)(2,1)}, f32[256,512]{1,0:T(8,128)S(1)}, f32[256,512]{1,0:T(8,128)S(1)}, bf16[128,512]{1,0:T(8,128)(2,1)S(1)}, bf16[256,512]{1,0:T(8,128)(2,1)}) custom-call(bf16[256,512]{1,0:T(8,128)(2,1)S(1)} %get-tuple-element.64.wquery_ref, bf16[256,512]{1,0:T(8,128)(2,1)S(1)} %get-tuple-element.65.wkey_ref, ...), custom_call_target="tpu_custom_call" | custom-call | tf_op jit(solution)/shard_map/pallas_call | solution.py:575
  35.0 0.0 collective-permute-done.14.refs_1_
  35.1 1.1 %collective-permute-start.15 = (bf16[320,128]{1,0:T(8,128)(2,1)S(1)}, bf16[320,128]{1,0:T(8,128)(2,1)S(1)}, u32[]{:S(2)}, u32[]{:S(2)}) collective-permute-start(bf16[320,128]{1,0:T(8,128)(2,1)S(1)} %shard_map.159.mine_ref), channel_id=1, source_target_pairs={{0,8},{4,12},{8,0},{12,4},{16,24},{20,28},{24,16},{28,20},{1,9},{5... | collective-permute-start | bytes 245768 | tf_op jit(solution)/shard_map/ppermute | solution.py:601
  36.2 1.2 %collective-permute-done.10.refs_1_ = bf16[320,128]{1,0:T(8,128)(2,1)S(1)} collective-permute-done((bf16[320,128]{1,0:T(8,128)(2,1)S(1)}, bf16[320,128]{1,0:T(8,128)(2,1)S(1)}, u32[]{:S(2)}, u32[]{:S(2)}) %collective-permute-start.10) | collective-permute-done | bytes 81952 | tf_op jit(solution)/shard_map/ppermute | solution.py:601
  37.4 0.1 collective-permute-start.11
  37.5 2.1 %collective-permute-start.13 = (bf16[128,512]{1,0:T(8,128)(2,1)S(1)}, bf16[128,512]{1,0:T(8,128)(2,1)S(1)}, u32[]{:S(2)}, u32[]{:S(2)}) collective-permute-start(bf16[128,512]{1,0:T(8,128)(2,1)S(1)} %get-tuple-element.100), channel_id=1, source_target_pairs={{4,0},{8,4},{12,8},{16,12},{20,16},{24,20},{28,24},{0,28},{5,1},{9... | collective-permute-start | bytes 393224 | tf_op jit(solution)/shard_map/ppermute | solution.py:687
  39.6 0.9 %collective-permute-done.15.theirs_ref.refs_2_ = bf16[320,128]{1,0:T(8,128)(2,1)S(1)} collective-permute-done((bf16[320,128]{1,0:T(8,128)(2,1)S(1)}, bf16[320,128]{1,0:T(8,128)(2,1)S(1)}, u32[]{:S(2)}, u32[]{:S(2)}) %collective-permute-start.15) | collective-permute-done | bytes 81952 | tf_op jit(solution)/shard_map/ppermute | solution.py:601
  40.5 1.3 %collective-permute-start.16 = (bf16[320,128]{1,0:T(8,128)(2,1)S(1)}, bf16[320,128]{1,0:T(8,128)(2,1)S(1)}, u32[]{:S(2)}, u32[]{:S(2)}) collective-permute-start(bf16[320,128]{1,0:T(8,128)(2,1)S(1)} %shard_map.160), channel_id=1, source_target_pairs={{0,16},{4,20},{8,24},{12,28},{16,0},{20,4},{24,8},{28,12},{1,17},{... | collective-permute-start | bytes 245768 | tf_op jit(solution)/shard_map/ppermute | solution.py:601
  41.8 0.5 collective-permute-done.11.refs_2_
  42.2 0.1 shard_map.157
  42.3 0.7 %collective-permute-start.12 = (bf16[320,128]{1,0:T(8,128)(2,1)S(1)}, bf16[320,128]{1,0:T(8,128)(2,1)S(1)}, u32[]{:S(2)}, u32[]{:S(2)}) collective-permute-start(bf16[320,128]{1,0:T(8,128)(2,1)S(1)} %shard_map.157), channel_id=1, source_target_pairs={{0,4},{4,0},{8,12},{12,8},{16,20},{20,16},{24,28},{28,24},{1,5},{5... | collective-permute-start | bytes 245768 | tf_op jit(solution)/shard_map/ppermute | solution.py:601
  43.0 2.1 %shard_map.158 = (bf16[64,256]{1,0:T(8,128)(2,1)S(1)}, f32[64,256]{1,0:T(8,128)S(1)}, f32[256,512]{1,0:T(8,128)S(1)}, bf16[4,256,160]{2,1,0:T(8,128)(2,1)S(1)}) custom-call(bf16[64,256]{1,0:T(8,128)(2,1)S(1)} %get-tuple-element.90.query_ref, bf16[64,256]{1,0:T(8,128)(2,1)S(1)} %get-tuple-element.59.key_ref.refs_4_, ...), custom_call_target="tpu_custom_call" | custom-call | tf_op jit(solution)/shard_map/pallas_call | solution.py:575
  45.1 0.0 collective-permute-done.13.refs_11_
  45.1 1.7 %collective-permute-done.16.refs_3_ = bf16[320,128]{1,0:T(8,128)(2,1)S(1)} collective-permute-done((bf16[320,128]{1,0:T(8,128)(2,1)S(1)}, bf16[320,128]{1,0:T(8,128)(2,1)S(1)}, u32[]{:S(2)}, u32[]{:S(2)}) %collective-permute-start.16) | collective-permute-done | bytes 81952 | tf_op jit(solution)/shard_map/ppermute | solution.py:601
  46.8 0.7 %shard_map.161 = (bf16[32,256]{1,0:T(8,128)(2,1)S(1)}, bf16[256,256]{1,0:T(8,128)(2,1)S(1)}, bf16[256,512]{1,0:T(8,128)(2,1)S(1)}) custom-call(s32[1]{0:T(128)} %bitcast.2.place_ref.refs_0_, bf16[320,128]{1,0:T(8,128)(2,1)S(1)} %collective-permute-done.14.refs_1_, bf16[320,128]{1,0:T(8,128)(2,1)S(1)} %collective-permute-done.15.theirs_ref.refs_2_, ...), custom_call_target="tpu_custom_call" | custom-call | tf_op jit(solution)/shard_map/pallas_call | solution.py:575
  47.5 0.0 collective-permute-done.12.refs_3_
  47.5 1.4 %shard_map.162 = (bf16[256,512]{1,0:T(8,128)(2,1)}, bf16[64,256]{1,0:T(8,128)(2,1)}, bf16[64,256]{1,0:T(8,128)(2,1)}, bf16[256,512]{1,0:T(8,128)(2,1)}) custom-call(s32[1]{0:T(128)} %bitcast.2.place_ref.refs_0_, bf16[320,128]{1,0:T(8,128)(2,1)S(1)} %collective-permute-done.10.refs_1_, bf16[320,128]{1,0:T(8,128)(2,1)S(1)} %collective-permute-done.11.refs_2_, ...), custom_call_target="tpu_custom_call" | custom-call | tf_op jit(solution)/shard_map/pallas_call | solution.py:575
  (3 shorter events, 0.1 us)
Async XLA Ops:
  2.4 6.1 %collective-permute-start.4 = (bf16[320,128]{1,0:T(8,128)(2,1)S(1)}, bf16[320,128]{1,0:T(8,128)(2,1)S(1)}, u32[]{:S(2)}, u32[]{:S(2)}) collective-permute-start(bf16[320,128]{1,0:T(8,128)(2,1)S(1)} %get-tuple-element.75.mine_ref), channel_id=1, source_target_pairs={{0,4},{4,0},{8,12},{12,8},{16,20},{20,16},{24,28},{28,24},{1,5},{5... | collective-permute-start | bytes 245768 | tf_op jit(solution)/shard_map/ppermute | solution.py:601
  5.4 6.7 %collective-permute-start.1 = (bf16[320,128]{1,0:T(8,128)(2,1)S(1)}, bf16[320,128]{1,0:T(8,128)(2,1)S(1)}, u32[]{:S(2)}, u32[]{:S(2)}) collective-permute-start(bf16[320,128]{1,0:T(8,128)(2,1)S(1)} %get-tuple-element.68.refs_2_.refs_3_), channel_id=1, source_target_pairs={{0,16},{4,20},{8,24},{12,28},{16,0},{20,4},{24,8},{28,12},{1,17},{... | collective-permute-start | bytes 245768 | tf_op jit(solution)/shard_map/ppermute | solution.py:601
  8.0 8.7 %collective-permute-start = (bf16[128,512]{1,0:T(8,128)(2,1)S(1)}, bf16[128,512]{1,0:T(8,128)(2,1)S(1)}, u32[]{:S(2)}, u32[]{:S(2)}) collective-permute-start(bf16[128,512]{1,0:T(8,128)(2,1)S(1)} %get-tuple-element.66), channel_id=1, source_target_pairs={{0,4},{4,8},{8,12},{12,16},{16,20},{20,24},{24,28},{28,0},{1,5},{5... | collective-permute-start | bytes 393224 | tf_op jit(solution)/shard_map/ppermute | solution.py:643
  8.7 4.5 %collective-permute-start.5 = (bf16[320,128]{1,0:T(8,128)(2,1)S(1)}, bf16[320,128]{1,0:T(8,128)(2,1)S(1)}, u32[]{:S(2)}, u32[]{:S(2)}) collective-permute-start(bf16[320,128]{1,0:T(8,128)(2,1)S(1)} %shard_map.150.mine_ref), channel_id=1, source_target_pairs={{0,8},{4,12},{8,0},{12,4},{16,24},{20,28},{24,16},{28,20},{1,9},{5... | collective-permute-start | bytes 245768 | tf_op jit(solution)/shard_map/ppermute | solution.py:601
  12.4 4.9 %collective-permute-start.2 = (bf16[320,128]{1,0:T(8,128)(2,1)S(1)}, bf16[320,128]{1,0:T(8,128)(2,1)S(1)}, u32[]{:S(2)}, u32[]{:S(2)}) collective-permute-start(bf16[320,128]{1,0:T(8,128)(2,1)S(1)} %shard_map.148), channel_id=1, source_target_pairs={{0,8},{4,12},{8,0},{12,4},{16,24},{20,28},{24,16},{28,20},{1,9},{5... | collective-permute-start | bytes 245768 | tf_op jit(solution)/shard_map/ppermute | solution.py:601
  13.5 7.7 %collective-permute-start.6 = (bf16[320,128]{1,0:T(8,128)(2,1)S(1)}, bf16[320,128]{1,0:T(8,128)(2,1)S(1)}, u32[]{:S(2)}, u32[]{:S(2)}) collective-permute-start(bf16[320,128]{1,0:T(8,128)(2,1)S(1)} %shard_map.151), channel_id=1, source_target_pairs={{0,16},{4,20},{8,24},{12,28},{16,0},{20,4},{24,8},{28,12},{1,17},{... | collective-permute-start | bytes 245768 | tf_op jit(solution)/shard_map/ppermute | solution.py:601
  17.5 4.5 %collective-permute-start.3 = (bf16[320,128]{1,0:T(8,128)(2,1)S(1)}, bf16[320,128]{1,0:T(8,128)(2,1)S(1)}, u32[]{:S(2)}, u32[]{:S(2)}) collective-permute-start(bf16[320,128]{1,0:T(8,128)(2,1)S(1)} %shard_map.149), channel_id=1, source_target_pairs={{0,4},{4,0},{8,12},{12,8},{16,20},{20,16},{24,28},{28,24},{1,5},{5... | collective-permute-start | bytes 245768 | tf_op jit(solution)/shard_map/ppermute | solution.py:601
  22.7 1.8 %collective-permute-start.9 = (f32[8,256]{1,0:T(8,128)S(1)}, f32[8,256]{1,0:T(8,128)S(1)}, u32[]{:S(2)}, u32[]{:S(2)}) collective-permute-start(f32[8,256]{1,0:T(8,128)S(1)} %get-tuple-element.78.refs_0_), channel_id=1, source_target_pairs={{0,3},{1,0},{2,1},{3,2},{4,7},{5,4},{6,5},{7,6},{8,11},{9,8},{10,9... | collective-permute-start | bytes 24584 | tf_op jit(solution)/shard_map/ppermute | solution.py:674
  22.8 3.7 %collective-permute-start.8 = (f32[8,256]{1,0:T(8,128)S(1)}, f32[8,256]{1,0:T(8,128)S(1)}, u32[]{:S(2)}, u32[]{:S(2)}) collective-permute-start(f32[8,256]{1,0:T(8,128)S(1)} %get-tuple-element.78.refs_0_), channel_id=1, source_target_pairs={{0,2},{1,3},{2,0},{3,1},{4,6},{5,7},{6,4},{7,5},{8,10},{9,11},{10,... | collective-permute-start | bytes 24584 | tf_op jit(solution)/shard_map/ppermute | solution.py:674
  24.3 3.1 %collective-permute-start.7 = (f32[8,256]{1,0:T(8,128)S(1)}, f32[8,256]{1,0:T(8,128)S(1)}, u32[]{:S(2)}, u32[]{:S(2)}) collective-permute-start(f32[8,256]{1,0:T(8,128)S(1)} %get-tuple-element.78.refs_0_), channel_id=1, source_target_pairs={{0,1},{1,2},{2,3},{3,0},{4,5},{5,6},{6,7},{7,4},{8,9},{9,10},{10,1... | collective-permute-start | bytes 24584 | tf_op jit(solution)/shard_map/ppermute | solution.py:674
  28.3 6.8 %collective-permute-start.14 = (bf16[320,128]{1,0:T(8,128)(2,1)S(1)}, bf16[320,128]{1,0:T(8,128)(2,1)S(1)}, u32[]{:S(2)}, u32[]{:S(2)}) collective-permute-start(bf16[320,128]{1,0:T(8,128)(2,1)S(1)} %get-tuple-element.101.refs_0_), channel_id=1, source_target_pairs={{0,4},{4,0},{8,12},{12,8},{16,20},{20,16},{24,28},{28,24},{1,5},{5... | collective-permute-start | bytes 245768 | tf_op jit(solution)/shard_map/ppermute | solution.py:601
  31.1 6.2 %collective-permute-start.10 = (bf16[320,128]{1,0:T(8,128)(2,1)S(1)}, bf16[320,128]{1,0:T(8,128)(2,1)S(1)}, u32[]{:S(2)}, u32[]{:S(2)}) collective-permute-start(bf16[320,128]{1,0:T(8,128)(2,1)S(1)} %get-tuple-element.89.refs_2_.refs_3_), channel_id=1, source_target_pairs={{0,16},{4,20},{8,24},{12,28},{16,0},{20,4},{24,8},{28,12},{1,17},{... | collective-permute-start | bytes 245768 | tf_op jit(solution)/shard_map/ppermute | solution.py:601
  35.1 5.4 %collective-permute-start.15 = (bf16[320,128]{1,0:T(8,128)(2,1)S(1)}, bf16[320,128]{1,0:T(8,128)(2,1)S(1)}, u32[]{:S(2)}, u32[]{:S(2)}) collective-permute-start(bf16[320,128]{1,0:T(8,128)(2,1)S(1)} %shard_map.159.mine_ref), channel_id=1, source_target_pairs={{0,8},{4,12},{8,0},{12,4},{16,24},{20,28},{24,16},{28,20},{1,9},{5... | collective-permute-start | bytes 245768 | tf_op jit(solution)/shard_map/ppermute | solution.py:601
  37.4 4.9 %collective-permute-start.11 = (bf16[320,128]{1,0:T(8,128)(2,1)S(1)}, bf16[320,128]{1,0:T(8,128)(2,1)S(1)}, u32[]{:S(2)}, u32[]{:S(2)}) collective-permute-start(bf16[320,128]{1,0:T(8,128)(2,1)S(1)} %shard_map.156), channel_id=1, source_target_pairs={{0,8},{4,12},{8,0},{12,4},{16,24},{20,28},{24,16},{28,20},{1,9},{5... | collective-permute-start | bytes 245768 | tf_op jit(solution)/shard_map/ppermute | solution.py:601
  37.5 7.6 %collective-permute-start.13 = (bf16[128,512]{1,0:T(8,128)(2,1)S(1)}, bf16[128,512]{1,0:T(8,128)(2,1)S(1)}, u32[]{:S(2)}, u32[]{:S(2)}) collective-permute-start(bf16[128,512]{1,0:T(8,128)(2,1)S(1)} %get-tuple-element.100), channel_id=1, source_target_pairs={{4,0},{8,4},{12,8},{16,12},{20,16},{24,20},{28,24},{0,28},{5,1},{9... | collective-permute-start | bytes 393224 | tf_op jit(solution)/shard_map/ppermute | solution.py:687
  40.5 6.3 %collective-permute-start.16 = (bf16[320,128]{1,0:T(8,128)(2,1)S(1)}, bf16[320,128]{1,0:T(8,128)(2,1)S(1)}, u32[]{:S(2)}, u32[]{:S(2)}) collective-permute-start(bf16[320,128]{1,0:T(8,128)(2,1)S(1)} %shard_map.160), channel_id=1, source_target_pairs={{0,16},{4,20},{8,24},{12,28},{16,0},{20,4},{24,8},{28,12},{1,17},{... | collective-permute-start | bytes 245768 | tf_op jit(solution)/shard_map/ppermute | solution.py:601
  42.3 5.2 %collective-permute-start.12 = (bf16[320,128]{1,0:T(8,128)(2,1)S(1)}, bf16[320,128]{1,0:T(8,128)(2,1)S(1)}, u32[]{:S(2)}, u32[]{:S(2)}) collective-permute-start(bf16[320,128]{1,0:T(8,128)(2,1)S(1)} %shard_map.157), channel_id=1, source_target_pairs={{0,4},{4,0},{8,12},{12,8},{16,20},{20,16},{24,28},{28,24},{1,5},{5... | collective-permute-start | bytes 245768 | tf_op jit(solution)/shard_map/ppermute | solution.py:601

commit v6 on v5

--- a/solution.py
+++ b/solution.py
@@ -432,28 +432,35 @@
     pad = jnp.zeros((WINDOW, HEAD_DIM), F32)
     inv_rms = cols_ref[:, heads : heads + 1]
     per = heads // CHUNKS
-    for h in range(heads):
-        columns = span(h, HEAD_DIM)
+    groups = [slice(s, s + WINDOW) for s in starts]
+    bands = [slice(s, s + 2 * WINDOW) for s in starts]
+    spans = [span(h, HEAD_DIM) for h in range(heads)]
+    keys = [jnp.concatenate([rim_ref[:WINDOW, c], wkey_ref[:, c]], axis=0) for c in spans]
+    values = [jnp.concatenate([rim_ref[WINDOW:, c], value_ref[:, c]], axis=0) for c in spans]
+    grads = [grad_ref[:, c].astype(BF16) for c in spans]
+    queries = [wquery_ref[:, c] for c in spans]
+    dprobs = [
+        jnp.concatenate([mm_nt(grad[g], value[band]) for g, band in zip(groups, bands)], axis=0)
+        for grad, value in zip(grads, values)
+    ]
+    dlogits = []
+    for h, dprob in enumerate(dprobs):
+        weights = weights_ref[h]
+        dlogits.append((weights * (dprob - lane_sum(weights * dprob))).astype(BF16))
+    for h, c in enumerate(spans):
+        dlogit, narrow = dlogits[h], weights_ref[h].astype(BF16)
+        key_parts = [mm_tn(dlogit[g], queries[h][g]) for g in groups]
+        value_parts = [mm_tn(narrow[g], grads[h][g]) for g in groups]
+        parts = [mm(dlogit[g], keys[h][band]) for g, band in zip(groups, bands)]
+        back_ref[:WINDOW, c] = (key_parts[0][:WINDOW] * root).astype(BF16)
+        back_ref[WINDOW:, c] = value_parts[0][:WINDOW].astype(BF16)
+        key_sum = [p[WINDOW:] + q[:WINDOW] for p, q in zip(key_parts, key_parts[1:] + [pad])]
+        value_sum = [p[WINDOW:] + q[:WINDOW] for p, q in zip(value_parts, value_parts[1:] + [pad])]
+        gwq_ref[:, c] = (jnp.concatenate(parts, axis=0) * root).astype(BF16)
+        gwk_ref[:, c] = jnp.concatenate(key_sum, axis=0) * root
+        gv_ref[:, c] = jnp.concatenate(value_sum, axis=0)
         merged = merged_refs[h // per][:, span(h % per, HEAD_DIM)]
-        normed_ref[:, columns] = (merged * inv_rms * gain_ref[0:1, columns]).astype(BF16)
-        keys = jnp.concatenate([rim_ref[:WINDOW, columns], wkey_ref[:, columns]], axis=0)
-        values = jnp.concatenate([rim_ref[WINDOW:, columns], value_ref[:, columns]], axis=0)
-        grad = grad_ref[:, columns].astype(BF16)
-        query = wquery_ref[:, columns]
-        weights = weights_ref[h]
-        narrow = weights.astype(BF16)
-        dprob = jnp.concatenate([mm_nt(grad[s : s + WINDOW], values[s : s + 2 * WINDOW]) for s in starts], axis=0)
-        dlogits = (weights * (dprob - lane_sum(weights * dprob))).astype(BF16)
-        grads = [mm(dlogits[s : s + WINDOW], keys[s : s + 2 * WINDOW]) for s in starts]
-        gwq_ref[:, columns] = (jnp.concatenate(grads, axis=0) * root).astype(BF16)
-        key_parts = [mm_tn(dlogits[s : s + WINDOW], query[s : s + WINDOW]) for s in starts]
-        value_parts = [mm_tn(narrow[s : s + WINDOW], grad[s : s + WINDOW]) for s in starts]
-        back_ref[:WINDOW, columns] = (key_parts[0][:WINDOW] * root).astype(BF16)
-        back_ref[WINDOW:, columns] = value_parts[0][:WINDOW].astype(BF16)
-        key_sum = [a[WINDOW:] + b[:WINDOW] for a, b in zip(key_parts, key_parts[1:] + [pad])]
-        value_sum = [a[WINDOW:] + b[:WINDOW] for a, b in zip(value_parts, value_parts[1:] + [pad])]
-        gwk_ref[:, columns] = jnp.concatenate(key_sum, axis=0) * root
-        gv_ref[:, columns] = jnp.concatenate(value_sum, axis=0)
+        normed_ref[:, c] = (merged * inv_rms * gain_ref[0:1, c]).astype(BF16)
 
 
 def local_back_body(query_ref, key_ref, value_ref, sel_ref, sel_t_ref, rows_ref, grad_ref, ratios_ref, gv_in_ref, *refs):

time: 49 us -> 48.5 us (0.990)
  Pallas kernels: 14.8 us -> 14.3 us
    pallas_call x18, Pallas kernels: 14.8 us -> 14.3 us  [call(): pl.pallas_call(body if not ties else lambda *refs: body(*refs[:given], *r...]
  transfers between devices with their start and end apart: 17 -> 17, of which waited for: 9 -> 9; matrix products, arithmetic and copies ran while one was open for 0% -> 0% of each run, Pallas kernels for 21% -> 20%
where the time goes in v6:
time: 48.5 us; the launch traced here: 48.3 us
  starting transfers between devices  24.6 us (51%)
  Pallas kernels  14.3 us (29%)
  waiting for transfers between devices  8.67 us (18%)
  between operations  0.74 us (2%)
    ppermute x12, starting transfers between devices, exchanged(): parts[c].append(lax.ppermute(held[c], 'seq', pairs))  20.5 us
    pallas_call x18, Pallas kernels, call(): pl.pallas_call(body if not ties else lambda *refs: body(*refs[:given], *r...  14.3 us
    ppermute x12, waiting for transfers between devices, exchanged(): parts[c].append(lax.ppermute(held[c], 'seq', pairs))  5.82 us
    ppermute x3, waiting for transfers between devices, shards(): lax.ppermute(stats, 'head', [(i, (i + s) % ring) for i in range(ring)])  2.85 us
    ppermute x1, starting transfers between devices, middle(): lax.ppermute(back, 'seq', [((i + 1) % count, i) for i in range(count)])  1.83 us
    ppermute x3, starting transfers between devices, shards(): lax.ppermute(stats, 'head', [(i, (i + s) % ring) for i in range(ring)])  1.78 us
  transfers between devices with their start and end apart: 17, of which 9 were waited for; matrix products, arithmetic and copies ran while one was open for 0% of the time, Pallas kernels for 20%

profile of v6, /device:TPU:0, one launch (start us, length us, event | category | flops | bytes accessed | tf_op | source)
XLA Modules:
  0.0 48.3 jit_solution(17006434714915614940)
XLA Ops:
  0.6 1.7 %shard_map.145 = (bf16[320,128]{1,0:T(8,128)(2,1)S(1)}, bf16[320,128]{1,0:T(8,128)(2,1)S(1)}, bf16[128,512]{1,0:T(8,128)(2,1)S(1)}, bf16[64,256]{1,0:T(8,128)(2,...) custom-call(bf16[64,256]{1,0:T(8,128)(2,1)} %bitcast.6, ...), custom_call_target="tpu_custom_call" | custom-call | tf_op jit(solution)/shard_map/pallas_call | solution.py:582
  2.4 3.0 %collective-permute-start.4 = (bf16[320,128]{1,0:T(8,128)(2,1)S(1)}, bf16[320,128]{1,0:T(8,128)(2,1)S(1)}, u32[]{:S(2)}, u32[]{:S(2)}) collective-permute-start(bf16[320,128]{1,0:T(8,128)(2,1)S(1)} %get-tuple-element.75.mine_ref), channel_id=1, source_target_pairs={{0,4},{4,0},{8,12},{12,8},{16,20},{20,16},{24,28},{28,24},{1,5},{5... | collective-permute-start | bytes 245768 | tf_op jit(solution)/shard_map/ppermute | solution.py:608
  5.4 2.6 %collective-permute-start.1 = (bf16[320,128]{1,0:T(8,128)(2,1)S(1)}, bf16[320,128]{1,0:T(8,128)(2,1)S(1)}, u32[]{:S(2)}, u32[]{:S(2)}) collective-permute-start(bf16[320,128]{1,0:T(8,128)(2,1)S(1)} %get-tuple-element.68.refs_2_.refs_3_), channel_id=1, source_target_pairs={{0,16},{4,20},{8,24},{12,28},{16,0},{20,4},{24,8},{28,12},{1,17},{... | collective-permute-start | bytes 245768 | tf_op jit(solution)/shard_map/ppermute | solution.py:608
  8.0 0.5 %collective-permute-start = (bf16[128,512]{1,0:T(8,128)(2,1)S(1)}, bf16[128,512]{1,0:T(8,128)(2,1)S(1)}, u32[]{:S(2)}, u32[]{:S(2)}) collective-permute-start(bf16[128,512]{1,0:T(8,128)(2,1)S(1)} %get-tuple-element.66), channel_id=1, source_target_pairs={{0,4},{4,8},{8,12},{12,16},{16,20},{20,24},{24,28},{28,0},{1,5},{5... | collective-permute-start | bytes 393224 | tf_op jit(solution)/shard_map/ppermute | solution.py:650
  8.5 0.0 collective-permute-done.4.theirs_ref.refs_1_
  8.5 0.2 shard_map.150.mine_ref
  8.7 1.6 %collective-permute-start.5 = (bf16[320,128]{1,0:T(8,128)(2,1)S(1)}, bf16[320,128]{1,0:T(8,128)(2,1)S(1)}, u32[]{:S(2)}, u32[]{:S(2)}) collective-permute-start(bf16[320,128]{1,0:T(8,128)(2,1)S(1)} %shard_map.150.mine_ref), channel_id=1, source_target_pairs={{0,8},{4,12},{8,0},{12,4},{16,24},{20,28},{24,16},{28,20},{1,9},{5... | collective-permute-start | bytes 245768 | tf_op jit(solution)/shard_map/ppermute | solution.py:608
  10.4 1.7 %shard_map.146 = (f32[256,512]{1,0:T(8,128)S(1)}, f32[256,128]{1,0:T(8,128)S(1)}, bf16[4,256,160]{2,1,0:T(8,128)(2,1)S(1)}, bf16[640,256]{1,0:T(8,128)(2,1)S(1)}...) custom-call(bf16[64,256]{1,0:T(8,128)(2,1)} %bitcast.7, ...), custom_call_target="tpu_custom_call" | custom-call | tf_op jit(solution)/shard_map/pallas_call | solution.py:582
  12.1 0.0 collective-permute-done.1.refs_1_
  12.1 0.2 shard_map.148
  12.4 0.5 %collective-permute-start.2 = (bf16[320,128]{1,0:T(8,128)(2,1)S(1)}, bf16[320,128]{1,0:T(8,128)(2,1)S(1)}, u32[]{:S(2)}, u32[]{:S(2)}) collective-permute-start(bf16[320,128]{1,0:T(8,128)(2,1)S(1)} %shard_map.148), channel_id=1, source_target_pairs={{0,8},{4,12},{8,0},{12,4},{16,24},{20,28},{24,16},{28,20},{1,9},{5... | collective-permute-start | bytes 245768 | tf_op jit(solution)/shard_map/ppermute | solution.py:608
  12.9 0.3 collective-permute-done.5.theirs_ref.refs_2_
  13.2 0.2 shard_map.151
  13.5 3.2 %collective-permute-start.6 = (bf16[320,128]{1,0:T(8,128)(2,1)S(1)}, bf16[320,128]{1,0:T(8,128)(2,1)S(1)}, u32[]{:S(2)}, u32[]{:S(2)}) collective-permute-start(bf16[320,128]{1,0:T(8,128)(2,1)S(1)} %shard_map.151), channel_id=1, source_target_pairs={{0,16},{4,20},{8,24},{12,28},{16,0},{20,4},{24,8},{28,12},{1,17},{... | collective-permute-start | bytes 245768 | tf_op jit(solution)/shard_map/ppermute | solution.py:608
  16.7 0.0 collective-permute-done.rim_ref.refs_4_
  16.7 0.6 %collective-permute-done.2.refs_2_ = bf16[320,128]{1,0:T(8,128)(2,1)S(1)} collective-permute-done((bf16[320,128]{1,0:T(8,128)(2,1)S(1)}, bf16[320,128]{1,0:T(8,128)(2,1)S(1)}, u32[]{:S(2)}, u32[]{:S(2)}) %collective-permute-start.2) | collective-permute-done | bytes 81952 | tf_op jit(solution)/shard_map/ppermute | solution.py:608
  17.3 0.2 shard_map.149
  17.5 2.0 %collective-permute-start.3 = (bf16[320,128]{1,0:T(8,128)(2,1)S(1)}, bf16[320,128]{1,0:T(8,128)(2,1)S(1)}, u32[]{:S(2)}, u32[]{:S(2)}) collective-permute-start(bf16[320,128]{1,0:T(8,128)(2,1)S(1)} %shard_map.149), channel_id=1, source_target_pairs={{0,4},{4,0},{8,12},{12,8},{16,20},{20,16},{24,28},{28,24},{1,5},{5... | collective-permute-start | bytes 245768 | tf_op jit(solution)/shard_map/ppermute | solution.py:608
  19.5 1.7 %shard_map.147 = (f32[256,512]{1,0:T(8,128)S(1)}, f32[4,256,128]{2,1,0:T(8,128)S(1)}, bf16[256,512]{1,0:T(8,128)(2,1)S(1)}, f32[1,512]{1,0:T(1,128)S(1)}) custom-call(s32[1]{0:T(128)} %bitcast.2.place_ref.refs_0_, bf16[256,512]{1,0:T(8,128)(2,1)} %cot_hbm.1, f32[1,512]{1,0:T(1,128)} %bitcast.8, bf16[256,512]{1,0:T(8,128)(2,1)S(1)} %get-tuple-element.64.wquery_ref, ...), custom_call_target="tpu_custom_call" | custom-call | tf_op jit(solution)/shard_map/pallas_call | solution.py:582
  21.2 0.0 collective-permute-done.6.refs_3_
  21.2 0.5 %shard_map.152 = (f32[256,256]{1,0:T(8,128)S(1)}, f32[256,256]{1,0:T(8,128)S(1)}, f32[256,128]{1,0:T(8,128)S(1)}, f32[320,128]{1,0:T(8,128)S(1)}, f32[16,160]{1,...) custom-call(s32[1]{0:T(128)} %bitcast.2.place_ref.refs_0_, ...), custom_call_target="tpu_custom_call" | custom-call | tf_op jit(solution)/shard_map/pallas_call | solution.py:582
  21.7 0.3 collective-permute-done.3.refs_3_
  22.0 0.7 %shard_map.153 = (f32[256,256]{1,0:T(8,128)S(1)}, f32[256,256]{1,0:T(8,128)S(1)}, f32[256,128]{1,0:T(8,128)S(1)}, f32[320,128]{1,0:T(8,128)S(1)}, f32[16,160]{1,0:T(8,128)S(1)}, /*index=5*/f32[8,256]{1,0:T(8,128)S(1)}) custom-call(s32[1]{0:T(128)} %bitcast.2.place_ref.refs_0_, bf16[320,128]{1,0:T(8,128)(2,1)S(1)} %collective-permute-done.1.refs_1_, ...), custom_call_target="tpu_custom_call" | custom-call | tf_op jit(solution)/shard_map/pallas_call | solution.py:582
  22.7 0.1 collective-permute-start.9
  22.8 1.5 %collective-permute-start.8 = (f32[8,256]{1,0:T(8,128)S(1)}, f32[8,256]{1,0:T(8,128)S(1)}, u32[]{:S(2)}, u32[]{:S(2)}) collective-permute-start(f32[8,256]{1,0:T(8,128)S(1)} %get-tuple-element.78.refs_0_), channel_id=1, source_target_pairs={{0,2},{1,3},{2,0},{3,1},{4,6},{5,7},{6,4},{7,5},{8,10},{9,11},{10,... | collective-permute-start | bytes 24584 | tf_op jit(solution)/shard_map/ppermute | solution.py:681
  24.3 0.2 collective-permute-start.7
  24.5 0.0 collective-permute-done.9.refs_3_
  24.5 2.0 %collective-permute-done.8.refs_2_ = f32[8,256]{1,0:T(8,128)S(1)} collective-permute-done((f32[8,256]{1,0:T(8,128)S(1)}, f32[8,256]{1,0:T(8,128)S(1)}, u32[]{:S(2)}, u32[]{:S(2)}) %collective-permute-start.8) | collective-permute-done | bytes 8224 | tf_op jit(solution)/shard_map/ppermute | solution.py:681
  26.5 0.9 %collective-permute-done.7.refs_1_ = f32[8,256]{1,0:T(8,128)S(1)} collective-permute-done((f32[8,256]{1,0:T(8,128)S(1)}, f32[8,256]{1,0:T(8,128)S(1)}, u32[]{:S(2)}, u32[]{:S(2)}) %collective-permute-start.7) | collective-permute-done | bytes 8224 | tf_op jit(solution)/shard_map/ppermute | solution.py:681
  27.4 0.9 %shard_map.154 = (bf16[320,128]{1,0:T(8,128)(2,1)S(1)}, bf16[320,128]{1,0:T(8,128)(2,1)S(1)}, f32[256,512]{1,0:T(8,128)S(1)}, f32[256,128]{1,0:T(8,128)S(1)}, f32[8,256]{1,0:T(8,128)S(1)}) custom-call(f32[8,256]{1,0:T(8,128)S(1)} %get-tuple-element.78.refs_0_, f32[8,256]{1,0:T(8,128)S(1)} %collective-permute-done.7.refs_1_, ...), custom_call_target="tpu_custom_call" | custom-call | tf_op jit(solution)/shard_map/pallas_call | solution.py:582
  28.3 2.8 %collective-permute-start.14 = (bf16[320,128]{1,0:T(8,128)(2,1)S(1)}, bf16[320,128]{1,0:T(8,128)(2,1)S(1)}, u32[]{:S(2)}, u32[]{:S(2)}) collective-permute-start(bf16[320,128]{1,0:T(8,128)(2,1)S(1)} %get-tuple-element.101.refs_0_), channel_id=1, source_target_pairs={{0,4},{4,0},{8,12},{12,8},{16,20},{20,16},{24,28},{28,24},{1,5},{5... | collective-permute-start | bytes 245768 | tf_op jit(solution)/shard_map/ppermute | solution.py:608
  31.1 1.7 %collective-permute-start.10 = (bf16[320,128]{1,0:T(8,128)(2,1)S(1)}, bf16[320,128]{1,0:T(8,128)(2,1)S(1)}, u32[]{:S(2)}, u32[]{:S(2)}) collective-permute-start(bf16[320,128]{1,0:T(8,128)(2,1)S(1)} %get-tuple-element.89.refs_2_.refs_3_), channel_id=1, source_target_pairs={{0,16},{4,20},{8,24},{12,28},{16,0},{20,4},{24,8},{28,12},{1,17},{... | collective-permute-start | bytes 245768 | tf_op jit(solution)/shard_map/ppermute | solution.py:608
  32.7 1.8 %shard_map.155 = (bf16[256,512]{1,0:T(8,128)(2,1)}, f32[256,512]{1,0:T(8,128)S(1)}, f32[256,512]{1,0:T(8,128)S(1)}, bf16[128,512]{1,0:T(8,128)(2,1)S(1)}, bf16[256,512]{1,0:T(8,128)(2,1)}) custom-call(bf16[256,512]{1,0:T(8,128)(2,1)S(1)} %get-tuple-element.64.wquery_ref, bf16[256,512]{1,0:T(8,128)(2,1)S(1)} %get-tuple-element.65.wkey_ref, ...), custom_call_target="tpu_custom_call" | custom-call | tf_op jit(solution)/shard_map/pallas_call | solution.py:582
  34.5 0.0 collective-permute-done.14.refs_1_
  34.6 1.1 %collective-permute-start.15 = (bf16[320,128]{1,0:T(8,128)(2,1)S(1)}, bf16[320,128]{1,0:T(8,128)(2,1)S(1)}, u32[]{:S(2)}, u32[]{:S(2)}) collective-permute-start(bf16[320,128]{1,0:T(8,128)(2,1)S(1)} %shard_map.159.mine_ref), channel_id=1, source_target_pairs={{0,8},{4,12},{8,0},{12,4},{16,24},{20,28},{24,16},{28,20},{1,9},{5... | collective-permute-start | bytes 245768 | tf_op jit(solution)/shard_map/ppermute | solution.py:608
  35.7 1.6 %collective-permute-done.10.refs_1_ = bf16[320,128]{1,0:T(8,128)(2,1)S(1)} collective-permute-done((bf16[320,128]{1,0:T(8,128)(2,1)S(1)}, bf16[320,128]{1,0:T(8,128)(2,1)S(1)}, u32[]{:S(2)}, u32[]{:S(2)}) %collective-permute-start.10) | collective-permute-done | bytes 81952 | tf_op jit(solution)/shard_map/ppermute | solution.py:608
  37.4 0.6 %collective-permute-start.11 = (bf16[320,128]{1,0:T(8,128)(2,1)S(1)}, bf16[320,128]{1,0:T(8,128)(2,1)S(1)}, u32[]{:S(2)}, u32[]{:S(2)}) collective-permute-start(bf16[320,128]{1,0:T(8,128)(2,1)S(1)} %shard_map.156), channel_id=1, source_target_pairs={{0,8},{4,12},{8,0},{12,4},{16,24},{20,28},{24,16},{28,20},{1,9},{5... | collective-permute-start | bytes 245768 | tf_op jit(solution)/shard_map/ppermute | solution.py:608
  38.0 1.8 %collective-permute-start.13 = (bf16[128,512]{1,0:T(8,128)(2,1)S(1)}, bf16[128,512]{1,0:T(8,128)(2,1)S(1)}, u32[]{:S(2)}, u32[]{:S(2)}) collective-permute-start(bf16[128,512]{1,0:T(8,128)(2,1)S(1)} %get-tuple-element.100), channel_id=1, source_target_pairs={{4,0},{8,4},{12,8},{16,12},{20,16},{24,20},{28,24},{0,28},{5,1},{9... | collective-permute-start | bytes 393224 | tf_op jit(solution)/shard_map/ppermute | solution.py:694
  39.8 0.2 collective-permute-done.15.theirs_ref.refs_2_
  40.0 1.3 %collective-permute-start.16 = (bf16[320,128]{1,0:T(8,128)(2,1)S(1)}, bf16[320,128]{1,0:T(8,128)(2,1)S(1)}, u32[]{:S(2)}, u32[]{:S(2)}) collective-permute-start(bf16[320,128]{1,0:T(8,128)(2,1)S(1)} %shard_map.160), channel_id=1, source_target_pairs={{0,16},{4,20},{8,24},{12,28},{16,0},{20,4},{24,8},{28,12},{1,17},{... | collective-permute-start | bytes 245768 | tf_op jit(solution)/shard_map/ppermute | solution.py:608
  41.3 0.8 %collective-permute-done.11.refs_2_ = bf16[320,128]{1,0:T(8,128)(2,1)S(1)} collective-permute-done((bf16[320,128]{1,0:T(8,128)(2,1)S(1)}, bf16[320,128]{1,0:T(8,128)(2,1)S(1)}, u32[]{:S(2)}, u32[]{:S(2)}) %collective-permute-start.11) | collective-permute-done | bytes 81952 | tf_op jit(solution)/shard_map/ppermute | solution.py:608
  42.1 0.1 shard_map.157
  42.1 0.1 collective-permute-start.12
  42.2 2.1 %shard_map.158 = (bf16[64,256]{1,0:T(8,128)(2,1)S(1)}, f32[64,256]{1,0:T(8,128)S(1)}, f32[256,512]{1,0:T(8,128)S(1)}, bf16[4,256,160]{2,1,0:T(8,128)(2,1)S(1)}) custom-call(bf16[64,256]{1,0:T(8,128)(2,1)S(1)} %get-tuple-element.90.query_ref, bf16[64,256]{1,0:T(8,128)(2,1)S(1)} %get-tuple-element.59.key_ref.refs_4_, ...), custom_call_target="tpu_custom_call" | custom-call | tf_op jit(solution)/shard_map/pallas_call | solution.py:582
  44.3 0.0 collective-permute-done.13.refs_11_
  44.3 2.0 %collective-permute-done.16.refs_3_ = bf16[320,128]{1,0:T(8,128)(2,1)S(1)} collective-permute-done((bf16[320,128]{1,0:T(8,128)(2,1)S(1)}, bf16[320,128]{1,0:T(8,128)(2,1)S(1)}, u32[]{:S(2)}, u32[]{:S(2)}) %collective-permute-start.16) | collective-permute-done | bytes 81952 | tf_op jit(solution)/shard_map/ppermute | solution.py:608
  46.3 0.7 %shard_map.161 = (bf16[32,256]{1,0:T(8,128)(2,1)S(1)}, bf16[256,256]{1,0:T(8,128)(2,1)S(1)}, bf16[256,512]{1,0:T(8,128)(2,1)S(1)}) custom-call(s32[1]{0:T(128)} %bitcast.2.place_ref.refs_0_, bf16[320,128]{1,0:T(8,128)(2,1)S(1)} %collective-permute-done.14.refs_1_, bf16[320,128]{1,0:T(8,128)(2,1)S(1)} %collective-permute-done.15.theirs_ref.refs_2_, ...), custom_call_target="tpu_custom_call" | custom-call | tf_op jit(solution)/shard_map/pallas_call | solution.py:582
  47.0 0.0 collective-permute-done.12.refs_3_
  47.0 1.4 %shard_map.162 = (bf16[256,512]{1,0:T(8,128)(2,1)}, bf16[64,256]{1,0:T(8,128)(2,1)}, bf16[64,256]{1,0:T(8,128)(2,1)}, bf16[256,512]{1,0:T(8,128)(2,1)}) custom-call(s32[1]{0:T(128)} %bitcast.2.place_ref.refs_0_, bf16[320,128]{1,0:T(8,128)(2,1)S(1)} %collective-permute-done.10.refs_1_, bf16[320,128]{1,0:T(8,128)(2,1)S(1)} %collective-permute-done.11.refs_2_, ...), custom_call_target="tpu_custom_call" | custom-call | tf_op jit(solution)/shard_map/pallas_call | solution.py:582
  (3 shorter events, 0.1 us)
Async XLA Ops:
  2.4 6.1 %collective-permute-start.4 = (bf16[320,128]{1,0:T(8,128)(2,1)S(1)}, bf16[320,128]{1,0:T(8,128)(2,1)S(1)}, u32[]{:S(2)}, u32[]{:S(2)}) collective-permute-start(bf16[320,128]{1,0:T(8,128)(2,1)S(1)} %get-tuple-element.75.mine_ref), channel_id=1, source_target_pairs={{0,4},{4,0},{8,12},{12,8},{16,20},{20,16},{24,28},{28,24},{1,5},{5... | collective-permute-start | bytes 245768 | tf_op jit(solution)/shard_map/ppermute | solution.py:608
  5.4 6.7 %collective-permute-start.1 = (bf16[320,128]{1,0:T(8,128)(2,1)S(1)}, bf16[320,128]{1,0:T(8,128)(2,1)S(1)}, u32[]{:S(2)}, u32[]{:S(2)}) collective-permute-start(bf16[320,128]{1,0:T(8,128)(2,1)S(1)} %get-tuple-element.68.refs_2_.refs_3_), channel_id=1, source_target_pairs={{0,16},{4,20},{8,24},{12,28},{16,0},{20,4},{24,8},{28,12},{1,17},{... | collective-permute-start | bytes 245768 | tf_op jit(solution)/shard_map/ppermute | solution.py:608
  8.0 8.7 %collective-permute-start = (bf16[128,512]{1,0:T(8,128)(2,1)S(1)}, bf16[128,512]{1,0:T(8,128)(2,1)S(1)}, u32[]{:S(2)}, u32[]{:S(2)}) collective-permute-start(bf16[128,512]{1,0:T(8,128)(2,1)S(1)} %get-tuple-element.66), channel_id=1, source_target_pairs={{0,4},{4,8},{8,12},{12,16},{16,20},{20,24},{24,28},{28,0},{1,5},{5... | collective-permute-start | bytes 393224 | tf_op jit(solution)/shard_map/ppermute | solution.py:650
  8.7 4.5 %collective-permute-start.5 = (bf16[320,128]{1,0:T(8,128)(2,1)S(1)}, bf16[320,128]{1,0:T(8,128)(2,1)S(1)}, u32[]{:S(2)}, u32[]{:S(2)}) collective-permute-start(bf16[320,128]{1,0:T(8,128)(2,1)S(1)} %shard_map.150.mine_ref), channel_id=1, source_target_pairs={{0,8},{4,12},{8,0},{12,4},{16,24},{20,28},{24,16},{28,20},{1,9},{5... | collective-permute-start | bytes 245768 | tf_op jit(solution)/shard_map/ppermute | solution.py:608
  12.4 4.9 %collective-permute-start.2 = (bf16[320,128]{1,0:T(8,128)(2,1)S(1)}, bf16[320,128]{1,0:T(8,128)(2,1)S(1)}, u32[]{:S(2)}, u32[]{:S(2)}) collective-permute-start(bf16[320,128]{1,0:T(8,128)(2,1)S(1)} %shard_map.148), channel_id=1, source_target_pairs={{0,8},{4,12},{8,0},{12,4},{16,24},{20,28},{24,16},{28,20},{1,9},{5... | collective-permute-start | bytes 245768 | tf_op jit(solution)/shard_map/ppermute | solution.py:608
  13.5 7.7 %collective-permute-start.6 = (bf16[320,128]{1,0:T(8,128)(2,1)S(1)}, bf16[320,128]{1,0:T(8,128)(2,1)S(1)}, u32[]{:S(2)}, u32[]{:S(2)}) collective-permute-start(bf16[320,128]{1,0:T(8,128)(2,1)S(1)} %shard_map.151), channel_id=1, source_target_pairs={{0,16},{4,20},{8,24},{12,28},{16,0},{20,4},{24,8},{28,12},{1,17},{... | collective-permute-start | bytes 245768 | tf_op jit(solution)/shard_map/ppermute | solution.py:608
  17.5 4.5 %collective-permute-start.3 = (bf16[320,128]{1,0:T(8,128)(2,1)S(1)}, bf16[320,128]{1,0:T(8,128)(2,1)S(1)}, u32[]{:S(2)}, u32[]{:S(2)}) collective-permute-start(bf16[320,128]{1,0:T(8,128)(2,1)S(1)} %shard_map.149), channel_id=1, source_target_pairs={{0,4},{4,0},{8,12},{12,8},{16,20},{20,16},{24,28},{28,24},{1,5},{5... | collective-permute-start | bytes 245768 | tf_op jit(solution)/shard_map/ppermute | solution.py:608
  22.7 1.8 %collective-permute-start.9 = (f32[8,256]{1,0:T(8,128)S(1)}, f32[8,256]{1,0:T(8,128)S(1)}, u32[]{:S(2)}, u32[]{:S(2)}) collective-permute-start(f32[8,256]{1,0:T(8,128)S(1)} %get-tuple-element.78.refs_0_), channel_id=1, source_target_pairs={{0,3},{1,0},{2,1},{3,2},{4,7},{5,4},{6,5},{7,6},{8,11},{9,8},{10,9... | collective-permute-start | bytes 24584 | tf_op jit(solution)/shard_map/ppermute | solution.py:681
  22.8 3.7 %collective-permute-start.8 = (f32[8,256]{1,0:T(8,128)S(1)}, f32[8,256]{1,0:T(8,128)S(1)}, u32[]{:S(2)}, u32[]{:S(2)}) collective-permute-start(f32[8,256]{1,0:T(8,128)S(1)} %get-tuple-element.78.refs_0_), channel_id=1, source_target_pairs={{0,2},{1,3},{2,0},{3,1},{4,6},{5,7},{6,4},{7,5},{8,10},{9,11},{10,... | collective-permute-start | bytes 24584 | tf_op jit(solution)/shard_map/ppermute | solution.py:681
  24.3 3.1 %collective-permute-start.7 = (f32[8,256]{1,0:T(8,128)S(1)}, f32[8,256]{1,0:T(8,128)S(1)}, u32[]{:S(2)}, u32[]{:S(2)}) collective-permute-start(f32[8,256]{1,0:T(8,128)S(1)} %get-tuple-element.78.refs_0_), channel_id=1, source_target_pairs={{0,1},{1,2},{2,3},{3,0},{4,5},{5,6},{6,7},{7,4},{8,9},{9,10},{10,1... | collective-permute-start | bytes 24584 | tf_op jit(solution)/shard_map/ppermute | solution.py:681
  28.3 6.3 %collective-permute-start.14 = (bf16[320,128]{1,0:T(8,128)(2,1)S(1)}, bf16[320,128]{1,0:T(8,128)(2,1)S(1)}, u32[]{:S(2)}, u32[]{:S(2)}) collective-permute-start(bf16[320,128]{1,0:T(8,128)(2,1)S(1)} %get-tuple-element.101.refs_0_), channel_id=1, source_target_pairs={{0,4},{4,0},{8,12},{12,8},{16,20},{20,16},{24,28},{28,24},{1,5},{5... | collective-permute-start | bytes 245768 | tf_op jit(solution)/shard_map/ppermute | solution.py:608
  31.1 6.2 %collective-permute-start.10 = (bf16[320,128]{1,0:T(8,128)(2,1)S(1)}, bf16[320,128]{1,0:T(8,128)(2,1)S(1)}, u32[]{:S(2)}, u32[]{:S(2)}) collective-permute-start(bf16[320,128]{1,0:T(8,128)(2,1)S(1)} %get-tuple-element.89.refs_2_.refs_3_), channel_id=1, source_target_pairs={{0,16},{4,20},{8,24},{12,28},{16,0},{20,4},{24,8},{28,12},{1,17},{... | collective-permute-start | bytes 245768 | tf_op jit(solution)/shard_map/ppermute | solution.py:608
  34.6 5.4 %collective-permute-start.15 = (bf16[320,128]{1,0:T(8,128)(2,1)S(1)}, bf16[320,128]{1,0:T(8,128)(2,1)S(1)}, u32[]{:S(2)}, u32[]{:S(2)}) collective-permute-start(bf16[320,128]{1,0:T(8,128)(2,1)S(1)} %shard_map.159.mine_ref), channel_id=1, source_target_pairs={{0,8},{4,12},{8,0},{12,4},{16,24},{20,28},{24,16},{28,20},{1,9},{5... | collective-permute-start | bytes 245768 | tf_op jit(solution)/shard_map/ppermute | solution.py:608
  37.4 4.7 %collective-permute-start.11 = (bf16[320,128]{1,0:T(8,128)(2,1)S(1)}, bf16[320,128]{1,0:T(8,128)(2,1)S(1)}, u32[]{:S(2)}, u32[]{:S(2)}) collective-permute-start(bf16[320,128]{1,0:T(8,128)(2,1)S(1)} %shard_map.156), channel_id=1, source_target_pairs={{0,8},{4,12},{8,0},{12,4},{16,24},{20,28},{24,16},{28,20},{1,9},{5... | collective-permute-start | bytes 245768 | tf_op jit(solution)/shard_map/ppermute | solution.py:608
  38.0 6.4 %collective-permute-start.13 = (bf16[128,512]{1,0:T(8,128)(2,1)S(1)}, bf16[128,512]{1,0:T(8,128)(2,1)S(1)}, u32[]{:S(2)}, u32[]{:S(2)}) collective-permute-start(bf16[128,512]{1,0:T(8,128)(2,1)S(1)} %get-tuple-element.100), channel_id=1, source_target_pairs={{4,0},{8,4},{12,8},{16,12},{20,16},{24,20},{28,24},{0,28},{5,1},{9... | collective-permute-start | bytes 393224 | tf_op jit(solution)/shard_map/ppermute | solution.py:694
  40.0 6.3 %collective-permute-start.16 = (bf16[320,128]{1,0:T(8,128)(2,1)S(1)}, bf16[320,128]{1,0:T(8,128)(2,1)S(1)}, u32[]{:S(2)}, u32[]{:S(2)}) collective-permute-start(bf16[320,128]{1,0:T(8,128)(2,1)S(1)} %shard_map.160), channel_id=1, source_target_pairs={{0,16},{4,20},{8,24},{12,28},{16,0},{20,4},{24,8},{28,12},{1,17},{... | collective-permute-start | bytes 245768 | tf_op jit(solution)/shard_map/ppermute | solution.py:608
  42.1 4.8 %collective-permute-start.12 = (bf16[320,128]{1,0:T(8,128)(2,1)S(1)}, bf16[320,128]{1,0:T(8,128)(2,1)S(1)}, u32[]{:S(2)}, u32[]{:S(2)}) collective-permute-start(bf16[320,128]{1,0:T(8,128)(2,1)S(1)} %shard_map.157), channel_id=1, source_target_pairs={{0,4},{4,0},{8,12},{12,8},{16,20},{20,16},{24,28},{28,24},{1,5},{5... | collective-permute-start | bytes 245768 | tf_op jit(solution)/shard_map/ppermute | solution.py:608
